TPU v7x, 32 devices: a whole 2x2x4 slice. The times are simulated.
32 devices in a mesh: gx: 4 (over z), gy: 4 (over y, x), gz: 2 (over core).
Axes of the slice: x: 2, y: 2, z: 4, core: 2. Of those that a mesh axis runs over, the one named last changes fastest.
Arguments:
- displacement: float32 [3, 32, 32, 256], P(None, 'gx', 'gy', 'gz'), may hold values from -0.15 to 0.15
- velocity: float32 [3, 32, 32, 256], P(None, 'gx', 'gy', 'gz'), may hold values from -0.2 to 0.2
- micromodulus: float32 [32, 32, 256], P('gx', 'gy', 'gz'), may hold values from 0.25 to 4
- damage_bits: int32 [12, 32, 32, 256], P(None, 'gx', 'gy', 'gz'), may hold values from 0 to 4095, as said below
Outputs:
- force_density: float32 [3, 32, 32, 256], P(None, 'gx', 'gy', 'gz')
- displacement_next: float32 [3, 32, 32, 256], P(None, 'gx', 'gy', 'gz')
- velocity_next: float32 [3, 32, 32, 256], P(None, 'gx', 'gy', 'gz')
Inputs may be any that keep to these rules, and one draw needn't show every extreme that they name: `damage_bits`: bit b of word w (w = 0 to 5) flags forward bond 12 w + b of the node as broken, in the order of the steps; words 6 to 11 hold the flags of the opposite offsets in the same places. Only bits 0 to 11 are used, and only bit 0 in words 5 and 11. The flag of offset -d at node j equals the flag of offset d at node j - d, and is clear where j - d lies outside the grid.
All inputs are finite; a program needn't handle non-finite values.
Results may differ from a plain program's by a relative error of at most 0.00002.
Values sent between devices are 32-bit elements; how exact they have to be, the bound alone decides.
No kernel may reach another device: no remote copies, remote signals or barrier semaphores. Data moves between devices by JAX's collectives and lax.ppermute only.
A program may use at most 64 MiB of HBM per device.

v0:
```python
import jax
import jax.numpy as jnp
from jax import lax
from jax.sharding import PartitionSpec as P

HORIZON = 3


DT_STEP = 0.25
BOND_SCALE = 5.0


def with_halo(cells, sides, width):
    for axis, dim in sides:
        count = lax.axis_size(axis)
        ends = count - 1
        head = lax.slice_in_dim(cells, 0, width, axis=dim)
        tail = lax.slice_in_dim(cells, cells.shape[dim] - width, cells.shape[dim], axis=dim)
        cells = jnp.concatenate(
            [
                lax.ppermute(tail, axis, [(i, (i + 1) % count) for i in range(ends)]),
                cells,
                lax.ppermute(head, axis, [((i + 1) % count, i) for i in range(ends)]),
            ],
            axis=dim,
        )
    return cells


def passed_along(block, axis, distance):
    devices = range(lax.axis_size(axis))
    route = [(i - distance, i) for i in devices if i - distance in devices]
    return lax.ppermute(block, axis, route)


def bond_offsets(margin):
    forward = []
    for step_x in range(-margin, margin + 1):
        for step_y in range(-margin, margin + 1):
            for step_z in range(-margin, margin + 1):
                radius = step_x * step_x + step_y * step_y + step_z * step_z
                leading = step_x > 0 or (
                    step_x == 0 and (step_y > 0 or (step_y == 0 and step_z > 0))
                )
                if 0 < radius <= margin * margin and leading:
                    forward.append((step_x, step_y, step_z))
    return forward


def bond_force(own_disp, far_disp, root_own, root_far, intact, offset):
    length = jnp.sqrt(
        jnp.float32(offset[0] * offset[0] + offset[1] * offset[1] + offset[2] * offset[2])
    )
    stretch_x = offset[0] + far_disp[0] - own_disp[0]
    stretch_y = offset[1] + far_disp[1] - own_disp[1]
    stretch_z = offset[2] + far_disp[2] - own_disp[2]
    current = jnp.sqrt(stretch_x * stretch_x + stretch_y * stretch_y + stretch_z * stretch_z)
    factor = (
        BOND_SCALE * root_own * root_far * intact * (current - length) / (length * length * current)
    )
    return jnp.stack([factor * stretch_x, factor * stretch_y, factor * stretch_z])


def unpack(damage_bits, word_id, bit_id):
    return 1.0 - jnp.bitwise_and(jnp.right_shift(damage_bits[word_id], bit_id), 1).astype(
        jnp.float32
    )


def body(displacement, velocity, micromodulus, damage_bits):
    margin = HORIZON
    advanced = displacement + DT_STEP * velocity
    root_mod = jnp.sqrt(micromodulus)
    fields = jnp.concatenate([advanced, root_mod[None]], axis=0)
    cells_x, cells_y, cells_z = advanced.shape[1:]
    forward = bond_offsets(margin)
    side_pad = with_halo(fields, (("gy", 2), ("gz", 3)), margin)
    top_rim = passed_along(side_pad[:, :margin], "gx", -1)
    padded = jnp.concatenate([side_pad, top_rim], axis=1)
    reaction = jnp.zeros(
        (3, cells_x + margin, cells_y + 2 * margin, cells_z + 2 * margin), jnp.float32
    )
    own_total = jnp.zeros_like(advanced)
    for number, offset in enumerate(forward):
        lead_x = offset[0]
        lead_y = margin + offset[1]
        lead_z = margin + offset[2]
        window = padded[
            :, lead_x : lead_x + cells_x, lead_y : lead_y + cells_y, lead_z : lead_z + cells_z
        ]
        intact = unpack(damage_bits, number // 12, number % 12)
        bond_pull = bond_force(advanced, window[:3], root_mod, window[3], intact, offset)
        own_total = own_total + bond_pull
        reaction = reaction.at[
            :, lead_x : lead_x + cells_x, lead_y : lead_y + cells_y, lead_z : lead_z + cells_z
        ].add(-bond_pull)
    reaction = reaction.at[:, :cells_x, margin : margin + cells_y, margin : margin + cells_z].add(
        own_total
    )
    incoming = passed_along(reaction[:, cells_x:], "gx", 1)
    reaction = reaction[:, :cells_x].at[:, :margin].add(incoming)
    low_rim = passed_along(reaction[:, :, :margin], "gy", -1)
    high_rim = passed_along(reaction[:, :, cells_y + margin :], "gy", 1)
    reaction = reaction[:, :, margin : cells_y + margin]
    reaction = reaction.at[:, :, cells_y - margin :].add(low_rim).at[:, :, :margin].add(high_rim)
    low_rim = passed_along(reaction[:, :, :, :margin], "gz", -1)
    high_rim = passed_along(reaction[:, :, :, cells_z + margin :], "gz", 1)
    reaction = reaction[:, :, :, margin : cells_z + margin]
    summed = (
        reaction.at[:, :, :, cells_z - margin :].add(low_rim).at[:, :, :, :margin].add(high_rim)
    )
    return (summed, advanced, velocity + DT_STEP * summed)


def solution(mesh):
    placed = (
        P(None, "gx", "gy", "gz"),
        P(None, "gx", "gy", "gz"),
        P("gx", "gy", "gz"),
        P(None, "gx", "gy", "gz"),
    )
    return jax.shard_map(
        body,
        mesh=mesh,
        in_specs=placed,
        out_specs=(P(None, "gx", "gy", "gz"), P(None, "gx", "gy", "gz"), P(None, "gx", "gy", "gz")),
        check_vma=False,
    )
```

profile of v0, /device:TPU:20, one launch (start us, length us, event | category | flops | bytes accessed | tf_op | source)
XLA Modules:
  0.0 584.6 jit_solution(15669476745935372675)
XLA Ops:
  27.6 7.5 %scatter-add.225 = f32[3,11,14,134]{3,2,1,0:T(8,128)S(1)} dynamic-update-slice(f32[3,11,14,134]{3,2,1,0:T(8,128)S(1)} %scatter-add.224, f32[3,8,8,128]{3,2,1,0:T(8,128)S(1)} %fusion.1, s32[]{:T(128)} %constant.2250.clone.1, s32[]{:T(128)} %constant.2250.clone.1, s32[]{:T(128)} %constant.2257.clone.1, s32[]{:T(128)} %constant.2258.clone.1) | dynamic-update-slice | bytes 196612 | tf_op jit(solution)/shard_map/scatter-add | solution.py:96
  37.6 9.3 %scatter-add.226 = f32[3,11,14,134]{3,2,1,0:T(8,128)S(1)} dynamic-update-slice(f32[3,11,14,134]{3,2,1,0:T(8,128)S(1)} %scatter-add.225, f32[3,8,8,128]{3,2,1,0:T(8,128)S(1)} %add_select_fusion, s32[]{:T(128)} %constant.2250.clone.1, s32[]{:T(128)} %bitcast.17, s32[]{:T(128)} %bitcast.18, s32[]{:T(128)} %bitcast.19) | dynamic-update-slice | bytes 196612 | tf_op jit(solution)/shard_map/scatter-add | solution.py:96
  48.6 7.5 %scatter-add.229 = f32[3,11,14,134]{3,2,1,0:T(8,128)S(1)} dynamic-update-slice(f32[3,11,14,134]{3,2,1,0:T(8,128)S(1)} %scatter-add.226, f32[3,8,8,128]{3,2,1,0:T(8,128)S(1)} %slice_add_fusion.63, s32[]{:T(128)} %constant.2250.clone.1, s32[]{:T(128)} %constant.2250.clone.1, s32[]{:T(128)} %constant.2267.clone.1, s32[]{:T(128)} %constant.2251.clone.1) | dynamic-update-slice | bytes 196612 | tf_op jit(solution)/shard_map/scatter-add | solution.py:96
  56.3 7.5 %scatter-add.230 = f32[3,11,14,134]{3,2,1,0:T(8,128)S(1)} dynamic-update-slice(f32[3,11,14,134]{3,2,1,0:T(8,128)S(1)} %scatter-add.229, f32[3,8,8,128]{3,2,1,0:T(8,128)S(1)} %slice_add_fusion.62, s32[]{:T(128)} %constant.2250.clone.1, s32[]{:T(128)} %constant.2250.clone.1, s32[]{:T(128)} %constant.2267.clone.1, s32[]{:T(128)} %constant.2262.clone.1) | dynamic-update-slice | bytes 196612 | tf_op jit(solution)/shard_map/scatter-add | solution.py:96
  64.7 7.5 %scatter-add.231 = f32[3,11,14,134]{3,2,1,0:T(8,128)S(1)} dynamic-update-slice(f32[3,11,14,134]{3,2,1,0:T(8,128)S(1)} %scatter-add.230, f32[3,8,8,128]{3,2,1,0:T(8,128)S(1)} %slice_add_fusion.61, s32[]{:T(128)} %constant.2250.clone.1, s32[]{:T(128)} %constant.2250.clone.1, s32[]{:T(128)} %constant.2267.clone.1, s32[]{:T(128)} %constant.2257.clone.1) | dynamic-update-slice | bytes 196612 | tf_op jit(solution)/shard_map/scatter-add | solution.py:96
  73.1 7.5 %scatter-add.234 = f32[3,11,14,134]{3,2,1,0:T(8,128)S(1)} dynamic-update-slice(f32[3,11,14,134]{3,2,1,0:T(8,128)S(1)} %scatter-add.231, f32[3,8,8,128]{3,2,1,0:T(8,128)S(1)} %slice_add_fusion.60, s32[]{:T(128)} %constant.2250.clone.1, s32[]{:T(128)} %constant.2250.clone.1, s32[]{:T(128)} %constant.2267.clone.1, s32[]{:T(128)} %constant.2267.clone.1) | dynamic-update-slice | bytes 196612 | tf_op jit(solution)/shard_map/scatter-add | solution.py:96
  80.7 7.5 %scatter-add.235 = f32[3,11,14,134]{3,2,1,0:T(8,128)S(1)} dynamic-update-slice(f32[3,11,14,134]{3,2,1,0:T(8,128)S(1)} %scatter-add.234, f32[3,8,8,128]{3,2,1,0:T(8,128)S(1)} %slice_add_fusion.59, s32[]{:T(128)} %constant.2250.clone.1, s32[]{:T(128)} %constant.2250.clone.1, s32[]{:T(128)} %constant.2267.clone.1, s32[]{:T(128)} %constant.2258.clone.1) | dynamic-update-slice | bytes 196612 | tf_op jit(solution)/shard_map/scatter-add | solution.py:96
  88.4 7.5 %scatter-add.236 = f32[3,11,14,134]{3,2,1,0:T(8,128)S(1)} dynamic-update-slice(f32[3,11,14,134]{3,2,1,0:T(8,128)S(1)} %scatter-add.235, f32[3,8,8,128]{3,2,1,0:T(8,128)S(1)} %slice_add_fusion.58, s32[]{:T(128)} %constant.2250.clone.1, s32[]{:T(128)} %constant.2250.clone.1, s32[]{:T(128)} %constant.2258.clone.1, s32[]{:T(128)} %constant.2251.clone.1) | dynamic-update-slice | bytes 196612 | tf_op jit(solution)/shard_map/scatter-add | solution.py:96
  96.0 7.5 %scatter-add.239 = f32[3,11,14,134]{3,2,1,0:T(8,128)S(1)} dynamic-update-slice(f32[3,11,14,134]{3,2,1,0:T(8,128)S(1)} %scatter-add.236, f32[3,8,8,128]{3,2,1,0:T(8,128)S(1)} %slice_add_fusion.57, s32[]{:T(128)} %constant.2250.clone.1, s32[]{:T(128)} %constant.2250.clone.1, s32[]{:T(128)} %constant.2258.clone.1, s32[]{:T(128)} %constant.2262.clone.1) | dynamic-update-slice | bytes 196612 | tf_op jit(solution)/shard_map/scatter-add | solution.py:96
  103.7 7.5 %scatter-add.240 = f32[3,11,14,134]{3,2,1,0:T(8,128)S(1)} dynamic-update-slice(f32[3,11,14,134]{3,2,1,0:T(8,128)S(1)} %scatter-add.239, f32[3,8,8,128]{3,2,1,0:T(8,128)S(1)} %slice_add_fusion.56, s32[]{:T(128)} %constant.2250.clone.1, s32[]{:T(128)} %constant.2250.clone.1, s32[]{:T(128)} %constant.2258.clone.1, s32[]{:T(128)} %constant.2257.clone.1) | dynamic-update-slice | bytes 196612 | tf_op jit(solution)/shard_map/scatter-add | solution.py:96
  111.3 7.5 %scatter-add.241 = f32[3,11,14,134]{3,2,1,0:T(8,128)S(1)} dynamic-update-slice(f32[3,11,14,134]{3,2,1,0:T(8,128)S(1)} %scatter-add.240, f32[3,8,8,128]{3,2,1,0:T(8,128)S(1)} %slice_add_fusion.55, s32[]{:T(128)} %constant.2250.clone.1, s32[]{:T(128)} %constant.2250.clone.1, s32[]{:T(128)} %constant.2258.clone.1, s32[]{:T(128)} %constant.2267.clone.1) | dynamic-update-slice | bytes 196612 | tf_op jit(solution)/shard_map/scatter-add | solution.py:96
  118.9 7.5 %scatter-add.244 = f32[3,11,14,134]{3,2,1,0:T(8,128)S(1)} dynamic-update-slice(f32[3,11,14,134]{3,2,1,0:T(8,128)S(1)} %scatter-add.241, f32[3,8,8,128]{3,2,1,0:T(8,128)S(1)} %slice_add_fusion.54, s32[]{:T(128)} %constant.2250.clone.1, s32[]{:T(128)} %constant.2250.clone.1, s32[]{:T(128)} %constant.2258.clone.1, s32[]{:T(128)} %constant.2258.clone.1) | dynamic-update-slice | bytes 196612 | tf_op jit(solution)/shard_map/scatter-add | solution.py:96
  126.6 8.0 %scatter-add.245 = f32[3,11,14,134]{3,2,1,0:T(8,128)S(1)} dynamic-update-slice(f32[3,11,14,134]{3,2,1,0:T(8,128)S(1)} %scatter-add.244, f32[3,8,8,128]{3,2,1,0:T(8,128)S(1)} %slice_add_fusion.53, s32[]{:T(128)} %constant.2250.clone.1, s32[]{:T(128)} %constant.2250.clone.1, s32[]{:T(128)} %constant.2270.clone.1, s32[]{:T(128)} %constant.2257.clone.1) | dynamic-update-slice | bytes 196612 | tf_op jit(solution)/shard_map/scatter-add | solution.py:96
  156.3 7.5 %scatter-add.246 = f32[3,11,14,134]{3,2,1,0:T(8,128)S(1)} dynamic-update-slice(f32[3,11,14,134]{3,2,1,0:T(8,128)S(1)} %scatter-add.245, f32[3,8,8,128]{3,2,1,0:T(8,128)S(1)} %slice_add_fusion.52, s32[]{:T(128)} %constant.2250.clone.1, s32[]{:T(128)} %constant.2251.clone.1, s32[]{:T(128)} %constant.2251.clone.1, s32[]{:T(128)} %constant.2251.clone.1) | dynamic-update-slice | bytes 196612 | tf_op jit(solution)/shard_map/scatter-add | solution.py:96
  164.0 7.5 %scatter-add.249 = f32[3,11,14,134]{3,2,1,0:T(8,128)S(1)} dynamic-update-slice(f32[3,11,14,134]{3,2,1,0:T(8,128)S(1)} %scatter-add.246, f32[3,8,8,128]{3,2,1,0:T(8,128)S(1)} %slice_add_fusion.51, s32[]{:T(128)} %constant.2250.clone.1, s32[]{:T(128)} %constant.2251.clone.1, s32[]{:T(128)} %constant.2251.clone.1, s32[]{:T(128)} %constant.2262.clone.1) | dynamic-update-slice | bytes 196612 | tf_op jit(solution)/shard_map/scatter-add | solution.py:96
  171.7 7.5 %scatter-add.250 = f32[3,11,14,134]{3,2,1,0:T(8,128)S(1)} dynamic-update-slice(f32[3,11,14,134]{3,2,1,0:T(8,128)S(1)} %scatter-add.249, f32[3,8,8,128]{3,2,1,0:T(8,128)S(1)} %slice_add_fusion.50, s32[]{:T(128)} %constant.2250.clone.1, s32[]{:T(128)} %constant.2251.clone.1, s32[]{:T(128)} %constant.2251.clone.1, s32[]{:T(128)} %constant.2257.clone.1) | dynamic-update-slice | bytes 196612 | tf_op jit(solution)/shard_map/scatter-add | solution.py:96
  180.1 7.5 %scatter-add.251 = f32[3,11,14,134]{3,2,1,0:T(8,128)S(1)} dynamic-update-slice(f32[3,11,14,134]{3,2,1,0:T(8,128)S(1)} %scatter-add.250, f32[3,8,8,128]{3,2,1,0:T(8,128)S(1)} %slice_add_fusion.49, s32[]{:T(128)} %constant.2250.clone.1, s32[]{:T(128)} %constant.2251.clone.1, s32[]{:T(128)} %constant.2251.clone.1, s32[]{:T(128)} %constant.2267.clone.1) | dynamic-update-slice | bytes 196612 | tf_op jit(solution)/shard_map/scatter-add | solution.py:96
  187.8 7.5 %scatter-add.254 = f32[3,11,14,134]{3,2,1,0:T(8,128)S(1)} dynamic-update-slice(f32[3,11,14,134]{3,2,1,0:T(8,128)S(1)} %scatter-add.251, f32[3,8,8,128]{3,2,1,0:T(8,128)S(1)} %slice_add_fusion.48, s32[]{:T(128)} %constant.2250.clone.1, s32[]{:T(128)} %constant.2251.clone.1, s32[]{:T(128)} %constant.2251.clone.1, s32[]{:T(128)} %constant.2258.clone.1) | dynamic-update-slice | bytes 196612 | tf_op jit(solution)/shard_map/scatter-add | solution.py:96
  195.4 7.5 %scatter-add.255 = f32[3,11,14,134]{3,2,1,0:T(8,128)S(1)} dynamic-update-slice(f32[3,11,14,134]{3,2,1,0:T(8,128)S(1)} %scatter-add.254, f32[3,8,8,128]{3,2,1,0:T(8,128)S(1)} %slice_add_fusion.47, s32[]{:T(128)} %constant.2250.clone.1, s32[]{:T(128)} %constant.2251.clone.1, s32[]{:T(128)} %constant.2262.clone.1, s32[]{:T(128)} %constant.2251.clone.1) | dynamic-update-slice | bytes 196612 | tf_op jit(solution)/shard_map/scatter-add | solution.py:96
  204.5 7.5 %scatter-add.256 = f32[3,11,14,134]{3,2,1,0:T(8,128)S(1)} dynamic-update-slice(f32[3,11,14,134]{3,2,1,0:T(8,128)S(1)} %scatter-add.255, f32[3,8,8,128]{3,2,1,0:T(8,128)S(1)} %slice_add_fusion.46, s32[]{:T(128)} %constant.2250.clone.1, s32[]{:T(128)} %constant.2251.clone.1, s32[]{:T(128)} %constant.2262.clone.1, s32[]{:T(128)} %constant.2262.clone.1) | dynamic-update-slice | bytes 196612 | tf_op jit(solution)/shard_map/scatter-add | solution.py:96
  212.1 7.5 %scatter-add.259 = f32[3,11,14,134]{3,2,1,0:T(8,128)S(1)} dynamic-update-slice(f32[3,11,14,134]{3,2,1,0:T(8,128)S(1)} %scatter-add.256, f32[3,8,8,128]{3,2,1,0:T(8,128)S(1)} %slice_add_fusion.45, s32[]{:T(128)} %constant.2250.clone.1, s32[]{:T(128)} %constant.2251.clone.1, s32[]{:T(128)} %constant.2262.clone.1, s32[]{:T(128)} %constant.2257.clone.1) | dynamic-update-slice | bytes 196612 | tf_op jit(solution)/shard_map/scatter-add | solution.py:96
  219.7 7.5 %scatter-add.260 = f32[3,11,14,134]{3,2,1,0:T(8,128)S(1)} dynamic-update-slice(f32[3,11,14,134]{3,2,1,0:T(8,128)S(1)} %scatter-add.259, f32[3,8,8,128]{3,2,1,0:T(8,128)S(1)} %slice_add_fusion.44, s32[]{:T(128)} %constant.2250.clone.1, s32[]{:T(128)} %constant.2251.clone.1, s32[]{:T(128)} %constant.2262.clone.1, s32[]{:T(128)} %constant.2267.clone.1) | dynamic-update-slice | bytes 196612 | tf_op jit(solution)/shard_map/scatter-add | solution.py:96
  228.9 7.5 %scatter-add.261 = f32[3,11,14,134]{3,2,1,0:T(8,128)S(1)} dynamic-update-slice(f32[3,11,14,134]{3,2,1,0:T(8,128)S(1)} %scatter-add.260, f32[3,8,8,128]{3,2,1,0:T(8,128)S(1)} %slice_add_fusion.43, s32[]{:T(128)} %constant.2250.clone.1, s32[]{:T(128)} %constant.2251.clone.1, s32[]{:T(128)} %constant.2262.clone.1, s32[]{:T(128)} %constant.2258.clone.1) | dynamic-update-slice | bytes 196612 | tf_op jit(solution)/shard_map/scatter-add | solution.py:96
  236.6 7.5 %scatter-add.264 = f32[3,11,14,134]{3,2,1,0:T(8,128)S(1)} dynamic-update-slice(f32[3,11,14,134]{3,2,1,0:T(8,128)S(1)} %scatter-add.261, f32[3,8,8,128]{3,2,1,0:T(8,128)S(1)} %slice_add_fusion.42, s32[]{:T(128)} %constant.2250.clone.1, s32[]{:T(128)} %constant.2251.clone.1, s32[]{:T(128)} %constant.2257.clone.1, s32[]{:T(128)} %constant.2251.clone.1) | dynamic-update-slice | bytes 196612 | tf_op jit(solution)/shard_map/scatter-add | solution.py:96
  244.2 7.7 %scatter-add.265 = f32[3,11,14,134]{3,2,1,0:T(8,128)S(1)} dynamic-update-slice(f32[3,11,14,134]{3,2,1,0:T(8,128)S(1)} %scatter-add.264, f32[3,8,8,128]{3,2,1,0:T(8,128)S(1)} %slice_add_fusion.41, s32[]{:T(128)} %constant.2250.clone.1, s32[]{:T(128)} %constant.2251.clone.1, s32[]{:T(128)} %constant.2257.clone.1, s32[]{:T(128)} %constant.2262.clone.1) | dynamic-update-slice | bytes 196612 | tf_op jit(solution)/shard_map/scatter-add | solution.py:96
  253.6 7.5 %scatter-add.266 = f32[3,11,14,134]{3,2,1,0:T(8,128)S(1)} dynamic-update-slice(f32[3,11,14,134]{3,2,1,0:T(8,128)S(1)} %scatter-add.265, f32[3,8,8,128]{3,2,1,0:T(8,128)S(1)} %slice_add_fusion.40, s32[]{:T(128)} %constant.2250.clone.1, s32[]{:T(128)} %constant.2251.clone.1, s32[]{:T(128)} %constant.2257.clone.1, s32[]{:T(128)} %constant.2257.clone.1) | dynamic-update-slice | bytes 196612 | tf_op jit(solution)/shard_map/scatter-add | solution.py:96
  261.2 7.5 %scatter-add.269 = f32[3,11,14,134]{3,2,1,0:T(8,128)S(1)} dynamic-update-slice(f32[3,11,14,134]{3,2,1,0:T(8,128)S(1)} %scatter-add.266, f32[3,8,8,128]{3,2,1,0:T(8,128)S(1)} %slice_add_fusion.39, s32[]{:T(128)} %constant.2250.clone.1, s32[]{:T(128)} %constant.2251.clone.1, s32[]{:T(128)} %constant.2257.clone.1, s32[]{:T(128)} %constant.2267.clone.1) | dynamic-update-slice | bytes 196612 | tf_op jit(solution)/shard_map/scatter-add | solution.py:96
  268.9 7.5 %scatter-add.270 = f32[3,11,14,134]{3,2,1,0:T(8,128)S(1)} dynamic-update-slice(f32[3,11,14,134]{3,2,1,0:T(8,128)S(1)} %scatter-add.269, f32[3,8,8,128]{3,2,1,0:T(8,128)S(1)} %slice_add_fusion.38, s32[]{:T(128)} %constant.2250.clone.1, s32[]{:T(128)} %constant.2251.clone.1, s32[]{:T(128)} %constant.2257.clone.1, s32[]{:T(128)} %constant.2258.clone.1) | dynamic-update-slice | bytes 196612 | tf_op jit(solution)/shard_map/scatter-add | solution.py:96
  278.5 7.5 %scatter-add.271 = f32[3,11,14,134]{3,2,1,0:T(8,128)S(1)} dynamic-update-slice(f32[3,11,14,134]{3,2,1,0:T(8,128)S(1)} %scatter-add.270, f32[3,8,8,128]{3,2,1,0:T(8,128)S(1)} %slice_add_fusion.37, s32[]{:T(128)} %constant.2250.clone.1, s32[]{:T(128)} %constant.2251.clone.1, s32[]{:T(128)} %constant.2267.clone.1, s32[]{:T(128)} %constant.2251.clone.1) | dynamic-update-slice | bytes 196612 | tf_op jit(solution)/shard_map/scatter-add | solution.py:96
  286.1 7.5 %scatter-add.274 = f32[3,11,14,134]{3,2,1,0:T(8,128)S(1)} dynamic-update-slice(f32[3,11,14,134]{3,2,1,0:T(8,128)S(1)} %scatter-add.271, f32[3,8,8,128]{3,2,1,0:T(8,128)S(1)} %slice_add_fusion.36, s32[]{:T(128)} %constant.2250.clone.1, s32[]{:T(128)} %constant.2251.clone.1, s32[]{:T(128)} %constant.2267.clone.1, s32[]{:T(128)} %constant.2262.clone.1) | dynamic-update-slice | bytes 196612 | tf_op jit(solution)/shard_map/scatter-add | solution.py:96
  295.8 7.5 %scatter-add.275 = f32[3,11,14,134]{3,2,1,0:T(8,128)S(1)} dynamic-update-slice(f32[3,11,14,134]{3,2,1,0:T(8,128)S(1)} %scatter-add.274, f32[3,8,8,128]{3,2,1,0:T(8,128)S(1)} %slice_add_fusion.35, s32[]{:T(128)} %constant.2250.clone.1, s32[]{:T(128)} %constant.2251.clone.1, s32[]{:T(128)} %constant.2267.clone.1, s32[]{:T(128)} %constant.2257.clone.1) | dynamic-update-slice | bytes 196612 | tf_op jit(solution)/shard_map/scatter-add | solution.py:96
  303.4 7.5 %scatter-add.276 = f32[3,11,14,134]{3,2,1,0:T(8,128)S(1)} dynamic-update-slice(f32[3,11,14,134]{3,2,1,0:T(8,128)S(1)} %scatter-add.275, f32[3,8,8,128]{3,2,1,0:T(8,128)S(1)} %slice_add_fusion.34, s32[]{:T(128)} %constant.2250.clone.1, s32[]{:T(128)} %constant.2251.clone.1, s32[]{:T(128)} %constant.2267.clone.1, s32[]{:T(128)} %constant.2267.clone.1) | dynamic-update-slice | bytes 196612 | tf_op jit(solution)/shard_map/scatter-add | solution.py:96
  313.1 7.5 %scatter-add.279 = f32[3,11,14,134]{3,2,1,0:T(8,128)S(1)} dynamic-update-slice(f32[3,11,14,134]{3,2,1,0:T(8,128)S(1)} %scatter-add.276, f32[3,8,8,128]{3,2,1,0:T(8,128)S(1)} %slice_add_fusion.33, s32[]{:T(128)} %constant.2250.clone.1, s32[]{:T(128)} %constant.2251.clone.1, s32[]{:T(128)} %constant.2267.clone.1, s32[]{:T(128)} %constant.2258.clone.1) | dynamic-update-slice | bytes 196612 | tf_op jit(solution)/shard_map/scatter-add | solution.py:96
  320.7 7.5 %scatter-add.280 = f32[3,11,14,134]{3,2,1,0:T(8,128)S(1)} dynamic-update-slice(f32[3,11,14,134]{3,2,1,0:T(8,128)S(1)} %scatter-add.279, f32[3,8,8,128]{3,2,1,0:T(8,128)S(1)} %slice_add_fusion.32, s32[]{:T(128)} %constant.2250.clone.1, s32[]{:T(128)} %constant.2251.clone.1, s32[]{:T(128)} %constant.2258.clone.1, s32[]{:T(128)} %constant.2251.clone.1) | dynamic-update-slice | bytes 196612 | tf_op jit(solution)/shard_map/scatter-add | solution.py:96
  330.4 7.5 %scatter-add.281 = f32[3,11,14,134]{3,2,1,0:T(8,128)S(1)} dynamic-update-slice(f32[3,11,14,134]{3,2,1,0:T(8,128)S(1)} %scatter-add.280, f32[3,8,8,128]{3,2,1,0:T(8,128)S(1)} %slice_add_fusion.31, s32[]{:T(128)} %constant.2250.clone.1, s32[]{:T(128)} %constant.2251.clone.1, s32[]{:T(128)} %constant.2258.clone.1, s32[]{:T(128)} %constant.2262.clone.1) | dynamic-update-slice | bytes 196612 | tf_op jit(solution)/shard_map/scatter-add | solution.py:96
  338.1 7.5 %scatter-add.284 = f32[3,11,14,134]{3,2,1,0:T(8,128)S(1)} dynamic-update-slice(f32[3,11,14,134]{3,2,1,0:T(8,128)S(1)} %scatter-add.281, f32[3,8,8,128]{3,2,1,0:T(8,128)S(1)} %slice_add_fusion.30, s32[]{:T(128)} %constant.2250.clone.1, s32[]{:T(128)} %constant.2251.clone.1, s32[]{:T(128)} %constant.2258.clone.1, s32[]{:T(128)} %constant.2257.clone.1) | dynamic-update-slice | bytes 196612 | tf_op jit(solution)/shard_map/scatter-add | solution.py:96
  347.8 7.5 %scatter-add.285 = f32[3,11,14,134]{3,2,1,0:T(8,128)S(1)} dynamic-update-slice(f32[3,11,14,134]{3,2,1,0:T(8,128)S(1)} %scatter-add.284, f32[3,8,8,128]{3,2,1,0:T(8,128)S(1)} %slice_add_fusion.29, s32[]{:T(128)} %constant.2250.clone.1, s32[]{:T(128)} %constant.2251.clone.1, s32[]{:T(128)} %constant.2258.clone.1, s32[]{:T(128)} %constant.2267.clone.1) | dynamic-update-slice | bytes 196612 | tf_op jit(solution)/shard_map/scatter-add | solution.py:96
  355.5 7.5 %scatter-add.286 = f32[3,11,14,134]{3,2,1,0:T(8,128)S(1)} dynamic-update-slice(f32[3,11,14,134]{3,2,1,0:T(8,128)S(1)} %scatter-add.285, f32[3,8,8,128]{3,2,1,0:T(8,128)S(1)} %slice_add_fusion.28, s32[]{:T(128)} %constant.2250.clone.1, s32[]{:T(128)} %constant.2251.clone.1, s32[]{:T(128)} %constant.2258.clone.1, s32[]{:T(128)} %constant.2258.clone.1) | dynamic-update-slice | bytes 196612 | tf_op jit(solution)/shard_map/scatter-add | solution.py:96
  365.3 7.5 %scatter-add.289 = f32[3,11,14,134]{3,2,1,0:T(8,128)S(1)} dynamic-update-slice(f32[3,11,14,134]{3,2,1,0:T(8,128)S(1)} %scatter-add.286, f32[3,8,8,128]{3,2,1,0:T(8,128)S(1)} %slice_add_fusion.27, s32[]{:T(128)} %constant.2250.clone.1, s32[]{:T(128)} %constant.2262.clone.1, s32[]{:T(128)} %constant.2251.clone.1, s32[]{:T(128)} %constant.2262.clone.1) | dynamic-update-slice | bytes 196612 | tf_op jit(solution)/shard_map/scatter-add | solution.py:96
  372.9 7.5 %scatter-add.290 = f32[3,11,14,134]{3,2,1,0:T(8,128)S(1)} dynamic-update-slice(f32[3,11,14,134]{3,2,1,0:T(8,128)S(1)} %scatter-add.289, f32[3,8,8,128]{3,2,1,0:T(8,128)S(1)} %slice_add_fusion.26, s32[]{:T(128)} %constant.2250.clone.1, s32[]{:T(128)} %constant.2262.clone.1, s32[]{:T(128)} %constant.2251.clone.1, s32[]{:T(128)} %constant.2257.clone.1) | dynamic-update-slice | bytes 196612 | tf_op jit(solution)/shard_map/scatter-add | solution.py:96
  382.7 7.5 %scatter-add.291 = f32[3,11,14,134]{3,2,1,0:T(8,128)S(1)} dynamic-update-slice(f32[3,11,14,134]{3,2,1,0:T(8,128)S(1)} %scatter-add.290, f32[3,8,8,128]{3,2,1,0:T(8,128)S(1)} %slice_add_fusion.25, s32[]{:T(128)} %constant.2250.clone.1, s32[]{:T(128)} %constant.2262.clone.1, s32[]{:T(128)} %constant.2251.clone.1, s32[]{:T(128)} %constant.2267.clone.1) | dynamic-update-slice | bytes 196612 | tf_op jit(solution)/shard_map/scatter-add | solution.py:96
  390.3 7.7 %scatter-add.294 = f32[3,11,14,134]{3,2,1,0:T(8,128)S(1)} dynamic-update-slice(f32[3,11,14,134]{3,2,1,0:T(8,128)S(1)} %scatter-add.291, f32[3,8,8,128]{3,2,1,0:T(8,128)S(1)} %slice_add_fusion.24, s32[]{:T(128)} %constant.2250.clone.1, s32[]{:T(128)} %constant.2262.clone.1, s32[]{:T(128)} %constant.2262.clone.1, s32[]{:T(128)} %constant.2251.clone.1) | dynamic-update-slice | bytes 196612 | tf_op jit(solution)/shard_map/scatter-add | solution.py:96
  400.3 7.5 %scatter-add.295 = f32[3,11,14,134]{3,2,1,0:T(8,128)S(1)} dynamic-update-slice(f32[3,11,14,134]{3,2,1,0:T(8,128)S(1)} %scatter-add.294, f32[3,8,8,128]{3,2,1,0:T(8,128)S(1)} %slice_add_fusion.23, s32[]{:T(128)} %constant.2250.clone.1, s32[]{:T(128)} %constant.2262.clone.1, s32[]{:T(128)} %constant.2262.clone.1, s32[]{:T(128)} %constant.2262.clone.1) | dynamic-update-slice | bytes 196612 | tf_op jit(solution)/shard_map/scatter-add | solution.py:96
  408.7 7.5 %scatter-add.296 = f32[3,11,14,134]{3,2,1,0:T(8,128)S(1)} dynamic-update-slice(f32[3,11,14,134]{3,2,1,0:T(8,128)S(1)} %scatter-add.295, f32[3,8,8,128]{3,2,1,0:T(8,128)S(1)} %slice_add_fusion.22, s32[]{:T(128)} %constant.2250.clone.1, s32[]{:T(128)} %constant.2262.clone.1, s32[]{:T(128)} %constant.2262.clone.1, s32[]{:T(128)} %constant.2257.clone.1) | dynamic-update-slice | bytes 196612 | tf_op jit(solution)/shard_map/scatter-add | solution.py:96
  418.4 7.5 %scatter-add.299 = f32[3,11,14,134]{3,2,1,0:T(8,128)S(1)} dynamic-update-slice(f32[3,11,14,134]{3,2,1,0:T(8,128)S(1)} %scatter-add.296, f32[3,8,8,128]{3,2,1,0:T(8,128)S(1)} %slice_add_fusion.21, s32[]{:T(128)} %constant.2250.clone.1, s32[]{:T(128)} %constant.2262.clone.1, s32[]{:T(128)} %constant.2262.clone.1, s32[]{:T(128)} %constant.2267.clone.1) | dynamic-update-slice | bytes 196612 | tf_op jit(solution)/shard_map/scatter-add | solution.py:96
  426.8 7.5 %scatter-add.300 = f32[3,11,14,134]{3,2,1,0:T(8,128)S(1)} dynamic-update-slice(f32[3,11,14,134]{3,2,1,0:T(8,128)S(1)} %scatter-add.299, f32[3,8,8,128]{3,2,1,0:T(8,128)S(1)} %slice_add_fusion.20, s32[]{:T(128)} %constant.2250.clone.1, s32[]{:T(128)} %constant.2262.clone.1, s32[]{:T(128)} %constant.2262.clone.1, s32[]{:T(128)} %constant.2258.clone.1) | dynamic-update-slice | bytes 196612 | tf_op jit(solution)/shard_map/scatter-add | solution.py:96
  436.4 7.5 %scatter-add.301 = f32[3,11,14,134]{3,2,1,0:T(8,128)S(1)} dynamic-update-slice(f32[3,11,14,134]{3,2,1,0:T(8,128)S(1)} %scatter-add.300, f32[3,8,8,128]{3,2,1,0:T(8,128)S(1)} %slice_add_fusion.19, s32[]{:T(128)} %constant.2250.clone.1, s32[]{:T(128)} %constant.2262.clone.1, s32[]{:T(128)} %constant.2257.clone.1, s32[]{:T(128)} %constant.2251.clone.1) | dynamic-update-slice | bytes 196612 | tf_op jit(solution)/shard_map/scatter-add | solution.py:96
  444.1 7.5 %scatter-add.304 = f32[3,11,14,134]{3,2,1,0:T(8,128)S(1)} dynamic-update-slice(f32[3,11,14,134]{3,2,1,0:T(8,128)S(1)} %scatter-add.301, f32[3,8,8,128]{3,2,1,0:T(8,128)S(1)} %slice_add_fusion.18, s32[]{:T(128)} %constant.2250.clone.1, s32[]{:T(128)} %constant.2262.clone.1, s32[]{:T(128)} %constant.2257.clone.1, s32[]{:T(128)} %constant.2262.clone.1) | dynamic-update-slice | bytes 196612 | tf_op jit(solution)/shard_map/scatter-add | solution.py:96
  451.8 7.5 %scatter-add.305 = f32[3,11,14,134]{3,2,1,0:T(8,128)S(1)} dynamic-update-slice(f32[3,11,14,134]{3,2,1,0:T(8,128)S(1)} %scatter-add.304, f32[3,8,8,128]{3,2,1,0:T(8,128)S(1)} %slice_add_fusion.17, s32[]{:T(128)} %constant.2250.clone.1, s32[]{:T(128)} %constant.2262.clone.1, s32[]{:T(128)} %constant.2257.clone.1, s32[]{:T(128)} %constant.2257.clone.1) | dynamic-update-slice | bytes 196612 | tf_op jit(solution)/shard_map/scatter-add | solution.py:96
  459.4 7.5 %scatter-add.306 = f32[3,11,14,134]{3,2,1,0:T(8,128)S(1)} dynamic-update-slice(f32[3,11,14,134]{3,2,1,0:T(8,128)S(1)} %scatter-add.305, f32[3,8,8,128]{3,2,1,0:T(8,128)S(1)} %slice_add_fusion.16, s32[]{:T(128)} %constant.2250.clone.1, s32[]{:T(128)} %constant.2262.clone.1, s32[]{:T(128)} %constant.2257.clone.1, s32[]{:T(128)} %constant.2267.clone.1) | dynamic-update-slice | bytes 196612 | tf_op jit(solution)/shard_map/scatter-add | solution.py:96
  467.1 7.5 %scatter-add.309 = f32[3,11,14,134]{3,2,1,0:T(8,128)S(1)} dynamic-update-slice(f32[3,11,14,134]{3,2,1,0:T(8,128)S(1)} %scatter-add.306, f32[3,8,8,128]{3,2,1,0:T(8,128)S(1)} %slice_add_fusion.15, s32[]{:T(128)} %constant.2250.clone.1, s32[]{:T(128)} %constant.2262.clone.1, s32[]{:T(128)} %constant.2257.clone.1, s32[]{:T(128)} %constant.2258.clone.1) | dynamic-update-slice | bytes 196612 | tf_op jit(solution)/shard_map/scatter-add | solution.py:96
  474.8 7.5 %scatter-add.310 = f32[3,11,14,134]{3,2,1,0:T(8,128)S(1)} dynamic-update-slice(f32[3,11,14,134]{3,2,1,0:T(8,128)S(1)} %scatter-add.309, f32[3,8,8,128]{3,2,1,0:T(8,128)S(1)} %slice_add_fusion.14, s32[]{:T(128)} %constant.2250.clone.1, s32[]{:T(128)} %constant.2262.clone.1, s32[]{:T(128)} %constant.2267.clone.1, s32[]{:T(128)} %constant.2251.clone.1) | dynamic-update-slice | bytes 196612 | tf_op jit(solution)/shard_map/scatter-add | solution.py:96
  482.4 7.5 %scatter-add.311 = f32[3,11,14,134]{3,2,1,0:T(8,128)S(1)} dynamic-update-slice(f32[3,11,14,134]{3,2,1,0:T(8,128)S(1)} %scatter-add.310, f32[3,8,8,128]{3,2,1,0:T(8,128)S(1)} %slice_add_fusion.13, s32[]{:T(128)} %constant.2250.clone.1, s32[]{:T(128)} %constant.2262.clone.1, s32[]{:T(128)} %constant.2267.clone.1, s32[]{:T(128)} %constant.2262.clone.1) | dynamic-update-slice | bytes 196612 | tf_op jit(solution)/shard_map/scatter-add | solution.py:96
  490.1 7.5 %scatter-add.314 = f32[3,11,14,134]{3,2,1,0:T(8,128)S(1)} dynamic-update-slice(f32[3,11,14,134]{3,2,1,0:T(8,128)S(1)} %scatter-add.311, f32[3,8,8,128]{3,2,1,0:T(8,128)S(1)} %slice_add_fusion.12, s32[]{:T(128)} %constant.2250.clone.1, s32[]{:T(128)} %constant.2262.clone.1, s32[]{:T(128)} %constant.2267.clone.1, s32[]{:T(128)} %constant.2257.clone.1) | dynamic-update-slice | bytes 196612 | tf_op jit(solution)/shard_map/scatter-add | solution.py:96
  497.8 7.5 %scatter-add.315 = f32[3,11,14,134]{3,2,1,0:T(8,128)S(1)} dynamic-update-slice(f32[3,11,14,134]{3,2,1,0:T(8,128)S(1)} %scatter-add.314, f32[3,8,8,128]{3,2,1,0:T(8,128)S(1)} %slice_add_fusion.11, s32[]{:T(128)} %constant.2250.clone.1, s32[]{:T(128)} %constant.2262.clone.1, s32[]{:T(128)} %constant.2267.clone.1, s32[]{:T(128)} %constant.2267.clone.1) | dynamic-update-slice | bytes 196612 | tf_op jit(solution)/shard_map/scatter-add | solution.py:96
  505.4 7.5 %scatter-add.316 = f32[3,11,14,134]{3,2,1,0:T(8,128)S(1)} dynamic-update-slice(f32[3,11,14,134]{3,2,1,0:T(8,128)S(1)} %scatter-add.315, f32[3,8,8,128]{3,2,1,0:T(8,128)S(1)} %slice_add_fusion.10, s32[]{:T(128)} %constant.2250.clone.1, s32[]{:T(128)} %constant.2262.clone.1, s32[]{:T(128)} %constant.2267.clone.1, s32[]{:T(128)} %constant.2258.clone.1) | dynamic-update-slice | bytes 196612 | tf_op jit(solution)/shard_map/scatter-add | solution.py:96
  513.1 7.5 %scatter-add.319 = f32[3,11,14,134]{3,2,1,0:T(8,128)S(1)} dynamic-update-slice(f32[3,11,14,134]{3,2,1,0:T(8,128)S(1)} %scatter-add.316, f32[3,8,8,128]{3,2,1,0:T(8,128)S(1)} %slice_add_fusion.9, s32[]{:T(128)} %constant.2250.clone.1, s32[]{:T(128)} %constant.2262.clone.1, s32[]{:T(128)} %constant.2258.clone.1, s32[]{:T(128)} %constant.2262.clone.1) | dynamic-update-slice | bytes 196612 | tf_op jit(solution)/shard_map/scatter-add | solution.py:96
  520.8 7.5 %scatter-add.320 = f32[3,11,14,134]{3,2,1,0:T(8,128)S(1)} dynamic-update-slice(f32[3,11,14,134]{3,2,1,0:T(8,128)S(1)} %scatter-add.319, f32[3,8,8,128]{3,2,1,0:T(8,128)S(1)} %slice_add_fusion.8, s32[]{:T(128)} %constant.2250.clone.1, s32[]{:T(128)} %constant.2262.clone.1, s32[]{:T(128)} %constant.2258.clone.1, s32[]{:T(128)} %constant.2257.clone.1) | dynamic-update-slice | bytes 196612 | tf_op jit(solution)/shard_map/scatter-add | solution.py:96
  528.6 7.5 %scatter-add.321 = f32[3,11,14,134]{3,2,1,0:T(8,128)S(1)} dynamic-update-slice(f32[3,11,14,134]{3,2,1,0:T(8,128)S(1)} %scatter-add.320, f32[3,8,8,128]{3,2,1,0:T(8,128)S(1)} %slice_add_fusion.7, s32[]{:T(128)} %constant.2250.clone.1, s32[]{:T(128)} %constant.2262.clone.1, s32[]{:T(128)} %constant.2258.clone.1, s32[]{:T(128)} %constant.2267.clone.1) | dynamic-update-slice | bytes 196612 | tf_op jit(solution)/shard_map/scatter-add | solution.py:96
  536.4 7.8 %scatter-add.324 = f32[3,11,14,134]{3,2,1,0:T(8,128)S(1)} dynamic-update-slice(f32[3,11,14,134]{3,2,1,0:T(8,128)S(1)} %scatter-add.321, f32[3,8,8,128]{3,2,1,0:T(8,128)S(1)} %slice_add_fusion.6, s32[]{:T(128)} %constant.2250.clone.1, s32[]{:T(128)} %constant.2257.clone.1, s32[]{:T(128)} %constant.2257.clone.1, s32[]{:T(128)} %constant.2257.clone.1) | dynamic-update-slice | bytes 196612 | tf_op jit(solution)/shard_map/scatter-add | solution.py:96
  547.2 7.5 %scatter-add.325 = f32[3,11,14,134]{3,2,1,0:T(8,128)S(1)} dynamic-update-slice(f32[3,11,14,134]{3,2,1,0:T(8,128)S(1)} %scatter-add.324, f32[3,8,8,128]{3,2,1,0:T(8,128)S(1)} %slice_add_fusion.5, s32[]{:T(128)} %constant.2250.clone.1, s32[]{:T(128)} %constant.2250.clone.1, s32[]{:T(128)} %constant.2257.clone.1, s32[]{:T(128)} %constant.2257.clone.1) | dynamic-update-slice | bytes 196612 | tf_op jit(solution)/shard_map/scatter-add | solution.py:97
  554.8 4.1 collective-permute-start.5
  562.3 4.2 collective-permute-start.6
  570.1 4.0 collective-permute-done.7
  (505 shorter events, 106.8 us)
Async XLA Ops:
  2.4 431.9 %copy-start = (f32[3,8,8,128]{3,2,1,0:T(8,128)}, f32[3,8,8,128]{3,2,1,0:T(8,128)S(1)}, u32[]{:S(2)}) copy-start(f32[3,8,8,128]{3,2,1,0:T(8,128)S(1)} %multiply_add_fusion.1) | copy-start | bytes 294916
  2.4 8.1 %collective-permute-start = (f32[4,8,3,128]{3,2,1,0:T(4,128)S(1)}, f32[4,8,3,128]{3,2,1,0:T(4,128)S(1)}, u32[]{:S(2)}, u32[]{:S(2)}) collective-permute-start(f32[4,8,3,128]{3,2,1,0:T(4,128)S(1)} %get-tuple-element.1201), channel_id=1, source_target_pairs={{0,2},{2,4},{4,6},{1,3},{3,5},{5,7},{8,10},{10,12},{12,14},{9,11},... | collective-permute-start | bytes 147464 | tf_op jit(solution)/shard_map/ppermute | solution.py:21
  5.8 6.2 %collective-permute-start.1 = (f32[4,8,3,128]{3,2,1,0:T(4,128)S(1)}, f32[4,8,3,128]{3,2,1,0:T(4,128)S(1)}, u32[]{:S(2)}, u32[]{:S(2)}) collective-permute-start(f32[4,8,3,128]{3,2,1,0:T(4,128)S(1)} %get-tuple-element.1202), channel_id=1, source_target_pairs={{2,0},{4,2},{6,4},{3,1},{5,3},{7,5},{10,8},{12,10},{14,12},{11,9},... | collective-permute-start | bytes 147464 | tf_op jit(solution)/shard_map/ppermute | solution.py:23
  12.2 3.5 collective-permute-start.3
  13.6 3.4 collective-permute-start.2
  22.3 112.3 %collective-permute-start.4 = (f32[4,3,14,134]{3,2,1,0:T(8,128)}, f32[4,3,14,134]{3,2,1,0:T(8,128)}, u32[]{:S(2)}, u32[]{:S(2)}) collective-permute-start(f32[4,3,14,134]{3,2,1,0:T(8,128)} %pad_maximum_fusion.4), channel_id=1, source_target_pairs={{8,0},{16,8},{24,16},{9,1},{17,9},{25,17},{10,2},{18,10},{26,18},{... | collective-permute-start | bytes 270152 | tf_op jit(solution)/shard_map/ppermute | solution.py:33
  26.9 8.2 %copy-start.16 = (f32[1,8,8,128]{3,2,1,0:T(8,128)}, f32[1,8,8,128]{3,2,1,0:T(8,128)S(1)}, u32[]{:S(2)}) copy-start(f32[1,8,8,128]{3,2,1,0:T(8,128)S(1)} %get-tuple-element.1173) | copy-start | bytes 98308
  26.9 8.2 %copy-start.18 = (f32[1,8,8,128]{3,2,1,0:T(8,128)}, f32[1,8,8,128]{3,2,1,0:T(8,128)S(1)}, u32[]{:S(2)}) copy-start(f32[1,8,8,128]{3,2,1,0:T(8,128)S(1)} %get-tuple-element.1174) | copy-start | bytes 98308
  145.1 280.7 %copy-start.29 = (f32[1,8,8,128]{3,2,1,0:T(8,128)}, f32[1,8,8,128]{3,2,1,0:T(8,128)S(1)}, u32[]{:S(2)}) copy-start(f32[1,8,8,128]{3,2,1,0:T(8,128)S(1)} %get-tuple-element.931) | copy-start | bytes 98308
  155.4 8.5 %copy-start.65 = (f32[1,8,8,128]{3,2,1,0:T(8,128)}, f32[1,8,8,128]{3,2,1,0:T(8,128)S(1)}, u32[]{:S(2)}) copy-start(f32[1,8,8,128]{3,2,1,0:T(8,128)S(1)} %get-tuple-element.1141) | copy-start | bytes 98308
  155.4 8.5 %copy-start.67 = (f32[1,8,8,128]{3,2,1,0:T(8,128)}, f32[1,8,8,128]{3,2,1,0:T(8,128)S(1)}, u32[]{:S(2)}) copy-start(f32[1,8,8,128]{3,2,1,0:T(8,128)S(1)} %get-tuple-element.1142) | copy-start | bytes 98308
  155.4 16.1 %copy-start.61 = (f32[1,8,8,128]{3,2,1,0:T(8,128)}, f32[1,8,8,128]{3,2,1,0:T(8,128)S(1)}, u32[]{:S(2)}) copy-start(f32[1,8,8,128]{3,2,1,0:T(8,128)S(1)} %get-tuple-element.1073) | copy-start | bytes 98308
  155.4 16.1 %copy-start.63 = (f32[1,8,8,128]{3,2,1,0:T(8,128)}, f32[1,8,8,128]{3,2,1,0:T(8,128)S(1)}, u32[]{:S(2)}) copy-start(f32[1,8,8,128]{3,2,1,0:T(8,128)S(1)} %get-tuple-element.1074) | copy-start | bytes 98308
  179.4 8.2 %copy-start.71 = (f32[1,8,8,128]{3,2,1,0:T(8,128)}, f32[1,8,8,128]{3,2,1,0:T(8,128)S(1)}, u32[]{:S(2)}) copy-start(f32[1,8,8,128]{3,2,1,0:T(8,128)S(1)} %get-tuple-element.1137) | copy-start | bytes 98308
  179.4 8.2 %copy-start.72 = (f32[1,8,8,128]{3,2,1,0:T(8,128)}, f32[1,8,8,128]{3,2,1,0:T(8,128)S(1)}, u32[]{:S(2)}) copy-start(f32[1,8,8,128]{3,2,1,0:T(8,128)S(1)} %get-tuple-element.1138) | copy-start | bytes 98308
  179.4 15.9 %copy-start.69 = (f32[1,8,8,128]{3,2,1,0:T(8,128)}, f32[1,8,8,128]{3,2,1,0:T(8,128)S(1)}, u32[]{:S(2)}) copy-start(f32[1,8,8,128]{3,2,1,0:T(8,128)S(1)} %get-tuple-element.1067) | copy-start | bytes 98308
  179.4 15.9 %copy-start.70 = (f32[1,8,8,128]{3,2,1,0:T(8,128)}, f32[1,8,8,128]{3,2,1,0:T(8,128)S(1)}, u32[]{:S(2)}) copy-start(f32[1,8,8,128]{3,2,1,0:T(8,128)S(1)} %get-tuple-element.1068) | copy-start | bytes 98308
  203.9 15.7 %copy-start.75 = (f32[1,8,8,128]{3,2,1,0:T(8,128)}, f32[1,8,8,128]{3,2,1,0:T(8,128)S(1)}, u32[]{:S(2)}) copy-start(f32[1,8,8,128]{3,2,1,0:T(8,128)S(1)} %get-tuple-element.1061) | copy-start | bytes 98308
  203.9 15.7 %copy-start.76 = (f32[1,8,8,128]{3,2,1,0:T(8,128)}, f32[1,8,8,128]{3,2,1,0:T(8,128)S(1)}, u32[]{:S(2)}) copy-start(f32[1,8,8,128]{3,2,1,0:T(8,128)S(1)} %get-tuple-element.1062) | copy-start | bytes 98308
  228.2 8.2 %copy-start.83 = (f32[1,8,8,128]{3,2,1,0:T(8,128)}, f32[1,8,8,128]{3,2,1,0:T(8,128)S(1)}, u32[]{:S(2)}) copy-start(f32[1,8,8,128]{3,2,1,0:T(8,128)S(1)} %get-tuple-element.1129) | copy-start | bytes 98308
  228.2 8.2 %copy-start.84 = (f32[1,8,8,128]{3,2,1,0:T(8,128)}, f32[1,8,8,128]{3,2,1,0:T(8,128)S(1)}, u32[]{:S(2)}) copy-start(f32[1,8,8,128]{3,2,1,0:T(8,128)S(1)} %get-tuple-element.1130) | copy-start | bytes 98308
  228.2 15.9 %copy-start.81 = (f32[1,8,8,128]{3,2,1,0:T(8,128)}, f32[1,8,8,128]{3,2,1,0:T(8,128)S(1)}, u32[]{:S(2)}) copy-start(f32[1,8,8,128]{3,2,1,0:T(8,128)S(1)} %get-tuple-element.1055) | copy-start | bytes 98308
  228.2 15.9 %copy-start.82 = (f32[1,8,8,128]{3,2,1,0:T(8,128)}, f32[1,8,8,128]{3,2,1,0:T(8,128)S(1)}, u32[]{:S(2)}) copy-start(f32[1,8,8,128]{3,2,1,0:T(8,128)S(1)} %get-tuple-element.1056) | copy-start | bytes 98308
  252.9 8.2 %copy-start.89 = (f32[1,8,8,128]{3,2,1,0:T(8,128)}, f32[1,8,8,128]{3,2,1,0:T(8,128)S(1)}, u32[]{:S(2)}) copy-start(f32[1,8,8,128]{3,2,1,0:T(8,128)S(1)} %get-tuple-element.1125) | copy-start | bytes 98308
  252.9 8.2 %copy-start.90 = (f32[1,8,8,128]{3,2,1,0:T(8,128)}, f32[1,8,8,128]{3,2,1,0:T(8,128)S(1)}, u32[]{:S(2)}) copy-start(f32[1,8,8,128]{3,2,1,0:T(8,128)S(1)} %get-tuple-element.1126) | copy-start | bytes 98308
  252.9 15.8 %copy-start.87 = (f32[1,8,8,128]{3,2,1,0:T(8,128)}, f32[1,8,8,128]{3,2,1,0:T(8,128)S(1)}, u32[]{:S(2)}) copy-start(f32[1,8,8,128]{3,2,1,0:T(8,128)S(1)} %get-tuple-element.1049) | copy-start | bytes 98308
  252.9 15.8 %copy-start.88 = (f32[1,8,8,128]{3,2,1,0:T(8,128)}, f32[1,8,8,128]{3,2,1,0:T(8,128)S(1)}, u32[]{:S(2)}) copy-start(f32[1,8,8,128]{3,2,1,0:T(8,128)S(1)} %get-tuple-element.1050) | copy-start | bytes 98308
  277.9 8.1 %copy-start.95 = (f32[1,8,8,128]{3,2,1,0:T(8,128)}, f32[1,8,8,128]{3,2,1,0:T(8,128)S(1)}, u32[]{:S(2)}) copy-start(f32[1,8,8,128]{3,2,1,0:T(8,128)S(1)} %get-tuple-element.1121) | copy-start | bytes 98308
  277.9 8.1 %copy-start.96 = (f32[1,8,8,128]{3,2,1,0:T(8,128)}, f32[1,8,8,128]{3,2,1,0:T(8,128)S(1)}, u32[]{:S(2)}) copy-start(f32[1,8,8,128]{3,2,1,0:T(8,128)S(1)} %get-tuple-element.1122) | copy-start | bytes 98308
  277.9 173.7 %copy-start.93 = (f32[1,8,8,128]{3,2,1,0:T(8,128)}, f32[1,8,8,128]{3,2,1,0:T(8,128)S(1)}, u32[]{:S(2)}) copy-start(f32[1,8,8,128]{3,2,1,0:T(8,128)S(1)} %get-tuple-element.1007) | copy-start | bytes 98308
  295.2 8.1 %copy-start.101 = (f32[1,8,8,128]{3,2,1,0:T(8,128)}, f32[1,8,8,128]{3,2,1,0:T(8,128)S(1)}, u32[]{:S(2)}) copy-start(f32[1,8,8,128]{3,2,1,0:T(8,128)S(1)} %get-tuple-element.1117) | copy-start | bytes 98308
  295.2 8.1 %copy-start.102 = (f32[1,8,8,128]{3,2,1,0:T(8,128)}, f32[1,8,8,128]{3,2,1,0:T(8,128)S(1)}, u32[]{:S(2)}) copy-start(f32[1,8,8,128]{3,2,1,0:T(8,128)S(1)} %get-tuple-element.1118) | copy-start | bytes 98308
  312.4 8.1 %copy-start.107 = (f32[1,8,8,128]{3,2,1,0:T(8,128)}, f32[1,8,8,128]{3,2,1,0:T(8,128)S(1)}, u32[]{:S(2)}) copy-start(f32[1,8,8,128]{3,2,1,0:T(8,128)S(1)} %get-tuple-element.1113) | copy-start | bytes 98308
  312.4 8.1 %copy-start.108 = (f32[1,8,8,128]{3,2,1,0:T(8,128)}, f32[1,8,8,128]{3,2,1,0:T(8,128)S(1)}, u32[]{:S(2)}) copy-start(f32[1,8,8,128]{3,2,1,0:T(8,128)S(1)} %get-tuple-element.1114) | copy-start | bytes 98308
  329.7 8.2 %copy-start.113 = (f32[1,8,8,128]{3,2,1,0:T(8,128)}, f32[1,8,8,128]{3,2,1,0:T(8,128)S(1)}, u32[]{:S(2)}) copy-start(f32[1,8,8,128]{3,2,1,0:T(8,128)S(1)} %get-tuple-element.1109) | copy-start | bytes 98308
  329.7 8.2 %copy-start.114 = (f32[1,8,8,128]{3,2,1,0:T(8,128)}, f32[1,8,8,128]{3,2,1,0:T(8,128)S(1)}, u32[]{:S(2)}) copy-start(f32[1,8,8,128]{3,2,1,0:T(8,128)S(1)} %get-tuple-element.1110) | copy-start | bytes 98308
  347.1 8.2 %copy-start.119 = (f32[1,8,8,128]{3,2,1,0:T(8,128)}, f32[1,8,8,128]{3,2,1,0:T(8,128)S(1)}, u32[]{:S(2)}) copy-start(f32[1,8,8,128]{3,2,1,0:T(8,128)S(1)} %get-tuple-element.1105) | copy-start | bytes 98308
  347.1 8.2 %copy-start.120 = (f32[1,8,8,128]{3,2,1,0:T(8,128)}, f32[1,8,8,128]{3,2,1,0:T(8,128)S(1)}, u32[]{:S(2)}) copy-start(f32[1,8,8,128]{3,2,1,0:T(8,128)S(1)} %get-tuple-element.1106) | copy-start | bytes 98308
  364.5 8.3 %copy-start.125 = (f32[1,8,8,128]{3,2,1,0:T(8,128)}, f32[1,8,8,128]{3,2,1,0:T(8,128)S(1)}, u32[]{:S(2)}) copy-start(f32[1,8,8,128]{3,2,1,0:T(8,128)S(1)} %get-tuple-element.1101) | copy-start | bytes 98308
  381.9 8.2 %copy-start.131 = (f32[1,8,8,128]{3,2,1,0:T(8,128)}, f32[1,8,8,128]{3,2,1,0:T(8,128)S(1)}, u32[]{:S(2)}) copy-start(f32[1,8,8,128]{3,2,1,0:T(8,128)S(1)} %get-tuple-element.1097) | copy-start | bytes 98308
  382.0 8.2 %copy-start.132 = (f32[1,8,8,128]{3,2,1,0:T(8,128)}, f32[1,8,8,128]{3,2,1,0:T(8,128)S(1)}, u32[]{:S(2)}) copy-start(f32[1,8,8,128]{3,2,1,0:T(8,128)S(1)} %get-tuple-element.1098) | copy-start | bytes 98308
  399.6 8.2 %copy-start.137 = (f32[1,8,8,128]{3,2,1,0:T(8,128)}, f32[1,8,8,128]{3,2,1,0:T(8,128)S(1)}, u32[]{:S(2)}) copy-start(f32[1,8,8,128]{3,2,1,0:T(8,128)S(1)} %get-tuple-element.1093) | copy-start | bytes 98308
  435.8 8.1 %copy-start.150 = (f32[1,8,8,128]{3,2,1,0:T(8,128)}, f32[1,8,8,128]{3,2,1,0:T(8,128)S(1)}, u32[]{:S(2)}) copy-start(f32[1,8,8,128]{3,2,1,0:T(8,128)S(1)} %get-tuple-element.1083) | copy-start | bytes 98308
  435.8 8.1 %copy-start.151 = (f32[1,8,8,128]{3,2,1,0:T(8,128)}, f32[1,8,8,128]{3,2,1,0:T(8,128)S(1)}, u32[]{:S(2)}) copy-start(f32[1,8,8,128]{3,2,1,0:T(8,128)S(1)} %get-tuple-element.1084) | copy-start | bytes 98308
  520.8 15.3 %copy-start.55 = (f32[1,8,8,128]{3,2,1,0:T(8,128)S(1)}, f32[1,8,8,128]{3,2,1,0:T(8,128)}, u32[]{:S(2)}) copy-start(f32[1,8,8,128]{3,2,1,0:T(8,128)} %get-tuple-element.807) | copy-start | bytes 98308
  528.4 15.7 %copy-start.23 = (f32[1,8,8,128]{3,2,1,0:T(8,128)S(1)}, f32[1,8,8,128]{3,2,1,0:T(8,128)}, u32[]{:S(2)}) copy-start(f32[1,8,8,128]{3,2,1,0:T(8,128)} %copy-done.22) | copy-start | bytes 98308
  528.4 15.7 %copy-start.26 = (f32[1,8,8,128]{3,2,1,0:T(8,128)S(1)}, f32[1,8,8,128]{3,2,1,0:T(8,128)}, u32[]{:S(2)}) copy-start(f32[1,8,8,128]{3,2,1,0:T(8,128)} %copy-done.25) | copy-start | bytes 98308
  528.5 15.6 %copy-start.42 = (f32[1,8,8,128]{3,2,1,0:T(8,128)S(1)}, f32[1,8,8,128]{3,2,1,0:T(8,128)}, u32[]{:S(2)}) copy-start(f32[1,8,8,128]{3,2,1,0:T(8,128)} %get-tuple-element.863) | copy-start | bytes 98308
  528.5 15.6 %copy-start.44 = (f32[1,8,8,128]{3,2,1,0:T(8,128)S(1)}, f32[1,8,8,128]{3,2,1,0:T(8,128)}, u32[]{:S(2)}) copy-start(f32[1,8,8,128]{3,2,1,0:T(8,128)} %get-tuple-element.959) | copy-start | bytes 98308
  528.5 15.6 %copy-start.47 = (f32[1,8,8,128]{3,2,1,0:T(8,128)S(1)}, f32[1,8,8,128]{3,2,1,0:T(8,128)}, u32[]{:S(2)}) copy-start(f32[1,8,8,128]{3,2,1,0:T(8,128)} %get-tuple-element.935) | copy-start | bytes 98308
  528.5 15.6 %copy-start.49 = (f32[1,8,8,128]{3,2,1,0:T(8,128)S(1)}, f32[1,8,8,128]{3,2,1,0:T(8,128)}, u32[]{:S(2)}) copy-start(f32[1,8,8,128]{3,2,1,0:T(8,128)} %get-tuple-element.875) | copy-start | bytes 98308
  528.6 15.6 %copy-start.51 = (f32[1,8,8,128]{3,2,1,0:T(8,128)S(1)}, f32[1,8,8,128]{3,2,1,0:T(8,128)}, u32[]{:S(2)}) copy-start(f32[1,8,8,128]{3,2,1,0:T(8,128)} %get-tuple-element.965) | copy-start | bytes 98308
  528.6 15.6 %copy-start.54 = (f32[1,8,8,128]{3,2,1,0:T(8,128)S(1)}, f32[1,8,8,128]{3,2,1,0:T(8,128)}, u32[]{:S(2)}) copy-start(f32[1,8,8,128]{3,2,1,0:T(8,128)} %get-tuple-element.941) | copy-start | bytes 98308
  528.6 15.6 %copy-start.57 = (f32[1,8,8,128]{3,2,1,0:T(8,128)S(1)}, f32[1,8,8,128]{3,2,1,0:T(8,128)}, u32[]{:S(2)}) copy-start(f32[1,8,8,128]{3,2,1,0:T(8,128)} %copy-done.56) | copy-start | bytes 98308
  528.6 15.6 %copy-start.60 = (f32[1,8,8,128]{3,2,1,0:T(8,128)S(1)}, f32[1,8,8,128]{3,2,1,0:T(8,128)}, u32[]{:S(2)}) copy-start(f32[1,8,8,128]{3,2,1,0:T(8,128)} %get-tuple-element.951) | copy-start | bytes 98308
  528.6 15.6 %copy-start.66 = (f32[1,8,8,128]{3,2,1,0:T(8,128)S(1)}, f32[1,8,8,128]{3,2,1,0:T(8,128)}, u32[]{:S(2)}) copy-start(f32[1,8,8,128]{3,2,1,0:T(8,128)} %copy-done.65) | copy-start | bytes 98308
  528.6 15.6 %copy-start.68 = (f32[1,8,8,128]{3,2,1,0:T(8,128)S(1)}, f32[1,8,8,128]{3,2,1,0:T(8,128)}, u32[]{:S(2)}) copy-start(f32[1,8,8,128]{3,2,1,0:T(8,128)} %copy-done.67) | copy-start | bytes 98308
  536.1 8.1 %copy-start.62 = (f32[1,8,8,128]{3,2,1,0:T(8,128)S(1)}, f32[1,8,8,128]{3,2,1,0:T(8,128)}, u32[]{:S(2)}) copy-start(f32[1,8,8,128]{3,2,1,0:T(8,128)} %copy-done.61) | copy-start | bytes 98308
  536.2 8.1 %copy-start.64 = (f32[1,8,8,128]{3,2,1,0:T(8,128)S(1)}, f32[1,8,8,128]{3,2,1,0:T(8,128)}, u32[]{:S(2)}) copy-start(f32[1,8,8,128]{3,2,1,0:T(8,128)} %copy-done.63) | copy-start | bytes 98308
  554.8 7.5 %collective-permute-start.5 = (f32[3,3,14,134]{3,2,1,0:T(8,128)S(1)}, f32[3,3,14,134]{3,2,1,0:T(8,128)S(1)}, u32[]{:S(2)}, u32[]{:S(2)}) collective-permute-start(f32[3,3,14,134]{3,2,1,0:T(8,128)S(1)} %slice.4792), channel_id=1, source_target_pairs={{0,8},{8,16},{16,24},{1,9},{9,17},{17,25},{2,10},{10,18},{18,26},{... | collective-permute-start | bytes 202616 | tf_op jit(solution)/shard_map/ppermute | solution.py:33
  562.3 7.4 %collective-permute-start.6 = (f32[3,8,3,134]{3,2,1,0:T(4,128)S(1)}, f32[3,8,3,134]{3,2,1,0:T(4,128)S(1)}, u32[]{:S(2)}, u32[]{:S(2)}) collective-permute-start(f32[3,8,3,134]{3,2,1,0:T(4,128)S(1)} %get-tuple-element.1184), channel_id=1, source_target_pairs={{2,0},{4,2},{6,4},{3,1},{5,3},{7,5},{10,8},{12,10},{14,12},{11,9},... | collective-permute-start | bytes 115784 | tf_op jit(solution)/shard_map/ppermute | solution.py:33
  566.6 7.4 %collective-permute-start.7 = (f32[3,8,3,134]{3,2,1,0:T(4,128)S(1)}, f32[3,8,3,134]{3,2,1,0:T(4,128)S(1)}, u32[]{:S(2)}, u32[]{:S(2)}) collective-permute-start(f32[3,8,3,134]{3,2,1,0:T(4,128)S(1)} %get-tuple-element.1183), channel_id=1, source_target_pairs={{0,2},{2,4},{4,6},{1,3},{3,5},{5,7},{8,10},{10,12},{12,14},{9,11},... | collective-permute-start | bytes 115784 | tf_op jit(solution)/shard_map/ppermute | solution.py:33
  574.4 4.4 collective-permute-start.8
  575.8 6.7 %collective-permute-start.9 = (f32[3,8,8,3]{3,2,1,0:T(8,128)S(1)}, f32[3,8,8,3]{3,2,1,0:T(8,128)S(1)}, u32[]{:S(2)}, u32[]{:S(2)}) collective-permute-start(f32[3,8,8,3]{3,2,1,0:T(8,128)S(1)} %get-tuple-element.1199), channel_id=1, source_target_pairs={{0,1},{2,3},{4,5},{6,7},{8,9},{10,11},{12,13},{14,15},{16,17},{18,... | collective-permute-start | bytes 6920 | tf_op jit(solution)/shard_map/ppermute | solution.py:33
  (119 other events, 577.1 us)
where the time goes:
time: 595 us; the launch traced here: 585 us
  local copies, waits for them, and re-layouts  479 us (81%)
  other arithmetic  63.6 us (11%)
  starting transfers between devices  26.5 us (4%)
  waiting for transfers between devices  11.3 us (2%)
    scatter-add x61, local copies, waits for them, and re-layouts, body(): reaction = reaction.at[:, lead_x:lead_x + cells_x, lead_y:lead_y + cells_...  454 us
    another operation x51, other arithmetic, bond_force(): jnp.stack([factor * stretch_x, factor * stretch_y, factor * stretch_z])  45.2 us
    ppermute x6, starting transfers between devices, passed_along(): return lax.ppermute(block, axis, route)  17 us
  transfers between devices with their start and end apart: 10, of which 5 were waited for; matrix products, arithmetic and copies ran while one was open for 19% of the time, Pallas kernels for 0%

commit v1 on v0

v1 whole, which is shorter than its diff:
```python
import functools

import jax
import jax.numpy as jnp
from jax import lax
from jax.experimental import pallas as pl
from jax.experimental.pallas import tpu as pltpu
from jax.sharding import PartitionSpec as P

HORIZON = 3
DT_STEP = 0.25
BOND_SCALE = 5.0
LANES = 128
FRAME = 16
OWN = 4
RIM = 24


def bond_table():
    table = {}
    number = 0
    reach = range(-HORIZON, HORIZON + 1)
    for dx in reach:
        for dy in reach:
            for dz in reach:
                radius = dx * dx + dy * dy + dz * dz
                if 0 < radius <= HORIZON * HORIZON and (dx, dy, dz) > (0, 0, 0):
                    table[dx, dy, dz] = (number // 12, number % 12)
                    table[-dx, -dy, -dz] = (6 + number // 12, number % 12)
                    number += 1
    return table


BONDS = bond_table()


def lane_ids(rows):
    return lax.broadcasted_iota(jnp.int32, (rows, LANES), 1)


def rolled(block, shift):
    shift = shift % LANES
    return pltpu.roll(block, shift, axis=block.ndim - 1) if shift else block


def z_window(main, side, dz, wide):
    if not wide:
        return rolled(main, -dz)
    lane = lane_ids(main.shape[0])
    if dz > 0:
        return rolled(jnp.where(lane < dz, side, main), -dz)
    return rolled(jnp.where(lane >= LANES + dz, side, main), -dz)


def pack_margins(rows):
    lane = lane_ids(8)
    packed = jnp.zeros((8, LANES), jnp.float32)
    for group in range(3):
        moved = rolled(rows[8 * group : 8 * group + 8], 2 + 8 * group)
        packed = jnp.where((lane >= 8 * group) & (lane < 8 * group + 4), moved, packed)
    return packed


def unpack_margins(packed, group):
    lane = lane_ids(8)
    moved = rolled(packed, -(2 + 8 * group))
    return jnp.where((lane >= 126) | (lane < 2), moved, 0.0)


def advance_kernel(cells_z, disp, vel, mod, adv_out, root_out, msg_out):
    lane = lane_ids(8)
    for field in range(4):
        packed = jnp.zeros((8, LANES), jnp.float32)
        for x in range(8):
            if field < 3:
                own = disp[field, x] + DT_STEP * vel[field, x]
                adv_out[field, x] = own
            else:
                own = jnp.sqrt(mod[x])
                root_out[x] = own
            top = rolled(own, 8 * x - (cells_z - 3))
            low = rolled(own, 64 + 8 * x)
            packed = jnp.where((lane >= 8 * x) & (lane < 8 * x + 3), top, packed)
            packed = jnp.where((lane >= 64 + 8 * x) & (lane < 64 + 8 * x + 3), low, packed)
        msg_out[field] = packed


def side_kernel(cells_z, adv, root, arrived, main_out, side_out, low_out, top_out, hold):
    wide = cells_z == LANES
    lane = lane_ids(8)
    first = cells_z % LANES
    for field in range(4):
        got = arrived[field]
        for x in range(8):
            own = adv[field, x] if field < 3 else root[x]
            below = rolled(got, 125 - 8 * x)
            above = rolled(got, first - (64 + 8 * x))
            side = jnp.where((lane >= first) & (lane < first + 3), above, 0.0)
            side = jnp.where(lane >= 125, below, side)
            if not wide:
                own = jnp.where(lane < cells_z, own, side)
            main_out[field, x] = own
            side_out[field, x] = side
            low_out[field, 3 * x : 3 * x + 3] = own[:3]
            top_out[field, 3 * x : 3 * x + 3] = own[5:]
            if wide:
                hold[0, 3 * x : 3 * x + 3] = side[:3]
                hold[1, 3 * x : 3 * x + 3] = side[5:]
        if wide:
            low_out[field, RIM:] = pack_margins(hold[0])
            top_out[field, RIM:] = pack_margins(hold[1])


def frame_kernel(wide, main, side, below, above, main_out, side_out, low_out, top_out, hold):
    for field in range(4):
        if wide:
            for group in range(3):
                hold[0, 8 * group : 8 * group + 8] = unpack_margins(below[field, RIM:], group)
                hold[1, 8 * group : 8 * group + 8] = unpack_margins(above[field, RIM:], group)
        for x in range(8):
            main_out[field, x, :1] = jnp.zeros((1, LANES), jnp.float32)
            main_out[field, x, 1:OWN] = below[field, 3 * x : 3 * x + 3]
            main_out[field, x, OWN : OWN + 8] = main[field, x]
            main_out[field, x, OWN + 8 : 15] = above[field, 3 * x : 3 * x + 3]
            main_out[field, x, 15:] = jnp.zeros((1, LANES), jnp.float32)
            if wide:
                side_out[field, x, :1] = jnp.zeros((1, LANES), jnp.float32)
                side_out[field, x, 1:OWN] = hold[0, 3 * x : 3 * x + 3]
                side_out[field, x, OWN : OWN + 8] = side[field, x]
                side_out[field, x, OWN + 8 : 15] = hold[1, 3 * x : 3 * x + 3]
                side_out[field, x, 15:] = jnp.zeros((1, LANES), jnp.float32)
        for out, layers in ((low_out, (0, 1, 2)), (top_out, (7, 6, 5))):
            out[field, :12] = main_out[field, layers[0], 2:14]
            out[field, 12:24] = main_out[field, layers[1], 2:14]
            out[field, 24:32] = main_out[field, layers[2], OWN : OWN + 8]
            if wide:
                hold[2, :12] = side_out[field, layers[0], 2:14]
                hold[2, 12:24] = side_out[field, layers[1], 2:14]
                out[field, 32:] = pack_margins(hold[2])


def bond_sum(dx, own, words, far, total):
    from_x = own[0] - float(dx)
    from_z = {dz: own[2] - float(dz) for dz in range(-HORIZON, HORIZON + 1)}
    for dy in range(-HORIZON, HORIZON + 1):
        from_y = own[1] - float(dy)
        for dz in range(-HORIZON, HORIZON + 1):
            if (dx, dy, dz) not in BONDS:
                continue
            radius = float(dx * dx + dy * dy + dz * dz)
            word, bit = BONDS[dx, dy, dz]
            there = far(dy, dz)
            stretch_x = there[0] - from_x
            stretch_y = there[1] - from_y
            stretch_z = there[2] - from_z[dz]
            inverse = lax.rsqrt(stretch_x * stretch_x + stretch_y * stretch_y + stretch_z * stretch_z)
            factor = (BOND_SCALE / radius - (BOND_SCALE / radius**0.5) * inverse) * there[3]
            factor = jnp.where((words(word) & (1 << bit)) == 0, factor, 0.0)
            total = (
                total[0] + factor * stretch_x,
                total[1] + factor * stretch_y,
                total[2] + factor * stretch_z,
            )
    return total


SHIFTS = (-2, -1, 1, 2)


def inner_kernel(wide, main, side, bits, total_out, near, far):
    for field in range(4):
        for x in range(8):
            for half in range(2):
                rows = slice(8 * half, 8 * half + 8)
                block = main[field, x, rows]
                margin = side[field, x, rows] if wide else None
                for slot, dz in enumerate(SHIFTS):
                    near[slot, field, x, rows] = z_window(block, margin, dz, wide)
            rows = slice(OWN, OWN + 8)
            block = main[field, x, rows]
            margin = side[field, x, rows] if wide else None
            for slot, dz in enumerate((-3, 3)):
                far[slot, field, x] = z_window(block, margin, dz, wide)

    for dx in (0, -1, 1, -2, 2, -3, 3):

        def step(x, carry, dx=dx):
            own = [main[field, x, OWN : OWN + 8] for field in range(3)]

            def there(dy, dz):
                rows = slice(OWN + dy, OWN + dy + 8)
                if dz == 0:
                    return [main[field, x + dx, rows] for field in range(4)]
                if abs(dz) == 3:
                    return [far[int(dz > 0), field, x + dx] for field in range(4)]
                slot = SHIFTS.index(dz)
                return [near[slot, field, x + dx, rows] for field in range(4)]

            if dx == 0:
                total = (jnp.zeros((8, LANES), jnp.float32),) * 3
            else:
                total = tuple(total_out[field, x] for field in range(3))
            total = bond_sum(dx, own, lambda word: bits[word, x], there, total)
            for field in range(3):
                total_out[field, x] = total[field]
            return carry

        lax.fori_loop(max(0, -dx), min(8, 8 - dx), step, 0)


def outer_kernel(wide, main, below, above, bits, vel, partial, force_out, vel_out, layer, near, hold):
    for face, block in enumerate((below, above)):
        for field in range(4):
            layer[face, 0, field, 2:14] = block[field, :12]
            layer[face, 1, field, 2:14] = block[field, 12:24]
            if wide:
                for group in range(3):
                    hold[0, 8 * group : 8 * group + 8] = unpack_margins(block[field, 32:], group)
                hold[1, 2:14] = hold[0, :12]
                hold[2, 2:14] = hold[0, 12:24]
            for depth in range(2):
                for half in range(2):
                    rows = slice(8 * half, 8 * half + 8)
                    inner = layer[face, depth, field, rows]
                    margin = hold[1 + depth, rows] if wide else None
                    for slot, dz in enumerate(SHIFTS):
                        near[face, depth, slot, field, rows] = z_window(inner, margin, dz, wide)
    for x in range(8):
        total = tuple(partial[field, x] for field in range(3))
        own = [main[field, x, OWN : OWN + 8] for field in range(4)]
        for dx in range(-HORIZON, HORIZON + 1):
            if 0 <= x + dx < 8:
                continue
            face = 0 if dx < 0 else 1
            depth = -(x + dx) - 1 if dx < 0 else x + dx - 8
            block = below if dx < 0 else above

            def there(dy, dz, face=face, depth=depth, block=block):
                rows = slice(OWN + dy, OWN + dy + 8)
                if depth == 2:
                    return [block[field, 24:32] for field in range(4)]
                if dz == 0:
                    return [layer[face, depth, field, rows] for field in range(4)]
                slot = SHIFTS.index(dz)
                return [near[face, depth, slot, field, rows] for field in range(4)]

            total = bond_sum(dx, own, lambda word, x=x: bits[word, x], there, total)
        for field in range(3):
            force = own[3] * total[field]
            force_out[field, x] = force
            vel_out[field, x] = vel[field, x] + DT_STEP * force


def call(kernel, outs, scratch, flops, *operands):
    shapes = [jax.ShapeDtypeStruct(shape, jnp.float32) for shape in outs]
    moved = sum(4 * int(a.size) for a in operands) + sum(4 * int(a.size) for a in shapes)
    vmem = pl.BlockSpec(memory_space=pltpu.VMEM)
    return pl.pallas_call(
        kernel,
        out_shape=shapes,
        in_specs=[vmem] * len(operands),
        out_specs=[vmem] * len(shapes),
        scratch_shapes=[pltpu.VMEM(shape, jnp.float32) for shape in scratch],
        compiler_params=pltpu.CompilerParams(vmem_limit_bytes=24 * 1024 * 1024),
        cost_estimate=pl.CostEstimate(flops=flops, bytes_accessed=moved, transcendentals=0),
    )(*operands)


def traded(low, top, axis):
    count = lax.axis_size(axis)
    even = lax.axis_index(axis) % 2 == 0
    got = []
    for start, block in ((0, jnp.where(even, top, low)), (1, jnp.where(even, low, top))):
        pairs = []
        for i in range(start, count - 1, 2):
            pairs += [(i, i + 1), (i + 1, i)]
        got.append(lax.ppermute(block, axis, pairs) if pairs else jnp.zeros_like(block))
    return jnp.where(even, got[1], got[0]), jnp.where(even, got[0], got[1])


def body(displacement, velocity, micromodulus, damage_bits):
    cells_z = micromodulus.shape[2]
    wide = cells_z == LANES
    if not wide:
        pad = [(0, 0), (0, 0), (0, 0), (0, LANES - cells_z)]
        displacement, velocity, damage_bits = (
            jnp.pad(a, pad) for a in (displacement, velocity, damage_bits)
        )
        micromodulus = jnp.pad(micromodulus, pad[1:])
    brick = (8, 8, LANES)
    advanced, root, z_msg = call(
        functools.partial(advance_kernel, cells_z),
        [(3, *brick), brick, (4, 8, LANES)],
        [],
        100_000,
        displacement,
        velocity,
        micromodulus,
    )
    first_half = lax.broadcasted_iota(jnp.int32, z_msg.shape, 2) < 64
    count = lax.axis_size("gz")
    place = lax.axis_index("gz")
    if count == 2:
        other = lax.ppermute(z_msg, "gz", [(0, 1), (1, 0)])
        z_got = jnp.where(first_half == (place == 1), other, 0.0)
    else:
        before, after = traded(z_msg, z_msg, "gz")
        z_got = jnp.where(first_half, before, after)
    main, side, low, top = call(
        functools.partial(side_kernel, cells_z),
        [(4, *brick), (4, *brick), (4, RIM + 8, LANES), (4, RIM + 8, LANES)],
        [(2, RIM, LANES)],
        100_000,
        advanced,
        root,
        z_got,
    )
    below, above = traded(low, top, "gy")
    framed = (4, 8, FRAME, LANES)
    main, side, low, top = call(
        functools.partial(frame_kernel, wide),
        [framed, framed, (4, 40, LANES), (4, 40, LANES)],
        [(3, RIM, LANES)],
        100_000,
        main,
        side,
        below,
        above,
    )
    below, above = traded(low, top, "gx")
    (partial,) = call(
        functools.partial(inner_kernel, wide),
        [(3, *brick)],
        [(4, *framed), (2, 4, *brick)],
        20_000_000,
        main,
        side,
        damage_bits,
    )
    force, moved = call(
        functools.partial(outer_kernel, wide),
        [(3, *brick), (3, *brick)],
        [(2, 2, 4, FRAME, LANES), (2, 2, 4, 4, FRAME, LANES), (3, RIM, LANES)],
        4_000_000,
        main,
        below,
        above,
        damage_bits,
        velocity,
        partial,
    )
    return force[..., :cells_z], advanced[..., :cells_z], moved[..., :cells_z]


def solution(mesh):
    placed = P(None, "gx", "gy", "gz")
    return jax.shard_map(
        body,
        mesh=mesh,
        in_specs=(placed, placed, P("gx", "gy", "gz"), placed),
        out_specs=(placed, placed, placed),
        check_vma=False,
    )
```

time: 595 us -> 26.2 us (0.04)
  the two profiles are of different devices: /device:TPU:20 before, /device:TPU:12 now
where the time goes in v1:
time: 26.2 us; the launch traced here: 25.9 us
  starting transfers between devices  9.05 us (35%)
  Pallas kernels  5.93 us (23%)
  waiting for transfers between devices  5.82 us (22%)
  local copies, waits for them, and re-layouts  4.28 us (16%)
  between operations  0.77 us (3%)
    ppermute x4, starting transfers between devices, traded(): lax.ppermute(block, axis, pairs)  9.04 us
    pallas_call x5, Pallas kernels, call(): pl.pallas_call(kernel, out_shape=shapes, in_specs=[vmem] * len(operands),...  5.93 us
    ppermute x4, waiting for transfers between devices, traded(): lax.ppermute(block, axis, pairs)  4.66 us
    unnamed x12, local copies, waits for them, and re-layouts  4.28 us
    ppermute x1, waiting for transfers between devices, body(): other = lax.ppermute(z_msg, 'gz', [(0, 1), (1, 0)])  1.16 us
  transfers between devices with their start and end apart: 5, of which 3 were waited for; matrix products, arithmetic and copies ran while one was open for 0% of the time, Pallas kernels for 14%

profile of v1, /device:TPU:12, one launch (start us, length us, event | category | flops | bytes accessed | tf_op | source)
XLA Modules:
  0.0 25.9 jit_solution(4183680585507676522)
XLA Ops:
  0.6 0.0 copy-start.1
  0.6 0.9 %copy-done.1 = f32[3,8,8,128]{3,2,1,0:T(8,128)S(1)} copy-done((f32[3,8,8,128]{3,2,1,0:T(8,128)S(1)}, f32[3,8,8,128]{3,2,1,0:T(8,128)}, u32[]{:S(2)}) %copy-start.1) | copy-done | bytes 98328
  1.5 0.0 copy-start.3
  1.5 0.9 %copy-done.3 = f32[3,8,8,128]{3,2,1,0:T(8,128)S(1)} copy-done((f32[3,8,8,128]{3,2,1,0:T(8,128)S(1)}, f32[3,8,8,128]{3,2,1,0:T(8,128)}, u32[]{:S(2)}) %copy-start.3) | copy-done | bytes 98328
  2.4 0.0 copy-start.5
  2.4 0.8 %copy-done.5 = f32[8,8,128]{2,1,0:T(8,128)S(1)} copy-done((f32[8,8,128]{2,1,0:T(8,128)S(1)}, f32[8,8,128]{2,1,0:T(8,128)}, u32[]{:S(2)}) %copy-start.5) | copy-done | bytes 32792
  3.2 0.7 %shard_map.67 = (f32[3,8,8,128]{3,2,1,0:T(8,128)}, f32[8,8,128]{2,1,0:T(8,128)S(1)}, f32[4,8,128]{2,1,0:T(8,128)S(1)}) custom-call(f32[3,8,8,128]{3,2,1,0:T(8,128)S(1)} %copy-done.3, f32[3,8,8,128]{3,2,1,0:T(8,128)S(1)} %copy-done.1, f32[8,8,128]{2,1,0:T(8,128)S(1)} %copy-done.5), custom_call_target="tpu_custom_call" | custom-call | flops 100000 | bytes 376832 | tf_op jit(solution)/shard_map/pallas_call | solution.py:258
  3.9 0.0 collective-permute-start
  3.9 1.2 %collective-permute-done = f32[4,8,128]{2,1,0:T(8,128)S(1)} collective-permute-done((f32[4,8,128]{2,1,0:T(8,128)S(1)}, f32[4,8,128]{2,1,0:T(8,128)S(1)}, u32[]{:S(2)}, u32[]{:S(2)}) %collective-permute-start) | collective-permute-done | bytes 16416 | tf_op jit(solution)/shard_map/ppermute | solution.py:304
  5.0 0.0 copy-start.4
  5.0 0.9 %copy-done.4 = f32[3,8,8,128]{3,2,1,0:T(8,128)S(1)} copy-done((f32[3,8,8,128]{3,2,1,0:T(8,128)S(1)}, f32[3,8,8,128]{3,2,1,0:T(8,128)}, u32[]{:S(2)}) %copy-start.4) | copy-done | bytes 98328
  5.9 0.2 shard_map.68
  6.2 1.6 %collective-permute-start.2 = (f32[4,32,128]{2,1,0:T(8,128)S(1)}, f32[4,32,128]{2,1,0:T(8,128)S(1)}, u32[]{:S(2)}, u32[]{:S(2)}) collective-permute-start(f32[4,32,128]{2,1,0:T(8,128)S(1)} %get-tuple-element.35), channel_id=1, source_target_pairs={{0,2},{2,0},{4,6},{6,4},{1,3},{3,1},{5,7},{7,5},{8,10},{10,8},{12,... | collective-permute-start | bytes 196616 | tf_op jit(solution)/shard_map/ppermute | solution.py:277
  7.7 2.4 %collective-permute-start.1 = (f32[4,32,128]{2,1,0:T(8,128)S(1)}, f32[4,32,128]{2,1,0:T(8,128)S(1)}, u32[]{:S(2)}, u32[]{:S(2)}) collective-permute-start(f32[4,32,128]{2,1,0:T(8,128)S(1)} %get-tuple-element.36), channel_id=1, source_target_pairs={{2,4},{4,2},{3,5},{5,3},{10,12},{12,10},{11,13},{13,11},{18,20},{2... | collective-permute-start | bytes 196616 | tf_op jit(solution)/shard_map/ppermute | solution.py:277
  10.1 0.4 %collective-permute-done.2 = f32[4,32,128]{2,1,0:T(8,128)S(1)} collective-permute-done((f32[4,32,128]{2,1,0:T(8,128)S(1)}, f32[4,32,128]{2,1,0:T(8,128)S(1)}, u32[]{:S(2)}, u32[]{:S(2)}) %collective-permute-start.2) | collective-permute-done | bytes 65568 | tf_op jit(solution)/shard_map/ppermute | solution.py:277
  10.5 4.3 %collective-permute-done.1 = f32[4,32,128]{2,1,0:T(8,128)S(1)} collective-permute-done((f32[4,32,128]{2,1,0:T(8,128)S(1)}, f32[4,32,128]{2,1,0:T(8,128)S(1)}, u32[]{:S(2)}, u32[]{:S(2)}) %collective-permute-start.1) | collective-permute-done | bytes 65568 | tf_op jit(solution)/shard_map/ppermute | solution.py:277
  14.8 0.0 copy-start
  14.8 0.2 shard_map.69
  15.1 0.5 %collective-permute-start.4 = (f32[4,40,128]{2,1,0:T(8,128)S(1)}, f32[4,40,128]{2,1,0:T(8,128)S(1)}, u32[]{:S(2)}, u32[]{:S(2)}) collective-permute-start(f32[4,40,128]{2,1,0:T(8,128)S(1)} %get-tuple-element.31), channel_id=1, source_target_pairs={{0,8},{8,0},{16,24},{24,16},{1,9},{9,1},{17,25},{25,17},{2,10},{10... | collective-permute-start | bytes 245768 | tf_op jit(solution)/shard_map/ppermute | solution.py:277
  15.6 4.6 %collective-permute-start.3 = (f32[4,40,128]{2,1,0:T(8,128)S(1)}, f32[4,40,128]{2,1,0:T(8,128)S(1)}, u32[]{:S(2)}, u32[]{:S(2)}) collective-permute-start(f32[4,40,128]{2,1,0:T(8,128)S(1)} %get-tuple-element.32), channel_id=1, source_target_pairs={{8,16},{16,8},{9,17},{17,9},{10,18},{18,10},{11,19},{19,11},{12,20... | collective-permute-start | bytes 245768 | tf_op jit(solution)/shard_map/ppermute | solution.py:277
  20.2 0.0 copy-done
  20.2 3.5 %shard_map.70.partial = f32[3,8,8,128]{3,2,1,0:T(8,128)S(1)} custom-call(f32[4,8,16,128]{3,2,1,0:T(8,128)S(1)} %get-tuple-element.23.main, f32[4,8,16,128]{3,2,1,0:T(8,128)S(1)} %get-tuple-element.26.side, s32[12,8,8,128]{3,2,1,0:T(8,128)S(1)} %copy-done), custom_call_target="tpu_custom_call" | custom-call | flops 20000000 | bytes 1015808 | tf_op jit(solution)/shard_map/pallas_call | solution.py:258
  23.7 0.0 copy-start.2
  23.7 0.0 collective-permute-done.4
  23.7 0.0 collective-permute-done.3
  23.8 0.8 %copy-done.2 = f32[3,8,8,128]{3,2,1,0:T(8,128)S(1)} copy-done((f32[3,8,8,128]{3,2,1,0:T(8,128)S(1)}, f32[3,8,8,128]{3,2,1,0:T(8,128)}, u32[]{:S(2)}) %copy-start.2) | copy-done | bytes 98328
  24.6 1.3 %shard_map.71 = (f32[3,8,8,128]{3,2,1,0:T(8,128)}, f32[3,8,8,128]{3,2,1,0:T(8,128)}) custom-call(f32[4,8,16,128]{3,2,1,0:T(8,128)S(1)} %get-tuple-element.23.main, f32[4,40,128]{2,1,0:T(8,128)S(1)} %get-tuple-element.30.below, f32[4,40,128]{2,1,0:T(8,128)S(1)} %get-tuple-element.29.above, s32[12,8,8,128]{3,2,1,0:T(8,128)S(1)} %copy-done, ...), custom_call_target="tpu_custom_call" | custom-call | flops 4000000 | bytes 1212416 | tf_op jit(solution)/shard_map/pallas_call | solution.py:258
  (6 shorter events, 0.1 us)
Async XLA Ops:
  0.6 0.9 %copy-start.1 = (f32[3,8,8,128]{3,2,1,0:T(8,128)S(1)}, f32[3,8,8,128]{3,2,1,0:T(8,128)}, u32[]{:S(2)}) copy-start(f32[3,8,8,128]{3,2,1,0:T(8,128)} %vel.3) | copy-start | bytes 294916
  1.5 0.9 %copy-start.3 = (f32[3,8,8,128]{3,2,1,0:T(8,128)S(1)}, f32[3,8,8,128]{3,2,1,0:T(8,128)}, u32[]{:S(2)}) copy-start(f32[3,8,8,128]{3,2,1,0:T(8,128)} %disp.1) | copy-start | bytes 294916
  2.4 0.8 %copy-start.5 = (f32[8,8,128]{2,1,0:T(8,128)S(1)}, f32[8,8,128]{2,1,0:T(8,128)}, u32[]{:S(2)}) copy-start(f32[8,8,128]{2,1,0:T(8,128)} %mod.1) | copy-start | bytes 98308
  3.9 1.2 %collective-permute-start = (f32[4,8,128]{2,1,0:T(8,128)S(1)}, f32[4,8,128]{2,1,0:T(8,128)S(1)}, u32[]{:S(2)}, u32[]{:S(2)}) collective-permute-start(f32[4,8,128]{2,1,0:T(8,128)S(1)} %get-tuple-element.18), channel_id=1, source_target_pairs={{0,1},{1,0},{2,3},{3,2},{4,5},{5,4},{6,7},{7,6},{8,9},{9,8},{10,11... | collective-permute-start | bytes 49160 | tf_op jit(solution)/shard_map/ppermute | solution.py:304
  5.0 0.9 %copy-start.4 = (f32[3,8,8,128]{3,2,1,0:T(8,128)S(1)}, f32[3,8,8,128]{3,2,1,0:T(8,128)}, u32[]{:S(2)}) copy-start(f32[3,8,8,128]{3,2,1,0:T(8,128)} %get-tuple-element.14.adv) | copy-start | bytes 294916
  6.2 4.3 %collective-permute-start.2 = (f32[4,32,128]{2,1,0:T(8,128)S(1)}, f32[4,32,128]{2,1,0:T(8,128)S(1)}, u32[]{:S(2)}, u32[]{:S(2)}) collective-permute-start(f32[4,32,128]{2,1,0:T(8,128)S(1)} %get-tuple-element.35), channel_id=1, source_target_pairs={{0,2},{2,0},{4,6},{6,4},{1,3},{3,1},{5,7},{7,5},{8,10},{10,8},{12,... | collective-permute-start | bytes 196616 | tf_op jit(solution)/shard_map/ppermute | solution.py:277
  7.7 7.0 %collective-permute-start.1 = (f32[4,32,128]{2,1,0:T(8,128)S(1)}, f32[4,32,128]{2,1,0:T(8,128)S(1)}, u32[]{:S(2)}, u32[]{:S(2)}) collective-permute-start(f32[4,32,128]{2,1,0:T(8,128)S(1)} %get-tuple-element.36), channel_id=1, source_target_pairs={{2,4},{4,2},{3,5},{5,3},{10,12},{12,10},{11,13},{13,11},{18,20},{2... | collective-permute-start | bytes 196616 | tf_op jit(solution)/shard_map/ppermute | solution.py:277
  14.8 5.4 %copy-start = (s32[12,8,8,128]{3,2,1,0:T(8,128)S(1)}, s32[12,8,8,128]{3,2,1,0:T(8,128)}, u32[]{:S(2)}) copy-start(s32[12,8,8,128]{3,2,1,0:T(8,128)} %bits.3) | copy-start | bytes 1179652
  15.1 8.7 %collective-permute-start.4 = (f32[4,40,128]{2,1,0:T(8,128)S(1)}, f32[4,40,128]{2,1,0:T(8,128)S(1)}, u32[]{:S(2)}, u32[]{:S(2)}) collective-permute-start(f32[4,40,128]{2,1,0:T(8,128)S(1)} %get-tuple-element.31), channel_id=1, source_target_pairs={{0,8},{8,0},{16,24},{24,16},{1,9},{9,1},{17,25},{25,17},{2,10},{10... | collective-permute-start | bytes 245768 | tf_op jit(solution)/shard_map/ppermute | solution.py:277
  15.6 8.2 %collective-permute-start.3 = (f32[4,40,128]{2,1,0:T(8,128)S(1)}, f32[4,40,128]{2,1,0:T(8,128)S(1)}, u32[]{:S(2)}, u32[]{:S(2)}) collective-permute-start(f32[4,40,128]{2,1,0:T(8,128)S(1)} %get-tuple-element.32), channel_id=1, source_target_pairs={{8,16},{16,8},{9,17},{17,9},{10,18},{18,10},{11,19},{19,11},{12,20... | collective-permute-start | bytes 245768 | tf_op jit(solution)/shard_map/ppermute | solution.py:277
  23.7 0.9 %copy-start.2 = (f32[3,8,8,128]{3,2,1,0:T(8,128)S(1)}, f32[3,8,8,128]{3,2,1,0:T(8,128)}, u32[]{:S(2)}) copy-start(f32[3,8,8,128]{3,2,1,0:T(8,128)} %vel.3) | copy-start | bytes 294916

commit v2 on v1

--- a/solution.py
+++ b/solution.py
@@ -14,6 +14,7 @@
 FRAME = 16
 OWN = 4
 RIM = 24
+DEEP = 32
 
 
 def bond_table():
@@ -52,32 +53,40 @@
     return rolled(jnp.where(lane >= LANES + dz, side, main), -dz)
 
 
-def pack_margins(rows):
+def pack_margins(packed, rows, field):
     lane = lane_ids(8)
-    packed = jnp.zeros((8, LANES), jnp.float32)
     for group in range(3):
-        moved = rolled(rows[8 * group : 8 * group + 8], 2 + 8 * group)
-        packed = jnp.where((lane >= 8 * group) & (lane < 8 * group + 4), moved, packed)
+        start = 4 * (3 * field + group)
+        moved = rolled(rows[8 * group : 8 * group + 8], 2 + start)
+        packed = jnp.where((lane >= start) & (lane < start + 4), moved, packed)
     return packed
 
 
-def unpack_margins(packed, group):
+def unpack_margins(packed, field, group):
     lane = lane_ids(8)
-    moved = rolled(packed, -(2 + 8 * group))
+    moved = rolled(packed, -(2 + 4 * (3 * field + group)))
     return jnp.where((lane >= 126) | (lane < 2), moved, 0.0)
 
 
-def advance_kernel(cells_z, disp, vel, mod, adv_out, root_out, msg_out):
+def advance_kernel(cells_z, disp, vel, mod, field_out, vel_out, msg_out, hold, hold_mod, sem):
+    copies = [
+        pltpu.make_async_copy(disp, hold, sem.at[0]),
+        pltpu.make_async_copy(vel, vel_out, sem.at[1]),
+        pltpu.make_async_copy(mod, hold_mod, sem.at[2]),
+    ]
+    for copy in copies:
+        copy.start()
+    for copy in copies:
+        copy.wait()
     lane = lane_ids(8)
     for field in range(4):
         packed = jnp.zeros((8, LANES), jnp.float32)
         for x in range(8):
             if field < 3:
-                own = disp[field, x] + DT_STEP * vel[field, x]
-                adv_out[field, x] = own
+                own = hold[field, x] + DT_STEP * vel_out[field, x]
             else:
-                own = jnp.sqrt(mod[x])
-                root_out[x] = own
+                own = jnp.sqrt(hold_mod[x])
+            field_out[field, x] = own
             top = rolled(own, 8 * x - (cells_z - 3))
             low = rolled(own, 64 + 8 * x)
             packed = jnp.where((lane >= 8 * x) & (lane < 8 * x + 3), top, packed)
@@ -85,43 +94,49 @@
         msg_out[field] = packed
 
 
-def side_kernel(cells_z, adv, root, arrived, main_out, side_out, low_out, top_out, hold):
+def side_kernel(cells_z, fields, arrived, main_out, side_out, low_out, top_out, hold):
     wide = cells_z == LANES
     lane = lane_ids(8)
     first = cells_z % LANES
+    packed = [jnp.zeros((8, LANES), jnp.float32)] * 2
     for field in range(4):
         got = arrived[field]
         for x in range(8):
-            own = adv[field, x] if field < 3 else root[x]
+            own = fields[field, x]
             below = rolled(got, 125 - 8 * x)
             above = rolled(got, first - (64 + 8 * x))
             side = jnp.where((lane >= first) & (lane < first + 3), above, 0.0)
             side = jnp.where(lane >= 125, below, side)
             if not wide:
                 own = jnp.where(lane < cells_z, own, side)
+            row = RIM * field + 3 * x
             main_out[field, x] = own
             side_out[field, x] = side
-            low_out[field, 3 * x : 3 * x + 3] = own[:3]
-            top_out[field, 3 * x : 3 * x + 3] = own[5:]
+            low_out[row : row + 3] = own[:3]
+            top_out[row : row + 3] = own[5:]
             if wide:
                 hold[0, 3 * x : 3 * x + 3] = side[:3]
                 hold[1, 3 * x : 3 * x + 3] = side[5:]
         if wide:
-            low_out[field, RIM:] = pack_margins(hold[0])
-            top_out[field, RIM:] = pack_margins(hold[1])
+            packed = [pack_margins(packed[face], hold[face], field) for face in range(2)]
+    low_out[4 * RIM :] = packed[0]
+    top_out[4 * RIM :] = packed[1]
 
 
 def frame_kernel(wide, main, side, below, above, main_out, side_out, low_out, top_out, hold):
+    packed = [jnp.zeros((8, LANES), jnp.float32)] * 2
     for field in range(4):
         if wide:
-            for group in range(3):
-                hold[0, 8 * group : 8 * group + 8] = unpack_margins(below[field, RIM:], group)
-                hold[1, 8 * group : 8 * group + 8] = unpack_margins(above[field, RIM:], group)
+            for face, block in enumerate((below, above)):
+                for group in range(3):
+                    rows = slice(8 * group, 8 * group + 8)
+                    hold[face, rows] = unpack_margins(block[4 * RIM :], field, group)
         for x in range(8):
+            row = RIM * field + 3 * x
             main_out[field, x, :1] = jnp.zeros((1, LANES), jnp.float32)
-            main_out[field, x, 1:OWN] = below[field, 3 * x : 3 * x + 3]
+            main_out[field, x, 1:OWN] = below[row : row + 3]
             main_out[field, x, OWN : OWN + 8] = main[field, x]
-            main_out[field, x, OWN + 8 : 15] = above[field, 3 * x : 3 * x + 3]
+            main_out[field, x, OWN + 8 : 15] = above[row : row + 3]
             main_out[field, x, 15:] = jnp.zeros((1, LANES), jnp.float32)
             if wide:
                 side_out[field, x, :1] = jnp.zeros((1, LANES), jnp.float32)
@@ -129,14 +144,17 @@
                 side_out[field, x, OWN : OWN + 8] = side[field, x]
                 side_out[field, x, OWN + 8 : 15] = hold[1, 3 * x : 3 * x + 3]
                 side_out[field, x, 15:] = jnp.zeros((1, LANES), jnp.float32)
-        for out, layers in ((low_out, (0, 1, 2)), (top_out, (7, 6, 5))):
-            out[field, :12] = main_out[field, layers[0], 2:14]
-            out[field, 12:24] = main_out[field, layers[1], 2:14]
-            out[field, 24:32] = main_out[field, layers[2], OWN : OWN + 8]
+        for face, (out, layers) in enumerate(((low_out, (0, 1, 2)), (top_out, (7, 6, 5)))):
+            row = DEEP * field
+            out[row : row + 12] = main_out[field, layers[0], 2:14]
+            out[row + 12 : row + 24] = main_out[field, layers[1], 2:14]
+            out[row + 24 : row + 32] = main_out[field, layers[2], OWN : OWN + 8]
             if wide:
-                hold[2, :12] = side_out[field, layers[0], 2:14]
-                hold[2, 12:24] = side_out[field, layers[1], 2:14]
-                out[field, 32:] = pack_margins(hold[2])
+                hold[2 + face, :12] = side_out[field, layers[0], 2:14]
+                hold[2 + face, 12:24] = side_out[field, layers[1], 2:14]
+                packed[face] = pack_margins(packed[face], hold[2 + face], field)
+    low_out[4 * DEEP :] = packed[0]
+    top_out[4 * DEEP :] = packed[1]
 
 
 def bond_sum(dx, own, words, far, total):
@@ -167,7 +185,9 @@
 SHIFTS = (-2, -1, 1, 2)
 
 
-def inner_kernel(wide, main, side, bits, total_out, near, far):
+def inner_kernel(wide, main, side, bits, fields, total_out, next_out, near, far, sem):
+    copy = pltpu.make_async_copy(fields.at[:3], next_out, sem)
+    copy.start()
     for field in range(4):
         for x in range(8):
             for half in range(2):
@@ -206,16 +226,34 @@
             return carry
 
         lax.fori_loop(max(0, -dx), min(8, 8 - dx), step, 0)
-
-
-def outer_kernel(wide, main, below, above, bits, vel, partial, force_out, vel_out, layer, near, hold):
+    copy.wait()
+
+
+def outer_kernel(
+    wide, main, below, above, bits, vel, partial, force_out, vel_out, layer, near, hold, force_buf, vel_buf, sem
+):
+    copies = []
+
+    def finish(x, total, root):
+        for field in range(3):
+            force = root * total[field]
+            force_buf[x, field] = force
+            vel_buf[x, field] = vel[field, x] + DT_STEP * force
+        for slot, (buf, out) in enumerate(((force_buf, force_out), (vel_buf, vel_out))):
+            copies.append(pltpu.make_async_copy(buf.at[x], out.at[:, x], sem.at[slot, x]))
+            copies[-1].start()
+
+    for x in (3, 4):
+        finish(x, [partial[field, x] for field in range(3)], main[3, x, OWN : OWN + 8])
     for face, block in enumerate((below, above)):
         for field in range(4):
-            layer[face, 0, field, 2:14] = block[field, :12]
-            layer[face, 1, field, 2:14] = block[field, 12:24]
+            row = DEEP * field
+            layer[face, 0, field, 2:14] = block[row : row + 12]
+            layer[face, 1, field, 2:14] = block[row + 12 : row + 24]
             if wide:
                 for group in range(3):
-                    hold[0, 8 * group : 8 * group + 8] = unpack_margins(block[field, 32:], group)
+                    rows = slice(8 * group, 8 * group + 8)
+                    hold[0, rows] = unpack_margins(block[4 * DEEP :], field, group)
                 hold[1, 2:14] = hold[0, :12]
                 hold[2, 2:14] = hold[0, 12:24]
             for depth in range(2):
@@ -225,7 +263,7 @@
                     margin = hold[1 + depth, rows] if wide else None
                     for slot, dz in enumerate(SHIFTS):
                         near[face, depth, slot, field, rows] = z_window(inner, margin, dz, wide)
-    for x in range(8):
+    for x in (2, 5, 1, 6, 0, 7):
         total = tuple(partial[field, x] for field in range(3))
         own = [main[field, x, OWN : OWN + 8] for field in range(4)]
         for dx in range(-HORIZON, HORIZON + 1):
@@ -238,35 +276,37 @@
             def there(dy, dz, face=face, depth=depth, block=block):
                 rows = slice(OWN + dy, OWN + dy + 8)
                 if depth == 2:
-                    return [block[field, 24:32] for field in range(4)]
+                    return [block[DEEP * field + 24 : DEEP * field + 32] for field in range(4)]
                 if dz == 0:
                     return [layer[face, depth, field, rows] for field in range(4)]
                 slot = SHIFTS.index(dz)
                 return [near[face, depth, slot, field, rows] for field in range(4)]
 
             total = bond_sum(dx, own, lambda word, x=x: bits[word, x], there, total)
-        for field in range(3):
-            force = own[3] * total[field]
-            force_out[field, x] = force
-            vel_out[field, x] = vel[field, x] + DT_STEP * force
-
-
-def call(kernel, outs, scratch, flops, *operands):
-    shapes = [jax.ShapeDtypeStruct(shape, jnp.float32) for shape in outs]
+        finish(x, total, own[3])
+    for copy in copies:
+        copy.wait()
+
+
+VMEM = pl.BlockSpec(memory_space=pltpu.VMEM)
+HBM = pl.BlockSpec(memory_space=pltpu.HBM)
+
+
+def call(kernel, ins, outs, scratch, flops, *operands):
+    shapes = [jax.ShapeDtypeStruct(shape, jnp.float32) for shape, _ in outs]
     moved = sum(4 * int(a.size) for a in operands) + sum(4 * int(a.size) for a in shapes)
-    vmem = pl.BlockSpec(memory_space=pltpu.VMEM)
     return pl.pallas_call(
         kernel,
         out_shape=shapes,
-        in_specs=[vmem] * len(operands),
-        out_specs=[vmem] * len(shapes),
-        scratch_shapes=[pltpu.VMEM(shape, jnp.float32) for shape in scratch],
+        in_specs=ins,
+        out_specs=[place for _, place in outs],
+        scratch_shapes=[pltpu.VMEM(a, jnp.float32) if isinstance(a, tuple) else a for a in scratch],
         compiler_params=pltpu.CompilerParams(vmem_limit_bytes=24 * 1024 * 1024),
         cost_estimate=pl.CostEstimate(flops=flops, bytes_accessed=moved, transcendentals=0),
     )(*operands)
 
 
-def traded(low, top, axis):
+def traded(low, top, axis, middle_first):
     count = lax.axis_size(axis)
     even = lax.axis_index(axis) % 2 == 0
     got = []
@@ -275,7 +315,11 @@
         for i in range(start, count - 1, 2):
             pairs += [(i, i + 1), (i + 1, i)]
         got.append(lax.ppermute(block, axis, pairs) if pairs else jnp.zeros_like(block))
-    return jnp.where(even, got[1], got[0]), jnp.where(even, got[0], got[1])
+    if middle_first:
+        outer, middle = lax.optimization_barrier((got[0], got[1]))
+    else:
+        middle, outer = lax.optimization_barrier((got[1], got[0]))
+    return jnp.where(even, middle, outer), jnp.where(even, outer, middle)
 
 
 def body(displacement, velocity, micromodulus, damage_bits):
@@ -288,14 +332,13 @@
         )
         micromodulus = jnp.pad(micromodulus, pad[1:])
     brick = (8, 8, LANES)
-    advanced, root, z_msg = call(
+    fields, kept, z_msg = call(
         functools.partial(advance_kernel, cells_z),
-        [(3, *brick), brick, (4, 8, LANES)],
-        [],
+        [HBM] * 3,
+        [((4, *brick), VMEM), ((3, *brick), VMEM), ((4, 8, LANES), VMEM)],
+        [(3, *brick), brick, pltpu.SemaphoreType.DMA((3,))],
         100_000,
-        displacement,
-        velocity,
-        micromodulus,
+        *(pltpu.with_memory_space_constraint(a, pltpu.HBM) for a in (displacement, velocity, micromodulus)),
     )
     first_half = lax.broadcasted_iota(jnp.int32, z_msg.shape, 2) < 64
     count = lax.axis_size("gz")
@@ -304,49 +347,62 @@
         other = lax.ppermute(z_msg, "gz", [(0, 1), (1, 0)])
         z_got = jnp.where(first_half == (place == 1), other, 0.0)
     else:
-        before, after = traded(z_msg, z_msg, "gz")
+        before, after = traded(z_msg, z_msg, "gz", False)
         z_got = jnp.where(first_half, before, after)
+    rim_msg = ((4 * RIM + 8, LANES), VMEM)
     main, side, low, top = call(
         functools.partial(side_kernel, cells_z),
-        [(4, *brick), (4, *brick), (4, RIM + 8, LANES), (4, RIM + 8, LANES)],
+        [VMEM] * 2,
+        [((4, *brick), VMEM), ((4, *brick), VMEM), rim_msg, rim_msg],
         [(2, RIM, LANES)],
         100_000,
-        advanced,
-        root,
+        fields,
         z_got,
     )
-    below, above = traded(low, top, "gy")
+    below, above = traded(low, top, "gy", False)
     framed = (4, 8, FRAME, LANES)
+    deep_msg = ((4 * DEEP + 8, LANES), VMEM)
     main, side, low, top = call(
         functools.partial(frame_kernel, wide),
-        [framed, framed, (4, 40, LANES), (4, 40, LANES)],
-        [(3, RIM, LANES)],
+        [VMEM] * 4,
+        [(framed, VMEM), (framed, VMEM), deep_msg, deep_msg],
+        [(4, RIM, LANES)],
         100_000,
         main,
         side,
         below,
         above,
     )
-    below, above = traded(low, top, "gx")
-    (partial,) = call(
+    below, above = traded(low, top, "gx", True)
+    partial, advanced = call(
         functools.partial(inner_kernel, wide),
-        [(3, *brick)],
-        [(4, *framed), (2, 4, *brick)],
+        [VMEM] * 4,
+        [((3, *brick), VMEM), ((3, *brick), HBM)],
+        [(4, *framed), (2, 4, *brick), pltpu.SemaphoreType.DMA],
         20_000_000,
         main,
         side,
         damage_bits,
+        fields,
     )
     force, moved = call(
         functools.partial(outer_kernel, wide),
-        [(3, *brick), (3, *brick)],
-        [(2, 2, 4, FRAME, LANES), (2, 2, 4, 4, FRAME, LANES), (3, RIM, LANES)],
+        [VMEM] * 6,
+        [((3, *brick), HBM), ((3, *brick), HBM)],
+        [
+            (2, 2, 4, FRAME, LANES),
+            (2, 2, 4, 4, FRAME, LANES),
+            (3, RIM, LANES),
+            (8, 3, 8, LANES),
+            (8, 3, 8, LANES),
+            pltpu.SemaphoreType.DMA((2, 8)),
+        ],
         4_000_000,
         main,
         below,
         above,
         damage_bits,
-        velocity,
+        kept,
         partial,
     )
     return force[..., :cells_z], advanced[..., :cells_z], moved[..., :cells_z]

time: 26.2 us -> 22.2 us (0.85)
  the two profiles are of different devices: /device:TPU:12 before, /device:TPU:4 now
where the time goes in v2:
time: 22.2 us; the launch traced here: 22.1 us
  starting transfers between devices  8.66 us (39%)
  Pallas kernels  6.46 us (29%)
  waiting for transfers between devices  6.12 us (28%)
  between operations  0.77 us (3%)
    ppermute x4, starting transfers between devices, traded(): lax.ppermute(block, axis, pairs)  8.59 us
    pallas_call x5, Pallas kernels, call(): pl.pallas_call(kernel, out_shape=shapes, in_specs=ins, out_specs=[place f...  6.46 us
    ppermute x4, waiting for transfers between devices, traded(): lax.ppermute(block, axis, pairs)  4.98 us
    ppermute x1, waiting for transfers between devices, body(): other = lax.ppermute(z_msg, 'gz', [(0, 1), (1, 0)])  1.14 us
  transfers between devices with their start and end apart: 5, of which 3 were waited for; matrix products, arithmetic and copies ran while one was open for 0% of the time, Pallas kernels for 16%

profile of v2, /device:TPU:4, one launch (start us, length us, event | category | flops | bytes accessed | tf_op | source)
XLA Modules:
  0.0 22.1 jit_solution(9409832290136990777)
XLA Ops:
  0.6 1.1 %shard_map.67 = (f32[4,8,8,128]{3,2,1,0:T(8,128)S(1)}, f32[3,8,8,128]{3,2,1,0:T(8,128)S(1)}, f32[4,8,128]{2,1,0:T(8,128)S(1)}) custom-call(f32[3,8,8,128]{3,2,1,0:T(8,128)} %disp.1, f32[3,8,8,128]{3,2,1,0:T(8,128)} %vel.1, f32[8,8,128]{2,1,0:T(8,128)} %mod.1), custom_call_target="tpu_custom_call" | custom-call | flops 100000 | bytes 475136 | tf_op jit(solution)/shard_map/pallas_call | solution.py:298
  1.7 0.1 collective-permute-start
  1.9 1.1 %collective-permute-done = f32[4,8,128]{2,1,0:T(8,128)S(1)} collective-permute-done((f32[4,8,128]{2,1,0:T(8,128)S(1)}, f32[4,8,128]{2,1,0:T(8,128)S(1)}, u32[]{:S(2)}, u32[]{:S(2)}) %collective-permute-start) | collective-permute-done | bytes 16416 | tf_op jit(solution)/shard_map/ppermute | solution.py:347
  3.0 0.2 %shard_map.68 = (f32[4,8,8,128]{3,2,1,0:T(8,128)S(1)}, f32[4,8,8,128]{3,2,1,0:T(8,128)S(1)}, f32[104,128]{1,0:T(8,128)S(1)}, f32[104,128]{1,0:T(8,128)S(1)}) custom-call(f32[4,8,8,128]{3,2,1,0:T(8,128)S(1)} %get-tuple-element.22.fields, f32[4,8,128]{2,1,0:T(8,128)S(1)} %broadcast_select_fusion.8.arrived), custom_call_target="tpu_custom_call" | custom-call | flops 100000 | bytes 516096 | tf_op jit(solution)/shard_map/pallas_call | solution.py:298
  3.2 1.6 %collective-permute-start.2 = (f32[104,128]{1,0:T(8,128)S(1)}, f32[104,128]{1,0:T(8,128)S(1)}, u32[]{:S(2)}, u32[]{:S(2)}) collective-permute-start(f32[104,128]{1,0:T(8,128)S(1)} %get-tuple-element.47), channel_id=1, source_target_pairs={{0,2},{2,0},{4,6},{6,4},{1,3},{3,1},{5,7},{7,5},{8,10},{10,8},{12,... | collective-permute-start | bytes 159752 | tf_op jit(solution)/shard_map/ppermute | solution.py:317
  4.8 1.9 %collective-permute-start.1 = (f32[104,128]{1,0:T(8,128)S(1)}, f32[104,128]{1,0:T(8,128)S(1)}, u32[]{:S(2)}, u32[]{:S(2)}) collective-permute-start(f32[104,128]{1,0:T(8,128)S(1)} %get-tuple-element.48), channel_id=1, source_target_pairs={{2,4},{4,2},{3,5},{5,3},{10,12},{12,10},{11,13},{13,11},{18,20},{2... | collective-permute-start | bytes 159752 | tf_op jit(solution)/shard_map/ppermute | solution.py:317
  6.7 0.0 copy-start
  6.7 0.7 %collective-permute-done.2 = f32[104,128]{1,0:T(8,128)S(1)} collective-permute-done((f32[104,128]{1,0:T(8,128)S(1)}, f32[104,128]{1,0:T(8,128)S(1)}, u32[]{:S(2)}, u32[]{:S(2)}) %collective-permute-start.2) | collective-permute-done | bytes 53280 | tf_op jit(solution)/shard_map/ppermute | solution.py:317
  7.4 4.3 %collective-permute-done.1 = f32[104,128]{1,0:T(8,128)S(1)} collective-permute-done((f32[104,128]{1,0:T(8,128)S(1)}, f32[104,128]{1,0:T(8,128)S(1)}, u32[]{:S(2)}, u32[]{:S(2)}) %collective-permute-start.1) | collective-permute-done | bytes 53280 | tf_op jit(solution)/shard_map/ppermute | solution.py:317
  11.7 0.2 shard_map.69
  12.0 0.7 %collective-permute-start.4 = (f32[136,128]{1,0:T(8,128)S(1)}, f32[136,128]{1,0:T(8,128)S(1)}, u32[]{:S(2)}, u32[]{:S(2)}) collective-permute-start(f32[136,128]{1,0:T(8,128)S(1)} %get-tuple-element.43), channel_id=1, source_target_pairs={{8,16},{16,8},{9,17},{17,9},{10,18},{18,10},{11,19},{19,11},{12,20... | collective-permute-start | bytes 208904 | tf_op jit(solution)/shard_map/ppermute | solution.py:317
  12.6 4.5 %collective-permute-start.3 = (f32[136,128]{1,0:T(8,128)S(1)}, f32[136,128]{1,0:T(8,128)S(1)}, u32[]{:S(2)}, u32[]{:S(2)}) collective-permute-start(f32[136,128]{1,0:T(8,128)S(1)} %get-tuple-element.44), channel_id=1, source_target_pairs={{0,8},{8,0},{16,24},{24,16},{1,9},{9,1},{17,25},{25,17},{2,10},{10... | collective-permute-start | bytes 208904 | tf_op jit(solution)/shard_map/ppermute | solution.py:317
  17.1 0.0 copy-done
  17.1 3.5 %shard_map.70 = (f32[3,8,8,128]{3,2,1,0:T(8,128)S(1)}, f32[3,8,8,128]{3,2,1,0:T(8,128)}) custom-call(f32[4,8,16,128]{3,2,1,0:T(8,128)S(1)} %get-tuple-element.30.main, f32[4,8,16,128]{3,2,1,0:T(8,128)S(1)} %get-tuple-element.36.side, s32[12,8,8,128]{3,2,1,0:T(8,128)S(1)} %copy-done, f32[4,8,8,128]{3,2,1,0:T(8,128)S(1)} %get-tuple-element.22.fields), custom_call_target="tpu_custom_call" | custom-call | flops 20000000 | bytes 1245184 | tf_op jit(solution)/shard_map/pallas_call | solution.py:298
  20.6 0.0 collective-permute-done.4
  20.7 0.0 collective-permute-done.3
  20.7 1.4 %shard_map.71 = (f32[3,8,8,128]{3,2,1,0:T(8,128)}, f32[3,8,8,128]{3,2,1,0:T(8,128)}) custom-call(f32[4,8,16,128]{3,2,1,0:T(8,128)S(1)} %get-tuple-element.30.main, f32[136,128]{1,0:T(8,128)S(1)} %get-tuple-element.42.below, f32[136,128]{1,0:T(8,128)S(1)} %get-tuple-element.41.above, s32[12,8,8,128]{3,2,1,0:T(8,128)S(1)} %copy-done, ...), custom_call_target="tpu_custom_call" | custom-call | flops 4000000 | bytes 1187840 | tf_op jit(solution)/shard_map/pallas_call | solution.py:298
  (6 shorter events, 0.1 us)
Async XLA Ops:
  1.7 1.2 %collective-permute-start = (f32[4,8,128]{2,1,0:T(8,128)S(1)}, f32[4,8,128]{2,1,0:T(8,128)S(1)}, u32[]{:S(2)}, u32[]{:S(2)}) collective-permute-start(f32[4,8,128]{2,1,0:T(8,128)S(1)} %get-tuple-element.23), channel_id=1, source_target_pairs={{0,1},{1,0},{2,3},{3,2},{4,5},{5,4},{6,7},{7,6},{8,9},{9,8},{10,11... | collective-permute-start | bytes 49160 | tf_op jit(solution)/shard_map/ppermute | solution.py:347
  3.2 4.2 %collective-permute-start.2 = (f32[104,128]{1,0:T(8,128)S(1)}, f32[104,128]{1,0:T(8,128)S(1)}, u32[]{:S(2)}, u32[]{:S(2)}) collective-permute-start(f32[104,128]{1,0:T(8,128)S(1)} %get-tuple-element.47), channel_id=1, source_target_pairs={{0,2},{2,0},{4,6},{6,4},{1,3},{3,1},{5,7},{7,5},{8,10},{10,8},{12,... | collective-permute-start | bytes 159752 | tf_op jit(solution)/shard_map/ppermute | solution.py:317
  4.8 6.9 %collective-permute-start.1 = (f32[104,128]{1,0:T(8,128)S(1)}, f32[104,128]{1,0:T(8,128)S(1)}, u32[]{:S(2)}, u32[]{:S(2)}) collective-permute-start(f32[104,128]{1,0:T(8,128)S(1)} %get-tuple-element.48), channel_id=1, source_target_pairs={{2,4},{4,2},{3,5},{5,3},{10,12},{12,10},{11,13},{13,11},{18,20},{2... | collective-permute-start | bytes 159752 | tf_op jit(solution)/shard_map/ppermute | solution.py:317
  6.7 10.4 %copy-start = (s32[12,8,8,128]{3,2,1,0:T(8,128)S(1)}, s32[12,8,8,128]{3,2,1,0:T(8,128)}, u32[]{:S(2)}) copy-start(s32[12,8,8,128]{3,2,1,0:T(8,128)} %bits.3) | copy-start | bytes 1179652
  12.0 8.7 %collective-permute-start.4 = (f32[136,128]{1,0:T(8,128)S(1)}, f32[136,128]{1,0:T(8,128)S(1)}, u32[]{:S(2)}, u32[]{:S(2)}) collective-permute-start(f32[136,128]{1,0:T(8,128)S(1)} %get-tuple-element.43), channel_id=1, source_target_pairs={{8,16},{16,8},{9,17},{17,9},{10,18},{18,10},{11,19},{19,11},{12,20... | collective-permute-start | bytes 208904 | tf_op jit(solution)/shard_map/ppermute | solution.py:317
  12.6 8.0 %collective-permute-start.3 = (f32[136,128]{1,0:T(8,128)S(1)}, f32[136,128]{1,0:T(8,128)S(1)}, u32[]{:S(2)}, u32[]{:S(2)}) collective-permute-start(f32[136,128]{1,0:T(8,128)S(1)} %get-tuple-element.44), channel_id=1, source_target_pairs={{0,8},{8,0},{16,24},{24,16},{1,9},{9,1},{17,25},{25,17},{2,10},{10... | collective-permute-start | bytes 208904 | tf_op jit(solution)/shard_map/ppermute | solution.py:317

commit v3 on v2

--- a/solution.py
+++ b/solution.py
@@ -123,7 +123,7 @@
     top_out[4 * RIM :] = packed[1]
 
 
-def frame_kernel(wide, main, side, below, above, main_out, side_out, low_out, top_out, hold):
+def deep_kernel(wide, main, side, below, above, low_out, top_out, hold):
     packed = [jnp.zeros((8, LANES), jnp.float32)] * 2
     for field in range(4):
         if wide:
@@ -131,36 +131,29 @@
                 for group in range(3):
                     rows = slice(8 * group, 8 * group + 8)
                     hold[face, rows] = unpack_margins(block[4 * RIM :], field, group)
-        for x in range(8):
-            row = RIM * field + 3 * x
-            main_out[field, x, :1] = jnp.zeros((1, LANES), jnp.float32)
-            main_out[field, x, 1:OWN] = below[row : row + 3]
-            main_out[field, x, OWN : OWN + 8] = main[field, x]
-            main_out[field, x, OWN + 8 : 15] = above[row : row + 3]
-            main_out[field, x, 15:] = jnp.zeros((1, LANES), jnp.float32)
+        for face, (out, layers) in enumerate(((low_out, (0, 1, 2)), (top_out, (7, 6, 5)))):
+            for depth, x in enumerate(layers[:2]):
+                row = DEEP * field + 12 * depth
+                rim = RIM * field + 3 * x
+                out[row : row + 2] = below[rim + 1 : rim + 3]
+                out[row + 2 : row + 10] = main[field, x]
+                out[row + 10 : row + 12] = above[rim : rim + 2]
+                if wide:
+                    row = 12 * depth
+                    hold[2 + face, row : row + 2] = hold[0, 3 * x + 1 : 3 * x + 3]
+                    hold[2 + face, row + 2 : row + 10] = side[field, x]
+                    hold[2 + face, row + 10 : row + 12] = hold[1, 3 * x : 3 * x + 2]
+            out[DEEP * field + 24 : DEEP * field + 32] = main[field, layers[2]]
             if wide:
-                side_out[field, x, :1] = jnp.zeros((1, LANES), jnp.float32)
-                side_out[field, x, 1:OWN] = hold[0, 3 * x : 3 * x + 3]
-                side_out[field, x, OWN : OWN + 8] = side[field, x]
-                side_out[field, x, OWN + 8 : 15] = hold[1, 3 * x : 3 * x + 3]
-                side_out[field, x, 15:] = jnp.zeros((1, LANES), jnp.float32)
-        for face, (out, layers) in enumerate(((low_out, (0, 1, 2)), (top_out, (7, 6, 5)))):
-            row = DEEP * field
-            out[row : row + 12] = main_out[field, layers[0], 2:14]
-            out[row + 12 : row + 24] = main_out[field, layers[1], 2:14]
-            out[row + 24 : row + 32] = main_out[field, layers[2], OWN : OWN + 8]
-            if wide:
-                hold[2 + face, :12] = side_out[field, layers[0], 2:14]
-                hold[2 + face, 12:24] = side_out[field, layers[1], 2:14]
                 packed[face] = pack_margins(packed[face], hold[2 + face], field)
     low_out[4 * DEEP :] = packed[0]
     top_out[4 * DEEP :] = packed[1]
 
 
-def bond_sum(dx, own, words, far, total):
+def bond_sum(dx, own, words, far, total, rows=range(-HORIZON, HORIZON + 1)):
     from_x = own[0] - float(dx)
     from_z = {dz: own[2] - float(dz) for dz in range(-HORIZON, HORIZON + 1)}
-    for dy in range(-HORIZON, HORIZON + 1):
+    for dy in rows:
         from_y = own[1] - float(dy)
         for dz in range(-HORIZON, HORIZON + 1):
             if (dx, dy, dz) not in BONDS:
@@ -185,52 +178,82 @@
 SHIFTS = (-2, -1, 1, 2)
 
 
-def inner_kernel(wide, main, side, bits, fields, total_out, next_out, near, far, sem):
+def inner_sum(x, rows, bits, own, total, field_rows, near, far):
+    def words(word):
+        return bits[word, x]
+
+    for dx in (0, -1, 1, -2, 2, -3, 3):
+        if 0 <= x + dx < 8:
+
+            def there(dy, dz, dx=dx):
+                if dz == 0:
+                    return [field_rows(field, x + dx, dy) for field in range(4)]
+                if abs(dz) == 3:
+                    return [far[int(dz > 0), field, x + dx] for field in range(4)]
+                rows = slice(OWN + dy, OWN + dy + 8)
+                return [near[SHIFTS.index(dz), field, x + dx, rows] for field in range(4)]
+
+            total = bond_sum(dx, own, words, there, total, rows)
+    return total
+
+
+def first_kernel(wide, main, side, bits, fields, partial_out, near_out, frame_out, next_out, far, sem):
     copy = pltpu.make_async_copy(fields.at[:3], next_out, sem)
     copy.start()
+    own_rows = slice(OWN, OWN + 8)
     for field in range(4):
         for x in range(8):
-            for half in range(2):
-                rows = slice(8 * half, 8 * half + 8)
-                block = main[field, x, rows]
-                margin = side[field, x, rows] if wide else None
-                for slot, dz in enumerate(SHIFTS):
-                    near[slot, field, x, rows] = z_window(block, margin, dz, wide)
-            rows = slice(OWN, OWN + 8)
-            block = main[field, x, rows]
-            margin = side[field, x, rows] if wide else None
+            block = main[field, x]
+            margin = side[field, x] if wide else None
+            frame_out[field, x, own_rows] = block
+            for slot, dz in enumerate(SHIFTS):
+                near_out[slot, field, x, own_rows] = z_window(block, margin, dz, wide)
             for slot, dz in enumerate((-3, 3)):
                 far[slot, field, x] = z_window(block, margin, dz, wide)
-
-    for dx in (0, -1, 1, -2, 2, -3, 3):
-
-        def step(x, carry, dx=dx):
-            own = [main[field, x, OWN : OWN + 8] for field in range(3)]
-
-            def there(dy, dz):
-                rows = slice(OWN + dy, OWN + dy + 8)
-                if dz == 0:
-                    return [main[field, x + dx, rows] for field in range(4)]
-                if abs(dz) == 3:
-                    return [far[int(dz > 0), field, x + dx] for field in range(4)]
-                slot = SHIFTS.index(dz)
-                return [near[slot, field, x + dx, rows] for field in range(4)]
-
-            if dx == 0:
-                total = (jnp.zeros((8, LANES), jnp.float32),) * 3
-            else:
-                total = tuple(total_out[field, x] for field in range(3))
-            total = bond_sum(dx, own, lambda word: bits[word, x], there, total)
-            for field in range(3):
-                total_out[field, x] = total[field]
-            return carry
-
-        lax.fori_loop(max(0, -dx), min(8, 8 - dx), step, 0)
+    for x in range(8):
+        own = [main[field, x] for field in range(3)]
+        total = (jnp.zeros((8, LANES), jnp.float32),) * 3
+
+        def field_rows(field, layer, dy):
+            return main[field, layer]
+
+        total = inner_sum(x, (0,), bits, own, total, field_rows, near_out, far)
+        for field in range(3):
+            partial_out[field, x] = total[field]
     copy.wait()
 
 
+def second_kernel(wide, below, above, bits, partial, near, frame, partial_out, near_out, frame_out, hold):
+    for face, block in enumerate((below, above)):
+        for field in range(4):
+            for group in range(3):
+                row = RIM * field + 8 * group
+                rows = block[row : row + 8]
+                margin = unpack_margins(block[4 * RIM :], field, group) if wide else None
+                for slot, dz in enumerate(SHIFTS):
+                    hold[face, slot, field, 8 * group : 8 * group + 8] = z_window(rows, margin, dz, wide)
+    for field in range(4):
+        for x in range(8):
+            row = RIM * field + 3 * x
+            frame_out[field, x, 1:OWN] = below[row : row + 3]
+            frame_out[field, x, OWN + 8 : 15] = above[row : row + 3]
+            for slot in range(4):
+                near_out[slot, field, x, 2:OWN] = hold[0, slot, field, 3 * x + 1 : 3 * x + 3]
+                near_out[slot, field, x, OWN + 8 : 14] = hold[1, slot, field, 3 * x : 3 * x + 2]
+    for x in range(8):
+        own = [frame_out[field, x, OWN : OWN + 8] for field in range(3)]
+        total = tuple(partial[field, x] for field in range(3))
+
+        def field_rows(field, layer, dy):
+            return frame_out[field, layer, OWN + dy : OWN + dy + 8]
+
+        total = inner_sum(x, (-3, -2, -1, 1, 2, 3), bits, own, total, field_rows, near_out, None)
+        for field in range(3):
+            partial_out[field, x] = total[field]
+
+
 def outer_kernel(
-    wide, main, below, above, bits, vel, partial, force_out, vel_out, layer, near, hold, force_buf, vel_buf, sem
+    wide, fields, below, above, bits, vel, partial, force_out, vel_out, layer, near, hold, force_buf, vel_buf, sem
 ):
     copies = []
 
@@ -244,7 +267,7 @@
             copies[-1].start()
 
     for x in (3, 4):
-        finish(x, [partial[field, x] for field in range(3)], main[3, x, OWN : OWN + 8])
+        finish(x, [partial[field, x] for field in range(3)], fields[3, x])
     for face, block in enumerate((below, above)):
         for field in range(4):
             row = DEEP * field
@@ -265,7 +288,7 @@
                         near[face, depth, slot, field, rows] = z_window(inner, margin, dz, wide)
     for x in (2, 5, 1, 6, 0, 7):
         total = tuple(partial[field, x] for field in range(3))
-        own = [main[field, x, OWN : OWN + 8] for field in range(4)]
+        own = [fields[field, x] for field in range(4)]
         for dx in range(-HORIZON, HORIZON + 1):
             if 0 <= x + dx < 8:
                 continue
@@ -292,7 +315,7 @@
 HBM = pl.BlockSpec(memory_space=pltpu.HBM)
 
 
-def call(kernel, ins, outs, scratch, flops, *operands):
+def call(kernel, ins, outs, scratch, flops, *operands, aliases=()):
     shapes = [jax.ShapeDtypeStruct(shape, jnp.float32) for shape, _ in outs]
     moved = sum(4 * int(a.size) for a in operands) + sum(4 * int(a.size) for a in shapes)
     return pl.pallas_call(
@@ -301,12 +324,17 @@
         in_specs=ins,
         out_specs=[place for _, place in outs],
         scratch_shapes=[pltpu.VMEM(a, jnp.float32) if isinstance(a, tuple) else a for a in scratch],
+        input_output_aliases=dict(aliases),
         compiler_params=pltpu.CompilerParams(vmem_limit_bytes=24 * 1024 * 1024),
         cost_estimate=pl.CostEstimate(flops=flops, bytes_accessed=moved, transcendentals=0),
     )(*operands)
 
 
-def traded(low, top, axis, middle_first):
+Y_TURNED = False
+X_TURNED = True
+
+
+def traded(low, top, axis, turned):
     count = lax.axis_size(axis)
     even = lax.axis_index(axis) % 2 == 0
     got = []
@@ -315,7 +343,7 @@
         for i in range(start, count - 1, 2):
             pairs += [(i, i + 1), (i + 1, i)]
         got.append(lax.ppermute(block, axis, pairs) if pairs else jnp.zeros_like(block))
-    if middle_first:
+    if turned:
         outer, middle = lax.optimization_barrier((got[0], got[1]))
     else:
         middle, outer = lax.optimization_barrier((got[1], got[0]))
@@ -359,13 +387,26 @@
         fields,
         z_got,
     )
-    below, above = traded(low, top, "gy", False)
-    framed = (4, 8, FRAME, LANES)
+    below, above = traded(low, top, "gy", Y_TURNED)
+    near = ((4, 4, 8, FRAME, LANES), VMEM)
+    framed = ((4, 8, FRAME, LANES), VMEM)
+    partial, windows, frame, advanced = call(
+        functools.partial(first_kernel, wide),
+        [VMEM] * 4,
+        [((3, *brick), VMEM), near, framed, ((3, *brick), HBM)],
+        [(2, 4, *brick), pltpu.SemaphoreType.DMA],
+        5_000_000,
+        main,
+        side,
+        damage_bits,
+        fields,
+    )
+    below, above, partial = lax.optimization_barrier((below, above, partial))
     deep_msg = ((4 * DEEP + 8, LANES), VMEM)
-    main, side, low, top = call(
-        functools.partial(frame_kernel, wide),
+    low, top = call(
+        functools.partial(deep_kernel, wide),
         [VMEM] * 4,
-        [(framed, VMEM), (framed, VMEM), deep_msg, deep_msg],
+        [deep_msg, deep_msg],
         [(4, RIM, LANES)],
         100_000,
         main,
@@ -373,17 +414,21 @@
         below,
         above,
     )
-    below, above = traded(low, top, "gx", True)
-    partial, advanced = call(
-        functools.partial(inner_kernel, wide),
-        [VMEM] * 4,
-        [((3, *brick), VMEM), ((3, *brick), HBM)],
-        [(4, *framed), (2, 4, *brick), pltpu.SemaphoreType.DMA],
+    rim_below, rim_above = below, above
+    below, above = traded(low, top, "gx", X_TURNED)
+    partial, _, _ = call(
+        functools.partial(second_kernel, wide),
+        [VMEM] * 6,
+        [((3, *brick), VMEM), near, framed],
+        [(2, 4, 4, RIM, LANES)],
         20_000_000,
-        main,
-        side,
+        rim_below,
+        rim_above,
         damage_bits,
-        fields,
+        partial,
+        windows,
+        frame,
+        aliases=((4, 1), (5, 2)),
     )
     force, moved = call(
         functools.partial(outer_kernel, wide),
@@ -398,7 +443,7 @@
             pltpu.SemaphoreType.DMA((2, 8)),
         ],
         4_000_000,
-        main,
+        fields,
         below,
         above,
         damage_bits,

time: 22.2 us -> 20.8 us (0.937)
  the two profiles are of different devices: /device:TPU:4 before, /device:TPU:16 now
where the time goes in v3:
time: 20.8 us; the launch traced here: 20.6 us
  starting transfers between devices  8.58 us (41%)
  Pallas kernels  5.78 us (28%)
  waiting for transfers between devices  5.47 us (26%)
  between operations  0.75 us (4%)
    ppermute x4, starting transfers between devices, traded(): lax.ppermute(block, axis, pairs)  8.51 us
    pallas_call x6, Pallas kernels, call(): pl.pallas_call(kernel, out_shape=shapes, in_specs=ins, out_specs=[place f...  5.78 us
    ppermute x4, waiting for transfers between devices, traded(): lax.ppermute(block, axis, pairs)  4.33 us
    ppermute x1, waiting for transfers between devices, body(): other = lax.ppermute(z_msg, 'gz', [(0, 1), (1, 0)])  1.14 us
  transfers between devices with their start and end apart: 5, of which 3 were waited for; matrix products, arithmetic and copies ran while one was open for 0% of the time, Pallas kernels for 14%

profile of v3, /device:TPU:16, one launch (start us, length us, event | category | flops | bytes accessed | tf_op | source)
XLA Modules:
  0.0 20.6 jit_solution(4793056099953249415)
XLA Ops:
  0.6 0.0 copy-start
  0.6 1.2 %shard_map.67 = (f32[4,8,8,128]{3,2,1,0:T(8,128)S(1)}, f32[3,8,8,128]{3,2,1,0:T(8,128)S(1)}, f32[4,8,128]{2,1,0:T(8,128)S(1)}) custom-call(f32[3,8,8,128]{3,2,1,0:T(8,128)} %disp.1, f32[3,8,8,128]{3,2,1,0:T(8,128)} %vel.1, f32[8,8,128]{2,1,0:T(8,128)} %mod.1), custom_call_target="tpu_custom_call" | custom-call | flops 100000 | bytes 475136 | tf_op jit(solution)/shard_map/pallas_call | solution.py:321
  1.8 0.1 collective-permute-start
  1.9 1.1 %collective-permute-done = f32[4,8,128]{2,1,0:T(8,128)S(1)} collective-permute-done((f32[4,8,128]{2,1,0:T(8,128)S(1)}, f32[4,8,128]{2,1,0:T(8,128)S(1)}, u32[]{:S(2)}, u32[]{:S(2)}) %collective-permute-start) | collective-permute-done | bytes 16416 | tf_op jit(solution)/shard_map/ppermute | solution.py:375
  3.1 0.2 %shard_map.68 = (f32[4,8,8,128]{3,2,1,0:T(8,128)S(1)}, f32[4,8,8,128]{3,2,1,0:T(8,128)S(1)}, f32[104,128]{1,0:T(8,128)S(1)}, f32[104,128]{1,0:T(8,128)S(1)}) custom-call(f32[4,8,8,128]{3,2,1,0:T(8,128)S(1)} %get-tuple-element.26.fields, f32[4,8,128]{2,1,0:T(8,128)S(1)} %broadcast_select_fusion.8.arrived), custom_call_target="tpu_custom_call" | custom-call | flops 100000 | bytes 516096 | tf_op jit(solution)/shard_map/pallas_call | solution.py:321
  3.3 0.7 %collective-permute-start.1 = (f32[104,128]{1,0:T(8,128)S(1)}, f32[104,128]{1,0:T(8,128)S(1)}, u32[]{:S(2)}, u32[]{:S(2)}) collective-permute-start(f32[104,128]{1,0:T(8,128)S(1)} %get-tuple-element.56), channel_id=1, source_target_pairs={{2,4},{4,2},{3,5},{5,3},{10,12},{12,10},{11,13},{13,11},{18,20},{2... | collective-permute-start | bytes 159752 | tf_op jit(solution)/shard_map/ppermute | solution.py:345
  4.0 4.3 %collective-permute-start.2 = (f32[104,128]{1,0:T(8,128)S(1)}, f32[104,128]{1,0:T(8,128)S(1)}, u32[]{:S(2)}, u32[]{:S(2)}) collective-permute-start(f32[104,128]{1,0:T(8,128)S(1)} %get-tuple-element.55), channel_id=1, source_target_pairs={{0,2},{2,0},{4,6},{6,4},{1,3},{3,1},{5,7},{7,5},{8,10},{10,8},{12,... | collective-permute-start | bytes 159752 | tf_op jit(solution)/shard_map/ppermute | solution.py:345
  8.3 0.0 copy-done
  8.3 0.7 %shard_map.69 = (f32[3,8,8,128]{3,2,1,0:T(8,128)S(1)}, f32[4,4,8,16,128]{4,3,2,1,0:T(8,128)S(1)}, f32[4,8,16,128]{3,2,1,0:T(8,128)S(1)}, f32[3,8,8,128]{3,2,1,0:T(8,128)}) custom-call(f32[4,8,8,128]{3,2,1,0:T(8,128)S(1)} %get-tuple-element.28.main, f32[4,8,8,128]{3,2,1,0:T(8,128)S(1)} %get-tuple-element.29.side, s32[12,8,8,128]{3,2,1,0:T(8,128)S(1)} %copy-done, ...), custom_call_target="tpu_custom_call" | custom-call | flops 5000000 | bytes 2293760 | tf_op jit(solution)/shard_map/pallas_call | solution.py:321
  9.0 0.0 collective-permute-done.1
  9.0 2.2 %collective-permute-done.2 = f32[104,128]{1,0:T(8,128)S(1)} collective-permute-done((f32[104,128]{1,0:T(8,128)S(1)}, f32[104,128]{1,0:T(8,128)S(1)}, u32[]{:S(2)}, u32[]{:S(2)}) %collective-permute-start.2) | collective-permute-done | bytes 53280 | tf_op jit(solution)/shard_map/ppermute | solution.py:345
  11.2 0.2 shard_map.70
  11.4 1.6 %collective-permute-start.3 = (f32[136,128]{1,0:T(8,128)S(1)}, f32[136,128]{1,0:T(8,128)S(1)}, u32[]{:S(2)}, u32[]{:S(2)}) collective-permute-start(f32[136,128]{1,0:T(8,128)S(1)} %get-tuple-element.52), channel_id=1, source_target_pairs={{0,8},{8,0},{16,24},{24,16},{1,9},{9,1},{17,25},{25,17},{2,10},{10... | collective-permute-start | bytes 208904 | tf_op jit(solution)/shard_map/ppermute | solution.py:345
  13.1 1.9 %collective-permute-start.4 = (f32[136,128]{1,0:T(8,128)S(1)}, f32[136,128]{1,0:T(8,128)S(1)}, u32[]{:S(2)}, u32[]{:S(2)}) collective-permute-start(f32[136,128]{1,0:T(8,128)S(1)} %get-tuple-element.51), channel_id=1, source_target_pairs={{8,16},{16,8},{9,17},{17,9},{10,18},{18,10},{11,19},{19,11},{12,20... | collective-permute-start | bytes 208904 | tf_op jit(solution)/shard_map/ppermute | solution.py:345
  15.0 2.1 %shard_map.71 = (f32[3,8,8,128]{3,2,1,0:T(8,128)S(1)}, f32[4,4,8,16,128]{4,3,2,1,0:T(8,128)S(1)}, f32[4,8,16,128]{3,2,1,0:T(8,128)S(1)}) custom-call(f32[104,128]{1,0:T(8,128)S(1)} %get-tuple-element.35.below, f32[104,128]{1,0:T(8,128)S(1)} %get-tuple-element.36.above, s32[12,8,8,128]{3,2,1,0:T(8,128)S(1)} %copy-done, ...), custom_call_target="tpu_custom_call", output_to_operand_aliasing={{1}: (4, {}), {2}: (5, {})} | custom-call | flops 20000000 | bytes 3317760 | tf_op jit(solution)/shard_map/pallas_call | solution.py:321
  17.1 0.0 collective-permute-done.3
  17.1 2.2 %collective-permute-done.4 = f32[136,128]{1,0:T(8,128)S(1)} collective-permute-done((f32[136,128]{1,0:T(8,128)S(1)}, f32[136,128]{1,0:T(8,128)S(1)}, u32[]{:S(2)}, u32[]{:S(2)}) %collective-permute-start.4) | collective-permute-done | bytes 69664 | tf_op jit(solution)/shard_map/ppermute | solution.py:345
  19.3 1.4 %shard_map.72 = (f32[3,8,8,128]{3,2,1,0:T(8,128)}, f32[3,8,8,128]{3,2,1,0:T(8,128)}) custom-call(f32[4,8,8,128]{3,2,1,0:T(8,128)S(1)} %get-tuple-element.26.fields, f32[136,128]{1,0:T(8,128)S(1)} %get-tuple-element.50.below, f32[136,128]{1,0:T(8,128)S(1)} %get-tuple-element.49.above, s32[12,8,8,128]{3,2,1,0:T(8,128)S(1)} %copy-done, ...), custom_call_target="tpu_custom_call" | custom-call | flops 4000000 | bytes 1056768 | tf_op jit(solution)/shard_map/pallas_call | solution.py:321
  (6 shorter events, 0.1 us)
Async XLA Ops:
  0.6 7.6 %copy-start = (s32[12,8,8,128]{3,2,1,0:T(8,128)S(1)}, s32[12,8,8,128]{3,2,1,0:T(8,128)}, u32[]{:S(2)}) copy-start(s32[12,8,8,128]{3,2,1,0:T(8,128)} %bits.5) | copy-start | bytes 1179652
  1.8 1.2 %collective-permute-start = (f32[4,8,128]{2,1,0:T(8,128)S(1)}, f32[4,8,128]{2,1,0:T(8,128)S(1)}, u32[]{:S(2)}, u32[]{:S(2)}) collective-permute-start(f32[4,8,128]{2,1,0:T(8,128)S(1)} %get-tuple-element.27), channel_id=1, source_target_pairs={{0,1},{1,0},{2,3},{3,2},{4,5},{5,4},{6,7},{7,6},{8,9},{9,8},{10,11... | collective-permute-start | bytes 49160 | tf_op jit(solution)/shard_map/ppermute | solution.py:375
  3.3 5.7 %collective-permute-start.1 = (f32[104,128]{1,0:T(8,128)S(1)}, f32[104,128]{1,0:T(8,128)S(1)}, u32[]{:S(2)}, u32[]{:S(2)}) collective-permute-start(f32[104,128]{1,0:T(8,128)S(1)} %get-tuple-element.56), channel_id=1, source_target_pairs={{2,4},{4,2},{3,5},{5,3},{10,12},{12,10},{11,13},{13,11},{18,20},{2... | collective-permute-start | bytes 159752 | tf_op jit(solution)/shard_map/ppermute | solution.py:345
  4.0 7.2 %collective-permute-start.2 = (f32[104,128]{1,0:T(8,128)S(1)}, f32[104,128]{1,0:T(8,128)S(1)}, u32[]{:S(2)}, u32[]{:S(2)}) collective-permute-start(f32[104,128]{1,0:T(8,128)S(1)} %get-tuple-element.55), channel_id=1, source_target_pairs={{0,2},{2,0},{4,6},{6,4},{1,3},{3,1},{5,7},{7,5},{8,10},{10,8},{12,... | collective-permute-start | bytes 159752 | tf_op jit(solution)/shard_map/ppermute | solution.py:345
  11.4 5.7 %collective-permute-start.3 = (f32[136,128]{1,0:T(8,128)S(1)}, f32[136,128]{1,0:T(8,128)S(1)}, u32[]{:S(2)}, u32[]{:S(2)}) collective-permute-start(f32[136,128]{1,0:T(8,128)S(1)} %get-tuple-element.52), channel_id=1, source_target_pairs={{0,8},{8,0},{16,24},{24,16},{1,9},{9,1},{17,25},{25,17},{2,10},{10... | collective-permute-start | bytes 208904 | tf_op jit(solution)/shard_map/ppermute | solution.py:345
  13.1 6.2 %collective-permute-start.4 = (f32[136,128]{1,0:T(8,128)S(1)}, f32[136,128]{1,0:T(8,128)S(1)}, u32[]{:S(2)}, u32[]{:S(2)}) collective-permute-start(f32[136,128]{1,0:T(8,128)S(1)} %get-tuple-element.51), channel_id=1, source_target_pairs={{8,16},{16,8},{9,17},{17,9},{10,18},{18,10},{11,19},{19,11},{12,20... | collective-permute-start | bytes 208904 | tf_op jit(solution)/shard_map/ppermute | solution.py:345

commit v4 on v2

v4 whole, which is shorter than its diff:
```python
import functools

import jax
import jax.numpy as jnp
from jax import lax
from jax.experimental import pallas as pl
from jax.experimental.pallas import tpu as pltpu
from jax.sharding import PartitionSpec as P

HORIZON = 3
DT_STEP = 0.25
BOND_SCALE = 5.0
LANES = 128
ROWS = 64
FRAME = 16
OWN = 4
CORE = slice(OWN, OWN + 8)
RIM = 24
DEEP = 32
SHIFTS = (-2, -1, 1, 2)
REACH = range(-HORIZON, HORIZON + 1)


def bond_table():
    table = {}
    number = 0
    for dx in REACH:
        for dy in REACH:
            for dz in REACH:
                radius = dx * dx + dy * dy + dz * dz
                if 0 < radius <= HORIZON * HORIZON and (dx, dy, dz) > (0, 0, 0):
                    table[dx, dy, dz] = (number // 12, number % 12)
                    table[-dx, -dy, -dz] = (6 + number // 12, number % 12)
                    number += 1
    return table


BONDS = bond_table()


def lane_ids():
    return lax.broadcasted_iota(jnp.int32, (8, LANES), 1)


def nothing():
    return jnp.zeros((8, LANES), jnp.float32)


def layer_rows(x):
    return slice(8 * x, 8 * x + 8)


def across(y):
    return pl.ds(y, 8, stride=8)


def rolled(block, shift):
    shift = shift % LANES
    return pltpu.roll(block, shift, axis=1) if shift else block


def z_window(main, side, dz, wide):
    if not wide:
        return rolled(main, -dz)
    lane = lane_ids()
    if dz > 0:
        return rolled(jnp.where(lane < dz, side, main), -dz)
    return rolled(jnp.where(lane >= LANES + dz, side, main), -dz)


def pack_margins(packed, rows, field, group):
    lane = lane_ids()
    start = 4 * (3 * field + group)
    return jnp.where((lane >= start) & (lane < start + 4), rolled(rows, 2 + start), packed)


def unpack_margins(packed, field, group):
    lane = lane_ids()
    return jnp.where((lane >= 126) | (lane < 2), rolled(packed, -(2 + 4 * (3 * field + group))), 0.0)


def bond_sum(offsets, own, words, far, total):
    bases = {}

    def base(axis, step):
        if (axis, step) not in bases:
            bases[axis, step] = own[axis] - float(step) if step else own[axis]
        return bases[axis, step]

    for offset in offsets:
        radius = float(sum(step * step for step in offset))
        word, bit = BONDS[offset]
        there = far(offset)
        stretch = [there[axis] - base(axis, offset[axis]) for axis in range(3)]
        inverse = lax.rsqrt(stretch[0] * stretch[0] + stretch[1] * stretch[1] + stretch[2] * stretch[2])
        factor = (BOND_SCALE / radius - (BOND_SCALE / radius**0.5) * inverse) * there[3]
        factor = jnp.where((words(word) & (1 << bit)) == 0, factor, 0.0)
        total = tuple(total[axis] + factor * stretch[axis] for axis in range(3))
    return total


def advance_kernel(cells_z, disp, vel, mod, field_out, vel_out, msg_out, hold, hold_mod, sem):
    copies = [
        pltpu.make_async_copy(disp, hold, sem.at[0]),
        pltpu.make_async_copy(vel, vel_out, sem.at[1]),
        pltpu.make_async_copy(mod, hold_mod, sem.at[2]),
    ]
    for copy in copies:
        copy.start()
    for copy in copies:
        copy.wait()
    lane = lane_ids()
    for field in range(4):
        packed = nothing()
        for x in range(8):
            rows = layer_rows(x)
            if field < 3:
                own = hold[field, rows] + DT_STEP * vel_out[field, rows]
            else:
                own = jnp.sqrt(hold_mod[rows])
            field_out[field, rows] = own
            top = rolled(own, 8 * x - (cells_z - 3))
            low = rolled(own, 64 + 8 * x)
            packed = jnp.where((lane >= 8 * x) & (lane < 8 * x + 3), top, packed)
            packed = jnp.where((lane >= 64 + 8 * x) & (lane < 64 + 8 * x + 3), low, packed)
        msg_out[field] = packed


def side_kernel(cells_z, fields, arrived, main_out, side_out, low_out, top_out):
    wide = cells_z == LANES
    lane = lane_ids()
    first = cells_z % LANES
    packed = [nothing(), nothing()]
    for field in range(4):
        got = arrived[field]
        for x in range(8):
            rows = layer_rows(x)
            own = fields[field, rows]
            below = rolled(got, 125 - 8 * x)
            above = rolled(got, first - (64 + 8 * x))
            side = jnp.where((lane >= first) & (lane < first + 3), above, 0.0)
            side = jnp.where(lane >= 125, below, side)
            if not wide:
                own = jnp.where(lane < cells_z, own, side)
            main_out[field, rows] = own
            side_out[field, rows] = side
        for face, out in enumerate((low_out, top_out)):
            for r in range(3):
                y = 5 * face + r
                out[RIM * field + 8 * r : RIM * field + 8 * r + 8] = main_out[field, across(y)]
                if wide:
                    packed[face] = pack_margins(packed[face], side_out[field, across(y)], field, r)
    low_out[4 * RIM :] = packed[0]
    top_out[4 * RIM :] = packed[1]


def inside_kernel(wide, main, side, bits, fields, partial_out, next_out, frame, near, far, sem):
    copy = pltpu.make_async_copy(fields.at[:3], next_out, sem)
    copy.start()
    blank = jnp.zeros((OWN, LANES), jnp.float32)
    for field in range(4):
        for x in range(8):
            block = main[field, layer_rows(x)]
            margin = side[field, layer_rows(x)] if wide else None
            frame[field, x, :OWN] = blank
            frame[field, x, OWN + 8 :] = blank
            frame[field, x, CORE] = block
            for slot, dz in enumerate(SHIFTS):
                near[slot, field, x, :OWN] = blank
                near[slot, field, x, OWN + 8 :] = blank
                near[slot, field, x, CORE] = z_window(block, margin, dz, wide)
            for slot, dz in enumerate((-3, 3)):
                far[slot, field, x] = z_window(block, margin, dz, wide)
    for x in range(8):

        def there(offset, x=x):
            dx, dy, dz = offset
            rows = slice(OWN + dy, OWN + dy + 8)
            if dz == 0:
                return [frame[field, x + dx, rows] for field in range(4)]
            if abs(dz) == 3:
                return [far[int(dz > 0), field, x + dx] for field in range(4)]
            return [near[SHIFTS.index(dz), field, x + dx, rows] for field in range(4)]

        rows = layer_rows(x)
        own = [main[field, rows] for field in range(3)]
        offsets = [offset for offset in BONDS if 0 <= x + offset[0] < 8]
        total = bond_sum(offsets, own, lambda word, rows=rows: bits[word, rows], there, (nothing(),) * 3)
        for axis in range(3):
            partial_out[axis, rows] = total[axis]
    copy.wait()


def deep_kernel(wide, main, side, below, above, low_out, top_out, hold):
    packed = [nothing(), nothing()]
    sources = ((below, 1, 0), (below, 2, 0), (above, 0, 1), (above, 1, 1))
    for field in range(4):
        if wide:
            for face, block in enumerate((below, above)):
                for r in range(3):
                    hold[face, 8 * r : 8 * r + 8] = unpack_margins(block[4 * RIM :], field, r)
        for face, (out, layers) in enumerate(((low_out, (0, 1, 2)), (top_out, (7, 6, 5)))):
            start = DEEP * field
            for depth, x in enumerate(layers):
                out[start + 8 * depth : start + 8 * depth + 8] = main[field, layer_rows(x)]
                if depth == 2:
                    continue
                for place, (block, r, source) in enumerate(sources):
                    row = 4 * depth + place
                    rim = RIM * field + 8 * r + x
                    out[start + 24 + row : start + 25 + row] = block[rim : rim + 1]
                    if wide:
                        hold[2 + face, row : row + 1] = hold[source, 8 * r + x : 8 * r + x + 1]
            if wide:
                for group, x in enumerate(layers[:2]):
                    packed[face] = pack_margins(packed[face], side[field, layer_rows(x)], field, group)
                packed[face] = pack_margins(packed[face], hold[2 + face, :8], field, 2)
    low_out[4 * DEEP :] = packed[0]
    top_out[4 * DEEP :] = packed[1]


def rim_kernel(wide, main, below, above, bits, partial, partial_out, frame, near):
    blank = jnp.zeros((OWN, LANES), jnp.float32)
    for face, block in enumerate((below, above)):
        for field in range(4):
            for r in range(3):
                rows = block[RIM * field + 8 * r : RIM * field + 8 * r + 8]
                height = r + 1 if face else 3 - r
                frame[face, height - 1, field, :OWN] = blank
                frame[face, height - 1, field, CORE] = rows
                frame[face, height - 1, field, OWN + 8 :] = blank
                if height == 3:
                    continue
                margin = unpack_margins(block[4 * RIM :], field, r) if wide else None
                for slot, dz in enumerate(SHIFTS):
                    near[slot, face, height - 1, field, :OWN] = blank
                    near[slot, face, height - 1, field, CORE] = z_window(rows, margin, dz, wide)
                    near[slot, face, height - 1, field, OWN + 8 :] = blank
    for axis in range(3):
        for x in range(8):
            partial_out[axis, layer_rows(x)] = partial[axis, layer_rows(x)]
    for face in range(2):
        for depth in range(3):
            y = 7 - depth if face else depth

            def there(offset, face=face, depth=depth):
                dx, dy, dz = offset
                height = abs(dy) - depth - 1
                rows = slice(OWN + dx, OWN + dx + 8)
                if dz == 0:
                    return [frame[face, height, field, rows] for field in range(4)]
                return [near[SHIFTS.index(dz), face, height, field, rows] for field in range(4)]

            own = [main[field, across(y)] for field in range(3)]
            offsets = [offset for offset in BONDS if not 0 <= y + offset[1] < 8]
            total = tuple(partial_out[axis, across(y)] for axis in range(3))
            total = bond_sum(offsets, own, lambda word, y=y: bits[word, across(y)], there, total)
            for axis in range(3):
                partial_out[axis, across(y)] = total[axis]


def face_layers(face):
    return (7, 6, 5) if face else (0, 1, 2)


def face_windows(wide, block, frame, near):
    for field in range(4):
        start = DEEP * field
        groups = [block[start + 8 * group : start + 8 * group + 8] for group in (0, 1, 3)]
        margins = [unpack_margins(block[4 * DEEP :], field, group) if wide else None for group in range(3)]
        views = [(frame, groups)]
        for slot, dz in enumerate(SHIFTS):
            views.append((near.at[slot], [z_window(*pair, dz, wide) for pair in zip(groups, margins)]))
        for ref, parts in views:
            for depth in range(2):
                ref[depth, field, CORE] = parts[depth]
                ref[depth, field, 2:OWN] = parts[2][4 * depth : 4 * depth + 2]
                ref[depth, field, OWN + 8 : 14] = parts[2][4 * depth + 2 : 4 * depth + 4]


def face_sum(face, x, main, block, bits, frame, near, total):
    def there(offset):
        dx, dy, dz = offset
        depth = x + dx - 8 if face else -(x + dx) - 1
        rows = slice(OWN + dy, OWN + dy + 8)
        if depth == 2:
            return [block[DEEP * field + 16 : DEEP * field + 24] for field in range(4)]
        if dz == 0:
            return [frame[depth, field, rows] for field in range(4)]
        return [near[SHIFTS.index(dz), depth, field, rows] for field in range(4)]

    rows = layer_rows(x)
    own = [main[field, rows] for field in range(3)]
    offsets = [offset for offset in BONDS if not 0 <= x + offset[0] < 8 and (offset[0] > 0) == bool(face)]
    return bond_sum(offsets, own, lambda word: bits[word, rows], there, total)


def first_face_kernel(wide, main, block, bits, partial, partial_out, frame, near):
    for axis in range(3):
        for x in range(8):
            partial_out[axis, layer_rows(x)] = partial[axis, layer_rows(x)]
    face_windows(wide, block, frame, near)
    even = lax.axis_index("gx") % 2 == 0
    for face in range(2):

        @pl.when(even if face else jnp.logical_not(even))
        def _(face=face):
            for x in face_layers(face):
                rows = layer_rows(x)
                total = tuple(partial[axis, rows] for axis in range(3))
                total = face_sum(face, x, main, block, bits, frame, near, total)
                for axis in range(3):
                    partial_out[axis, rows] = total[axis]


def last_face_kernel(
    wide, main, block, bits, vel, partial, force_out, vel_out, frame, near, force_buf, vel_buf, sem
):
    def finish(x, total, copies):
        rows = layer_rows(x)
        root = main[3, rows]
        for axis in range(3):
            force = root * total[axis]
            force_buf[axis, rows] = force
            vel_buf[axis, rows] = vel[axis, rows] + DT_STEP * force
        for slot, (buf, out) in enumerate(((force_buf, force_out), (vel_buf, vel_out))):
            copies.append(pltpu.make_async_copy(buf.at[:, rows], out.at[:, rows], sem.at[slot, x]))
            copies[-1].start()

    even = lax.axis_index("gx") % 2 == 0
    for face in range(2):

        @pl.when(jnp.logical_not(even) if face else even)
        def _(face=face):
            copies = []
            layers = face_layers(face)
            for x in range(8):
                if x not in layers:
                    finish(x, [partial[axis, layer_rows(x)] for axis in range(3)], copies)
            face_windows(wide, block, frame, near)
            for x in layers[::-1]:
                total = tuple(partial[axis, layer_rows(x)] for axis in range(3))
                finish(x, face_sum(face, x, main, block, bits, frame, near, total), copies)
            for copy in copies:
                copy.wait()


VMEM = pl.BlockSpec(memory_space=pltpu.VMEM)
HBM = pl.BlockSpec(memory_space=pltpu.HBM)


def call(kernel, ins, outs, scratch, flops, *operands):
    shapes = [jax.ShapeDtypeStruct(shape, jnp.float32) for shape, _ in outs]
    moved = sum(4 * int(a.size) for a in operands) + sum(4 * int(a.size) for a in shapes)
    return pl.pallas_call(
        kernel,
        out_shape=shapes,
        in_specs=ins,
        out_specs=[place for _, place in outs],
        scratch_shapes=[pltpu.VMEM(a, jnp.float32) if isinstance(a, tuple) else a for a in scratch],
        compiler_params=pltpu.CompilerParams(vmem_limit_bytes=24 * 1024 * 1024),
        cost_estimate=pl.CostEstimate(flops=flops, bytes_accessed=moved, transcendentals=0),
    )(*operands)


def traded(low, top, axis):
    count = lax.axis_size(axis)
    even = lax.axis_index(axis) % 2 == 0
    got = []
    for start, block in ((0, jnp.where(even, top, low)), (1, jnp.where(even, low, top))):
        pairs = []
        for i in range(start, count - 1, 2):
            pairs += [(i, i + 1), (i + 1, i)]
        got.append(lax.ppermute(block, axis, pairs) if pairs else jnp.zeros_like(block))
    return even, got


def body(displacement, velocity, micromodulus, damage_bits):
    cells_z = micromodulus.shape[2]
    wide = cells_z == LANES
    if not wide:
        pad = [(0, 0), (0, 0), (0, 0), (0, LANES - cells_z)]
        displacement, velocity, damage_bits = (
            jnp.pad(a, pad) for a in (displacement, velocity, damage_bits)
        )
        micromodulus = jnp.pad(micromodulus, pad[1:])
    shape = displacement.shape
    displacement = displacement.reshape(3, ROWS, LANES)
    velocity = velocity.reshape(3, ROWS, LANES)
    micromodulus = micromodulus.reshape(ROWS, LANES)
    damage_bits = damage_bits.reshape(12, ROWS, LANES)
    vectors = (3, ROWS, LANES)
    all_fields = (4, ROWS, LANES)
    fields, kept, z_msg = call(
        functools.partial(advance_kernel, cells_z),
        [HBM] * 3,
        [(all_fields, VMEM), (vectors, VMEM), ((4, 8, LANES), VMEM)],
        [vectors, (ROWS, LANES), pltpu.SemaphoreType.DMA((3,))],
        100_000,
        *(pltpu.with_memory_space_constraint(a, pltpu.HBM) for a in (displacement, velocity, micromodulus)),
    )
    first_half = lax.broadcasted_iota(jnp.int32, z_msg.shape, 2) < 64
    place = lax.axis_index("gz")
    if lax.axis_size("gz") == 2:
        other = lax.ppermute(z_msg, "gz", [(0, 1), (1, 0)])
        z_got = jnp.where(first_half == (place == 1), other, 0.0)
    else:
        even, got = traded(z_msg, z_msg, "gz")
        z_got = jnp.where(first_half == even, got[1], got[0])
    rim_msg = ((4 * RIM + 8, LANES), VMEM)
    main, side, low, top = call(
        functools.partial(side_kernel, cells_z),
        [VMEM] * 2,
        [(all_fields, VMEM), (all_fields, VMEM), rim_msg, rim_msg],
        [],
        100_000,
        fields,
        z_got,
    )
    even, got = traded(low, top, "gy")
    partial, advanced = call(
        functools.partial(inside_kernel, wide),
        [VMEM] * 4,
        [(vectors, VMEM), (vectors, HBM)],
        [(4, 8, FRAME, LANES), (4, 4, 8, FRAME, LANES), (2, 4, 8, 8, LANES), pltpu.SemaphoreType.DMA],
        20_000_000,
        main,
        side,
        damage_bits,
        fields,
    )
    outer, inner, partial = lax.optimization_barrier((got[0], got[1], partial))
    below = jnp.where(even, inner, outer)
    above = jnp.where(even, outer, inner)
    deep_msg = ((4 * DEEP + 8, LANES), VMEM)
    low, top = call(
        functools.partial(deep_kernel, wide),
        [VMEM] * 4,
        [deep_msg, deep_msg],
        [(4, RIM, LANES)],
        100_000,
        main,
        side,
        below,
        above,
    )
    even, got = traded(low, top, "gx")
    (partial,) = call(
        functools.partial(rim_kernel, wide),
        [VMEM] * 5,
        [(vectors, VMEM)],
        [(2, 3, 4, FRAME, LANES), (4, 2, 2, 4, FRAME, LANES)],
        4_000_000,
        main,
        below,
        above,
        damage_bits,
        partial,
    )
    windows = [(2, 4, FRAME, LANES), (4, 2, 4, FRAME, LANES)]
    (partial,) = call(
        functools.partial(first_face_kernel, wide),
        [VMEM] * 4,
        [(vectors, VMEM)],
        windows,
        2_000_000,
        main,
        got[0],
        damage_bits,
        partial,
    )
    force, moved = call(
        functools.partial(last_face_kernel, wide),
        [VMEM] * 5,
        [(vectors, HBM), (vectors, HBM)],
        [*windows, vectors, vectors, pltpu.SemaphoreType.DMA((2, 8))],
        2_000_000,
        main,
        got[1],
        damage_bits,
        kept,
        partial,
    )
    return tuple(a.reshape(shape)[..., :cells_z] for a in (force, advanced, moved))


def solution(mesh):
    placed = P(None, "gx", "gy", "gz")
    return jax.shard_map(
        body,
        mesh=mesh,
        in_specs=(placed, placed, P("gx", "gy", "gz"), placed),
        out_specs=(placed, placed, placed),
        check_vma=False,
    )
```

time: 22.2 us -> 20.6 us (0.928)
  the two profiles are of different devices: /device:TPU:4 before, /device:TPU:16 now
where the time goes in v4:
time: 20.6 us; the launch traced here: 20.5 us
  starting transfers between devices  8.58 us (42%)
  Pallas kernels  6.69 us (32%)
  waiting for transfers between devices  4.39 us (21%)
  between operations  0.76 us (4%)
    ppermute x4, starting transfers between devices, traded(): lax.ppermute(block, axis, pairs)  8.51 us
    pallas_call x7, Pallas kernels, call(): pl.pallas_call(kernel, out_shape=shapes, in_specs=ins, out_specs=[place f...  6.69 us
    ppermute x4, waiting for transfers between devices, traded(): lax.ppermute(block, axis, pairs)  3.25 us
    ppermute x1, waiting for transfers between devices, body(): other = lax.ppermute(z_msg, 'gz', [(0, 1), (1, 0)])  1.14 us
  transfers between devices with their start and end apart: 5, of which 3 were waited for; matrix products, arithmetic and copies ran while one was open for 0% of the time, Pallas kernels for 19%

profile of v4, /device:TPU:16, one launch (start us, length us, event | category | flops | bytes accessed | tf_op | source)
XLA Modules:
  0.0 20.5 jit_solution(3883017418527759008)
XLA Ops:
  0.6 0.0 copy-start
  0.6 1.2 %shard_map.67 = (f32[4,64,128]{2,1,0:T(8,128)S(1)}, f32[3,64,128]{2,1,0:T(8,128)S(1)}, f32[4,8,128]{2,1,0:T(8,128)S(1)}) custom-call(f32[3,64,128]{2,1,0:T(8,128)} %bitcast.11, f32[3,64,128]{2,1,0:T(8,128)} %bitcast.12, f32[64,128]{1,0:T(8,128)} %bitcast.13), custom_call_target="tpu_custom_call" | custom-call | flops 100000 | bytes 475136 | tf_op jit(solution)/shard_map/pallas_call | solution.py:355
  1.8 0.1 collective-permute-start
  1.9 1.1 %collective-permute-done = f32[4,8,128]{2,1,0:T(8,128)S(1)} collective-permute-done((f32[4,8,128]{2,1,0:T(8,128)S(1)}, f32[4,8,128]{2,1,0:T(8,128)S(1)}, u32[]{:S(2)}, u32[]{:S(2)}) %collective-permute-start) | collective-permute-done | bytes 16416 | tf_op jit(solution)/shard_map/ppermute | solution.py:405
  3.1 0.2 %shard_map.68 = (f32[4,64,128]{2,1,0:T(8,128)S(1)}, f32[4,64,128]{2,1,0:T(8,128)S(1)}, f32[104,128]{1,0:T(8,128)S(1)}, f32[104,128]{1,0:T(8,128)S(1)}) custom-call(f32[4,64,128]{2,1,0:T(8,128)S(1)} %get-tuple-element.19.fields, f32[4,8,128]{2,1,0:T(8,128)S(1)} %broadcast_select_fusion.6.arrived), custom_call_target="tpu_custom_call" | custom-call | flops 100000 | bytes 516096 | tf_op jit(solution)/shard_map/pallas_call | solution.py:355
  3.3 0.7 %collective-permute-start.2 = (f32[104,128]{1,0:T(8,128)S(1)}, f32[104,128]{1,0:T(8,128)S(1)}, u32[]{:S(2)}, u32[]{:S(2)}) collective-permute-start(f32[104,128]{1,0:T(8,128)S(1)} %get-tuple-element.39), channel_id=1, source_target_pairs={{2,4},{4,2},{3,5},{5,3},{10,12},{12,10},{11,13},{13,11},{18,20},{2... | collective-permute-start | bytes 159752 | tf_op jit(solution)/shard_map/ppermute | solution.py:374
  4.0 4.3 %collective-permute-start.1 = (f32[104,128]{1,0:T(8,128)S(1)}, f32[104,128]{1,0:T(8,128)S(1)}, u32[]{:S(2)}, u32[]{:S(2)}) collective-permute-start(f32[104,128]{1,0:T(8,128)S(1)} %get-tuple-element.40), channel_id=1, source_target_pairs={{0,2},{2,0},{4,6},{6,4},{1,3},{3,1},{5,7},{7,5},{8,10},{10,8},{12,... | collective-permute-start | bytes 159752 | tf_op jit(solution)/shard_map/ppermute | solution.py:374
  8.3 0.0 copy-done
  8.3 3.0 %shard_map.69 = (f32[3,64,128]{2,1,0:T(8,128)S(1)}, f32[3,64,128]{2,1,0:T(8,128)}) custom-call(f32[4,64,128]{2,1,0:T(8,128)S(1)} %get-tuple-element.21.main, f32[4,64,128]{2,1,0:T(8,128)S(1)} %get-tuple-element.22.side, s32[12,64,128]{2,1,0:T(8,128)S(1)} %bitcast.7, f32[4,64,128]{2,1,0:T(8,128)S(1)} %get-tuple-element.19.fields), custom_call_target="tpu_custom_call" | custom-call | flops 20000000 | bytes 983040 | tf_op jit(solution)/shard_map/pallas_call | solution.py:355
  11.2 0.0 collective-permute-done.2
  11.2 0.0 collective-permute-done.1
  11.3 0.2 shard_map.70
  11.5 1.6 %collective-permute-start.4 = (f32[136,128]{1,0:T(8,128)S(1)}, f32[136,128]{1,0:T(8,128)S(1)}, u32[]{:S(2)}, u32[]{:S(2)}) collective-permute-start(f32[136,128]{1,0:T(8,128)S(1)} %get-tuple-element.35), channel_id=1, source_target_pairs={{0,8},{8,0},{16,24},{24,16},{1,9},{9,1},{17,25},{25,17},{2,10},{10... | collective-permute-start | bytes 208904 | tf_op jit(solution)/shard_map/ppermute | solution.py:374
  13.1 1.9 %collective-permute-start.3 = (f32[136,128]{1,0:T(8,128)S(1)}, f32[136,128]{1,0:T(8,128)S(1)}, u32[]{:S(2)}, u32[]{:S(2)}) collective-permute-start(f32[136,128]{1,0:T(8,128)S(1)} %get-tuple-element.36), channel_id=1, source_target_pairs={{8,16},{16,8},{9,17},{17,9},{10,18},{18,10},{11,19},{19,11},{12,20... | collective-permute-start | bytes 208904 | tf_op jit(solution)/shard_map/ppermute | solution.py:374
  15.0 0.6 %shard_map.71.partial = f32[3,64,128]{2,1,0:T(8,128)S(1)} custom-call(f32[4,64,128]{2,1,0:T(8,128)S(1)} %get-tuple-element.21.main, f32[104,128]{1,0:T(8,128)S(1)} %get-tuple-element.38.below, f32[104,128]{1,0:T(8,128)S(1)} %get-tuple-element.37.above, s32[12,64,128]{2,1,0:T(8,128)S(1)} %bitcast.8, f32[3,64,128]{2,1,0:T(8,128)S(1)} %get-tuple-element.31.partial), custom_call_target="tpu_custom_call" | custom-call | flops 4000000 | bytes 827392 | tf_op jit(solution)/shard_map/pallas_call | solution.py:355
  15.7 0.2 collective-permute-done.4.block
  15.9 0.4 %shard_map.72.partial = f32[3,64,128]{2,1,0:T(8,128)S(1)} custom-call(f32[4,64,128]{2,1,0:T(8,128)S(1)} %get-tuple-element.21.main, f32[136,128]{1,0:T(8,128)S(1)} %collective-permute-done.4.block, s32[12,64,128]{2,1,0:T(8,128)S(1)} %bitcast.9, f32[3,64,128]{2,1,0:T(8,128)S(1)} %shard_map.71.partial), custom_call_target="tpu_custom_call" | custom-call | flops 2000000 | bytes 790528 | tf_op jit(solution)/shard_map/pallas_call | solution.py:355
  16.3 3.0 %collective-permute-done.3.block = f32[136,128]{1,0:T(8,128)S(1)} collective-permute-done((f32[136,128]{1,0:T(8,128)S(1)}, f32[136,128]{1,0:T(8,128)S(1)}, u32[]{:S(2)}, u32[]{:S(2)}) %collective-permute-start.3) | collective-permute-done | bytes 69664 | tf_op jit(solution)/shard_map/ppermute | solution.py:374
  19.3 1.1 %shard_map.73 = (f32[3,64,128]{2,1,0:T(8,128)}, f32[3,64,128]{2,1,0:T(8,128)}) custom-call(f32[4,64,128]{2,1,0:T(8,128)S(1)} %get-tuple-element.21.main, f32[136,128]{1,0:T(8,128)S(1)} %collective-permute-done.3.block, s32[12,64,128]{2,1,0:T(8,128)S(1)} %bitcast.10, f32[3,64,128]{2,1,0:T(8,128)S(1)} %get-tuple-element.30.vel, ...), custom_call_target="tpu_custom_call" | custom-call | flops 2000000 | bytes 987136 | tf_op jit(solution)/shard_map/pallas_call | solution.py:355
  (5 shorter events, 0.0 us)
Async XLA Ops:
  0.6 7.6 %copy-start = (s32[12,8,8,128]{3,2,1,0:T(8,128)S(1)}, s32[12,8,8,128]{3,2,1,0:T(8,128)}, u32[]{:S(2)}) copy-start(s32[12,8,8,128]{3,2,1,0:T(8,128)} %param.7) | copy-start | bytes 1179652
  1.8 1.2 %collective-permute-start = (f32[4,8,128]{2,1,0:T(8,128)S(1)}, f32[4,8,128]{2,1,0:T(8,128)S(1)}, u32[]{:S(2)}, u32[]{:S(2)}) collective-permute-start(f32[4,8,128]{2,1,0:T(8,128)S(1)} %get-tuple-element.20), channel_id=1, source_target_pairs={{0,1},{1,0},{2,3},{3,2},{4,5},{5,4},{6,7},{7,6},{8,9},{9,8},{10,11... | collective-permute-start | bytes 49160 | tf_op jit(solution)/shard_map/ppermute | solution.py:405
  3.3 7.9 %collective-permute-start.2 = (f32[104,128]{1,0:T(8,128)S(1)}, f32[104,128]{1,0:T(8,128)S(1)}, u32[]{:S(2)}, u32[]{:S(2)}) collective-permute-start(f32[104,128]{1,0:T(8,128)S(1)} %get-tuple-element.39), channel_id=1, source_target_pairs={{2,4},{4,2},{3,5},{5,3},{10,12},{12,10},{11,13},{13,11},{18,20},{2... | collective-permute-start | bytes 159752 | tf_op jit(solution)/shard_map/ppermute | solution.py:374
  4.0 7.3 %collective-permute-start.1 = (f32[104,128]{1,0:T(8,128)S(1)}, f32[104,128]{1,0:T(8,128)S(1)}, u32[]{:S(2)}, u32[]{:S(2)}) collective-permute-start(f32[104,128]{1,0:T(8,128)S(1)} %get-tuple-element.40), channel_id=1, source_target_pairs={{0,2},{2,0},{4,6},{6,4},{1,3},{3,1},{5,7},{7,5},{8,10},{10,8},{12,... | collective-permute-start | bytes 159752 | tf_op jit(solution)/shard_map/ppermute | solution.py:374
  11.5 4.4 %collective-permute-start.4 = (f32[136,128]{1,0:T(8,128)S(1)}, f32[136,128]{1,0:T(8,128)S(1)}, u32[]{:S(2)}, u32[]{:S(2)}) collective-permute-start(f32[136,128]{1,0:T(8,128)S(1)} %get-tuple-element.35), channel_id=1, source_target_pairs={{0,8},{8,0},{16,24},{24,16},{1,9},{9,1},{17,25},{25,17},{2,10},{10... | collective-permute-start | bytes 208904 | tf_op jit(solution)/shard_map/ppermute | solution.py:374
  13.1 6.2 %collective-permute-start.3 = (f32[136,128]{1,0:T(8,128)S(1)}, f32[136,128]{1,0:T(8,128)S(1)}, u32[]{:S(2)}, u32[]{:S(2)}) collective-permute-start(f32[136,128]{1,0:T(8,128)S(1)} %get-tuple-element.36), channel_id=1, source_target_pairs={{8,16},{16,8},{9,17},{17,9},{10,18},{18,10},{11,19},{19,11},{12,20... | collective-permute-start | bytes 208904 | tf_op jit(solution)/shard_map/ppermute | solution.py:374

commit v5 on v4

--- a/solution.py
+++ b/solution.py
@@ -299,12 +299,13 @@
     for axis in range(3):
         for x in range(8):
             partial_out[axis, layer_rows(x)] = partial[axis, layer_rows(x)]
-    face_windows(wide, block, frame, near)
     even = lax.axis_index("gx") % 2 == 0
+    joined = partnered("gx", 0)
     for face in range(2):
 
-        @pl.when(even if face else jnp.logical_not(even))
+        @pl.when(jnp.logical_and(joined, even if face else jnp.logical_not(even)))
         def _(face=face):
+            face_windows(wide, block, frame, near)
             for x in face_layers(face):
                 rows = layer_rows(x)
                 total = tuple(partial[axis, rows] for axis in range(3))
@@ -328,9 +329,19 @@
             copies[-1].start()
 
     even = lax.axis_index("gx") % 2 == 0
+    joined = partnered("gx", 1)
+
+    @pl.when(jnp.logical_not(joined))
+    def _():
+        copies = []
+        for x in range(8):
+            finish(x, [partial[axis, layer_rows(x)] for axis in range(3)], copies)
+        for copy in copies:
+            copy.wait()
+
     for face in range(2):
 
-        @pl.when(jnp.logical_not(even) if face else even)
+        @pl.when(jnp.logical_and(joined, jnp.logical_not(even) if face else even))
         def _(face=face):
             copies = []
             layers = face_layers(face)
@@ -363,16 +374,36 @@
     )(*operands)
 
 
+AXES = ("gx", "gy", "gz")
+
+
+def partnered(axis, start):
+    place = lax.axis_index(axis)
+    last = start + (lax.axis_size(axis) - start) // 2 * 2
+    return jnp.logical_and(place >= start, place < last)
+
+
+def pairs_of(axis, start):
+    sizes = [lax.axis_size(name) for name in AXES]
+    which = AXES.index(axis)
+    last = start + (sizes[which] - start) // 2 * 2
+    stride = 1
+    for size in sizes[which + 1 :]:
+        stride *= size
+    pairs = []
+    for device in range(sizes[0] * sizes[1] * sizes[2]):
+        place = device // stride % sizes[which]
+        if start <= place < last:
+            pairs.append((device, device - stride if (place - start) % 2 else device + stride))
+        elif axis != "gz" and sizes[2] % 2 == 0:
+            pairs.append((device, device ^ 1))
+    return pairs
+
+
 def traded(low, top, axis):
-    count = lax.axis_size(axis)
     even = lax.axis_index(axis) % 2 == 0
-    got = []
-    for start, block in ((0, jnp.where(even, top, low)), (1, jnp.where(even, low, top))):
-        pairs = []
-        for i in range(start, count - 1, 2):
-            pairs += [(i, i + 1), (i + 1, i)]
-        got.append(lax.ppermute(block, axis, pairs) if pairs else jnp.zeros_like(block))
-    return even, got
+    blocks = jnp.where(even, top, low), jnp.where(even, low, top)
+    return even, [lax.ppermute(block, AXES, pairs_of(axis, start)) for start, block in enumerate(blocks)]
 
 
 def body(displacement, velocity, micromodulus, damage_bits):
@@ -406,6 +437,7 @@
         z_got = jnp.where(first_half == (place == 1), other, 0.0)
     else:
         even, got = traded(z_msg, z_msg, "gz")
+        got = [jnp.where(partnered("gz", start), a, 0.0) for start, a in enumerate(got)]
         z_got = jnp.where(first_half == even, got[1], got[0])
     rim_msg = ((4 * RIM + 8, LANES), VMEM)
     main, side, low, top = call(
@@ -430,6 +462,8 @@
         fields,
     )
     outer, inner, partial = lax.optimization_barrier((got[0], got[1], partial))
+    outer = jnp.where(partnered("gy", 0), outer, 0.0)
+    inner = jnp.where(partnered("gy", 1), inner, 0.0)
     below = jnp.where(even, inner, outer)
     above = jnp.where(even, outer, inner)
     deep_msg = ((4 * DEEP + 8, LANES), VMEM)

time: 20.6 us -> 16.8 us (0.82)
  starting transfers between devices: 8.58 us -> 4.76 us
    ppermute x4, starting transfers between devices: 8.51 us -> 4.69 us  [traded(): lax.ppermute(block, AXES, pairs_of(axis, start))]
  transfers between devices with their start and end apart: 5 -> 5, of which waited for: 3 -> 3; matrix products, arithmetic and copies ran while one was open for 0% -> 0% of each run, Pallas kernels for 19% -> 24%
where the time goes in v5:
time: 16.8 us; the launch traced here: 16.7 us
  Pallas kernels  6.65 us (40%)
  starting transfers between devices  4.76 us (28%)
  waiting for transfers between devices  4.49 us (27%)
  between operations  0.73 us (4%)
    pallas_call x7, Pallas kernels, call(): pl.pallas_call(kernel, out_shape=shapes, in_specs=ins, out_specs=[place f...  6.65 us
    ppermute x4, starting transfers between devices, traded(): lax.ppermute(block, AXES, pairs_of(axis, start))  4.69 us
    ppermute x4, waiting for transfers between devices, traded(): lax.ppermute(block, AXES, pairs_of(axis, start))  3.35 us
    ppermute x1, waiting for transfers between devices, body(): other = lax.ppermute(z_msg, 'gz', [(0, 1), (1, 0)])  1.14 us
  transfers between devices with their start and end apart: 5, of which 3 were waited for; matrix products, arithmetic and copies ran while one was open for 0% of the time, Pallas kernels for 24%

profile of v5, /device:TPU:16, one launch (start us, length us, event | category | flops | bytes accessed | tf_op | source)
XLA Modules:
  0.0 16.7 jit_solution(17095827250183602405)
XLA Ops:
  0.6 0.0 copy-start
  0.6 1.2 %shard_map.67 = (f32[4,64,128]{2,1,0:T(8,128)S(1)}, f32[3,64,128]{2,1,0:T(8,128)S(1)}, f32[4,8,128]{2,1,0:T(8,128)S(1)}) custom-call(f32[3,64,128]{2,1,0:T(8,128)} %bitcast.11, f32[3,64,128]{2,1,0:T(8,128)} %bitcast.12, f32[64,128]{1,0:T(8,128)} %bitcast.13), custom_call_target="tpu_custom_call" | custom-call | flops 100000 | bytes 475136 | tf_op jit(solution)/shard_map/pallas_call | solution.py:366
  1.8 0.1 collective-permute-start
  1.9 1.1 %collective-permute-done = f32[4,8,128]{2,1,0:T(8,128)S(1)} collective-permute-done((f32[4,8,128]{2,1,0:T(8,128)S(1)}, f32[4,8,128]{2,1,0:T(8,128)S(1)}, u32[]{:S(2)}, u32[]{:S(2)}) %collective-permute-start) | collective-permute-done | bytes 16416 | tf_op jit(solution)/shard_map/ppermute | solution.py:436
  3.1 0.2 %shard_map.68 = (f32[4,64,128]{2,1,0:T(8,128)S(1)}, f32[4,64,128]{2,1,0:T(8,128)S(1)}, f32[104,128]{1,0:T(8,128)S(1)}, f32[104,128]{1,0:T(8,128)S(1)}) custom-call(f32[4,64,128]{2,1,0:T(8,128)S(1)} %get-tuple-element.19.fields, f32[4,8,128]{2,1,0:T(8,128)S(1)} %broadcast_select_fusion.4.arrived), custom_call_target="tpu_custom_call" | custom-call | flops 100000 | bytes 516096 | tf_op jit(solution)/shard_map/pallas_call | solution.py:366
  3.3 0.2 %collective-permute-start.2 = (f32[104,128]{1,0:T(8,128)S(1)}, f32[104,128]{1,0:T(8,128)S(1)}, u32[]{:S(2)}, u32[]{:S(2)}) collective-permute-start(f32[104,128]{1,0:T(8,128)S(1)} %get-tuple-element.39), channel_id=1, source_target_pairs={{0,1},{1,0},{2,4},{3,5},{4,2},{5,3},{6,7},{7,6},{8,9},{9,8},{10,12... | collective-permute-start | bytes 159752 | tf_op jit(solution)/shard_map/ppermute | solution.py:406
  3.5 2.8 %collective-permute-start.1 = (f32[104,128]{1,0:T(8,128)S(1)}, f32[104,128]{1,0:T(8,128)S(1)}, u32[]{:S(2)}, u32[]{:S(2)}) collective-permute-start(f32[104,128]{1,0:T(8,128)S(1)} %get-tuple-element.40), channel_id=1, source_target_pairs={{0,2},{1,3},{2,0},{3,1},{4,6},{5,7},{6,4},{7,5},{8,10},{9,11},{10,... | collective-permute-start | bytes 159752 | tf_op jit(solution)/shard_map/ppermute | solution.py:406
  6.3 0.0 copy-done
  6.4 3.0 %shard_map.69 = (f32[3,64,128]{2,1,0:T(8,128)S(1)}, f32[3,64,128]{2,1,0:T(8,128)}) custom-call(f32[4,64,128]{2,1,0:T(8,128)S(1)} %get-tuple-element.21.main, f32[4,64,128]{2,1,0:T(8,128)S(1)} %get-tuple-element.22.side, s32[12,64,128]{2,1,0:T(8,128)S(1)} %bitcast.7, f32[4,64,128]{2,1,0:T(8,128)S(1)} %get-tuple-element.19.fields), custom_call_target="tpu_custom_call" | custom-call | flops 20000000 | bytes 983040 | tf_op jit(solution)/shard_map/pallas_call | solution.py:366
  9.3 0.0 collective-permute-done.2
  9.3 0.0 collective-permute-done.1
  9.4 0.2 %shard_map.70 = (f32[136,128]{1,0:T(8,128)S(1)}, f32[136,128]{1,0:T(8,128)S(1)}) custom-call(f32[4,64,128]{2,1,0:T(8,128)S(1)} %get-tuple-element.21.main, f32[4,64,128]{2,1,0:T(8,128)S(1)} %get-tuple-element.22.side, f32[104,128]{1,0:T(8,128)S(1)} %get-tuple-element.38.below, f32[104,128]{1,0:T(8,128)S(1)} %get-tuple-element.37.above), custom_call_target="tpu_custom_call" | custom-call | flops 100000 | bytes 507904 | tf_op jit(solution)/shard_map/pallas_call | solution.py:366
  9.6 1.6 %collective-permute-start.4 = (f32[136,128]{1,0:T(8,128)S(1)}, f32[136,128]{1,0:T(8,128)S(1)}, u32[]{:S(2)}, u32[]{:S(2)}) collective-permute-start(f32[136,128]{1,0:T(8,128)S(1)} %get-tuple-element.35), channel_id=1, source_target_pairs={{0,8},{1,9},{2,10},{3,11},{4,12},{5,13},{6,14},{7,15},{8,0},{9,1},... | collective-permute-start | bytes 208904 | tf_op jit(solution)/shard_map/ppermute | solution.py:406
  11.2 0.0 collective-permute-start.3
  11.2 0.6 %shard_map.71.partial = f32[3,64,128]{2,1,0:T(8,128)S(1)} custom-call(f32[4,64,128]{2,1,0:T(8,128)S(1)} %get-tuple-element.21.main, f32[104,128]{1,0:T(8,128)S(1)} %get-tuple-element.38.below, f32[104,128]{1,0:T(8,128)S(1)} %get-tuple-element.37.above, s32[12,64,128]{2,1,0:T(8,128)S(1)} %bitcast.8, f32[3,64,128]{2,1,0:T(8,128)S(1)} %get-tuple-element.31.partial), custom_call_target="tpu_custom_call" | custom-call | flops 4000000 | bytes 827392 | tf_op jit(solution)/shard_map/pallas_call | solution.py:366
  11.8 2.1 %collective-permute-done.4.block = f32[136,128]{1,0:T(8,128)S(1)} collective-permute-done((f32[136,128]{1,0:T(8,128)S(1)}, f32[136,128]{1,0:T(8,128)S(1)}, u32[]{:S(2)}, u32[]{:S(2)}) %collective-permute-start.4) | collective-permute-done | bytes 69664 | tf_op jit(solution)/shard_map/ppermute | solution.py:406
  14.0 0.4 %shard_map.72.partial = f32[3,64,128]{2,1,0:T(8,128)S(1)} custom-call(f32[4,64,128]{2,1,0:T(8,128)S(1)} %get-tuple-element.21.main, f32[136,128]{1,0:T(8,128)S(1)} %collective-permute-done.4.block, s32[12,64,128]{2,1,0:T(8,128)S(1)} %bitcast.9, f32[3,64,128]{2,1,0:T(8,128)S(1)} %shard_map.71.partial), custom_call_target="tpu_custom_call" | custom-call | flops 2000000 | bytes 790528 | tf_op jit(solution)/shard_map/pallas_call | solution.py:366
  14.3 1.2 %collective-permute-done.3.block = f32[136,128]{1,0:T(8,128)S(1)} collective-permute-done((f32[136,128]{1,0:T(8,128)S(1)}, f32[136,128]{1,0:T(8,128)S(1)}, u32[]{:S(2)}, u32[]{:S(2)}) %collective-permute-start.3) | collective-permute-done | bytes 69664 | tf_op jit(solution)/shard_map/ppermute | solution.py:406
  15.5 1.1 %shard_map.73 = (f32[3,64,128]{2,1,0:T(8,128)}, f32[3,64,128]{2,1,0:T(8,128)}) custom-call(f32[4,64,128]{2,1,0:T(8,128)S(1)} %get-tuple-element.21.main, f32[136,128]{1,0:T(8,128)S(1)} %collective-permute-done.3.block, s32[12,64,128]{2,1,0:T(8,128)S(1)} %bitcast.10, f32[3,64,128]{2,1,0:T(8,128)S(1)} %get-tuple-element.30.vel, ...), custom_call_target="tpu_custom_call" | custom-call | flops 2000000 | bytes 987136 | tf_op jit(solution)/shard_map/pallas_call | solution.py:366
  (5 shorter events, 0.0 us)
Async XLA Ops:
  0.6 5.7 %copy-start = (s32[12,8,8,128]{3,2,1,0:T(8,128)S(1)}, s32[12,8,8,128]{3,2,1,0:T(8,128)}, u32[]{:S(2)}) copy-start(s32[12,8,8,128]{3,2,1,0:T(8,128)} %param.7) | copy-start | bytes 1179652
  1.8 1.2 %collective-permute-start = (f32[4,8,128]{2,1,0:T(8,128)S(1)}, f32[4,8,128]{2,1,0:T(8,128)S(1)}, u32[]{:S(2)}, u32[]{:S(2)}) collective-permute-start(f32[4,8,128]{2,1,0:T(8,128)S(1)} %get-tuple-element.20), channel_id=1, source_target_pairs={{0,1},{1,0},{2,3},{3,2},{4,5},{5,4},{6,7},{7,6},{8,9},{9,8},{10,11... | collective-permute-start | bytes 49160 | tf_op jit(solution)/shard_map/ppermute | solution.py:436
  3.3 6.0 %collective-permute-start.2 = (f32[104,128]{1,0:T(8,128)S(1)}, f32[104,128]{1,0:T(8,128)S(1)}, u32[]{:S(2)}, u32[]{:S(2)}) collective-permute-start(f32[104,128]{1,0:T(8,128)S(1)} %get-tuple-element.39), channel_id=1, source_target_pairs={{0,1},{1,0},{2,4},{3,5},{4,2},{5,3},{6,7},{7,6},{8,9},{9,8},{10,12... | collective-permute-start | bytes 159752 | tf_op jit(solution)/shard_map/ppermute | solution.py:406
  3.5 5.8 %collective-permute-start.1 = (f32[104,128]{1,0:T(8,128)S(1)}, f32[104,128]{1,0:T(8,128)S(1)}, u32[]{:S(2)}, u32[]{:S(2)}) collective-permute-start(f32[104,128]{1,0:T(8,128)S(1)} %get-tuple-element.40), channel_id=1, source_target_pairs={{0,2},{1,3},{2,0},{3,1},{4,6},{5,7},{6,4},{7,5},{8,10},{9,11},{10,... | collective-permute-start | bytes 159752 | tf_op jit(solution)/shard_map/ppermute | solution.py:406
  9.6 4.4 %collective-permute-start.4 = (f32[136,128]{1,0:T(8,128)S(1)}, f32[136,128]{1,0:T(8,128)S(1)}, u32[]{:S(2)}, u32[]{:S(2)}) collective-permute-start(f32[136,128]{1,0:T(8,128)S(1)} %get-tuple-element.35), channel_id=1, source_target_pairs={{0,8},{1,9},{2,10},{3,11},{4,12},{5,13},{6,14},{7,15},{8,0},{9,1},... | collective-permute-start | bytes 208904 | tf_op jit(solution)/shard_map/ppermute | solution.py:406
  11.2 4.3 %collective-permute-start.3 = (f32[136,128]{1,0:T(8,128)S(1)}, f32[136,128]{1,0:T(8,128)S(1)}, u32[]{:S(2)}, u32[]{:S(2)}) collective-permute-start(f32[136,128]{1,0:T(8,128)S(1)} %get-tuple-element.36), channel_id=1, source_target_pairs={{0,1},{1,0},{2,3},{3,2},{4,5},{5,4},{6,7},{7,6},{8,16},{9,17},{10,... | collective-permute-start | bytes 208904 | tf_op jit(solution)/shard_map/ppermute | solution.py:406

commit v6 on v5

--- a/solution.py
+++ b/solution.py
@@ -154,7 +154,7 @@
     top_out[4 * RIM :] = packed[1]
 
 
-def inside_kernel(wide, main, side, bits, fields, partial_out, next_out, frame, near, far, sem):
+def inside_kernel(wide, main, side, bits, fields, partial_out, next_out, near, far, sem):
     copy = pltpu.make_async_copy(fields.at[:3], next_out, sem)
     copy.start()
     blank = jnp.zeros((OWN, LANES), jnp.float32)
@@ -162,9 +162,6 @@
         for x in range(8):
             block = main[field, layer_rows(x)]
             margin = side[field, layer_rows(x)] if wide else None
-            frame[field, x, :OWN] = blank
-            frame[field, x, OWN + 8 :] = blank
-            frame[field, x, CORE] = block
             for slot, dz in enumerate(SHIFTS):
                 near[slot, field, x, :OWN] = blank
                 near[slot, field, x, OWN + 8 :] = blank
@@ -176,15 +173,13 @@
         def there(offset, x=x):
             dx, dy, dz = offset
             rows = slice(OWN + dy, OWN + dy + 8)
-            if dz == 0:
-                return [frame[field, x + dx, rows] for field in range(4)]
             if abs(dz) == 3:
                 return [far[int(dz > 0), field, x + dx] for field in range(4)]
             return [near[SHIFTS.index(dz), field, x + dx, rows] for field in range(4)]
 
         rows = layer_rows(x)
         own = [main[field, rows] for field in range(3)]
-        offsets = [offset for offset in BONDS if 0 <= x + offset[0] < 8]
+        offsets = [offset for offset in BONDS if 0 <= x + offset[0] < 8 and offset[2]]
         total = bond_sum(offsets, own, lambda word, rows=rows: bits[word, rows], there, (nothing(),) * 3)
         for axis in range(3):
             partial_out[axis, rows] = total[axis]
@@ -219,8 +214,26 @@
     top_out[4 * DEEP :] = packed[1]
 
 
-def rim_kernel(wide, main, below, above, bits, partial, partial_out, frame, near):
+def rim_kernel(wide, main, below, above, bits, partial, partial_out, level, frame, near):
     blank = jnp.zeros((OWN, LANES), jnp.float32)
+    for field in range(4):
+        for x in range(8):
+            level[field, x, :OWN] = blank
+            level[field, x, CORE] = main[field, layer_rows(x)]
+            level[field, x, OWN + 8 :] = blank
+    for x in range(8):
+
+        def beside(offset, x=x):
+            rows = slice(OWN + offset[1], OWN + offset[1] + 8)
+            return [level[field, x + offset[0], rows] for field in range(4)]
+
+        rows = layer_rows(x)
+        own = [main[field, rows] for field in range(3)]
+        offsets = [offset for offset in BONDS if 0 <= x + offset[0] < 8 and not offset[2]]
+        total = tuple(partial[axis, rows] for axis in range(3))
+        total = bond_sum(offsets, own, lambda word, rows=rows: bits[word, rows], beside, total)
+        for axis in range(3):
+            partial_out[axis, rows] = total[axis]
     for face, block in enumerate((below, above)):
         for field in range(4):
             for r in range(3):
@@ -236,9 +249,6 @@
                     near[slot, face, height - 1, field, :OWN] = blank
                     near[slot, face, height - 1, field, CORE] = z_window(rows, margin, dz, wide)
                     near[slot, face, height - 1, field, OWN + 8 :] = blank
-    for axis in range(3):
-        for x in range(8):
-            partial_out[axis, layer_rows(x)] = partial[axis, layer_rows(x)]
     for face in range(2):
         for depth in range(3):
             y = 7 - depth if face else depth
@@ -295,15 +305,26 @@
     return bond_sum(offsets, own, lambda word: bits[word, rows], there, total)
 
 
-def first_face_kernel(wide, main, block, bits, partial, partial_out, frame, near):
+def face_turn(turn):
+    place = lax.axis_index("gx")
+    odd = place % 2 == 1
+    if turn == 0:
+        return joined("gx", 0), jnp.logical_not(odd)
+    if turn == 1:
+        return jnp.logical_and(joined("gx", 1), place >= 2), odd
+    early = place < 2
+    used = jnp.logical_or(joined("gx", 2), jnp.logical_and(early, joined("gx", 1)))
+    return used, jnp.logical_or(early, jnp.logical_not(odd))
+
+
+def face_kernel(wide, turn, main, block, bits, partial, partial_out, frame, near):
     for axis in range(3):
         for x in range(8):
             partial_out[axis, layer_rows(x)] = partial[axis, layer_rows(x)]
-    even = lax.axis_index("gx") % 2 == 0
-    joined = partnered("gx", 0)
+    used, upper = face_turn(turn)
     for face in range(2):
 
-        @pl.when(jnp.logical_and(joined, even if face else jnp.logical_not(even)))
+        @pl.when(jnp.logical_and(used, upper if face else jnp.logical_not(upper)))
         def _(face=face):
             face_windows(wide, block, frame, near)
             for x in face_layers(face):
@@ -328,10 +349,9 @@
             copies.append(pltpu.make_async_copy(buf.at[:, rows], out.at[:, rows], sem.at[slot, x]))
             copies[-1].start()
 
-    even = lax.axis_index("gx") % 2 == 0
-    joined = partnered("gx", 1)
-
-    @pl.when(jnp.logical_not(joined))
+    used, upper = face_turn(2)
+
+    @pl.when(jnp.logical_not(used))
     def _():
         copies = []
         for x in range(8):
@@ -341,7 +361,7 @@
 
     for face in range(2):
 
-        @pl.when(jnp.logical_and(joined, jnp.logical_not(even) if face else even))
+        @pl.when(jnp.logical_and(used, upper if face else jnp.logical_not(upper)))
         def _(face=face):
             copies = []
             layers = face_layers(face)
@@ -377,23 +397,28 @@
 AXES = ("gx", "gy", "gz")
 
 
-def partnered(axis, start):
+def joined(axis, turn):
     place = lax.axis_index(axis)
-    last = start + (lax.axis_size(axis) - start) // 2 * 2
-    return jnp.logical_and(place >= start, place < last)
-
-
-def pairs_of(axis, start):
+    start, end = span(lax.axis_size(axis), turn)
+    return jnp.logical_and(place >= start, place < end)
+
+
+def span(count, turn):
+    start = turn
+    return start, 2 if turn == 0 else start + (count - start) // 2 * 2
+
+
+def pairs_of(axis, turn):
     sizes = [lax.axis_size(name) for name in AXES]
     which = AXES.index(axis)
-    last = start + (sizes[which] - start) // 2 * 2
+    start, end = span(sizes[which], turn)
     stride = 1
     for size in sizes[which + 1 :]:
         stride *= size
     pairs = []
     for device in range(sizes[0] * sizes[1] * sizes[2]):
         place = device // stride % sizes[which]
-        if start <= place < last:
+        if start <= place < end:
             pairs.append((device, device - stride if (place - start) % 2 else device + stride))
         elif axis != "gz" and sizes[2] % 2 == 0:
             pairs.append((device, device ^ 1))
@@ -402,8 +427,17 @@
 
 def traded(low, top, axis):
     even = lax.axis_index(axis) % 2 == 0
-    blocks = jnp.where(even, top, low), jnp.where(even, low, top)
-    return even, [lax.ppermute(block, AXES, pairs_of(axis, start)) for start, block in enumerate(blocks)]
+    outer, inner = jnp.where(even, top, low), jnp.where(even, low, top)
+    return [lax.ppermute(block, AXES, pairs_of(axis, turn)) for turn, block in enumerate((outer, inner, outer))]
+
+
+def sorted_out(axis, got):
+    place = lax.axis_index(axis)
+    outer = jnp.where(place < 2, got[0], got[2])
+    outer = jnp.where(jnp.logical_or(joined(axis, 0), joined(axis, 2)), outer, 0.0)
+    inner = jnp.where(joined(axis, 1), got[1], 0.0)
+    even = place % 2 == 0
+    return jnp.where(even, inner, outer), jnp.where(even, outer, inner)
 
 
 def body(displacement, velocity, micromodulus, damage_bits):
@@ -436,9 +470,8 @@
         other = lax.ppermute(z_msg, "gz", [(0, 1), (1, 0)])
         z_got = jnp.where(first_half == (place == 1), other, 0.0)
     else:
-        even, got = traded(z_msg, z_msg, "gz")
-        got = [jnp.where(partnered("gz", start), a, 0.0) for start, a in enumerate(got)]
-        z_got = jnp.where(first_half == even, got[1], got[0])
+        before, after = sorted_out("gz", traded(z_msg, z_msg, "gz"))
+        z_got = jnp.where(first_half, before, after)
     rim_msg = ((4 * RIM + 8, LANES), VMEM)
     main, side, low, top = call(
         functools.partial(side_kernel, cells_z),
@@ -449,23 +482,20 @@
         fields,
         z_got,
     )
-    even, got = traded(low, top, "gy")
+    got = traded(low, top, "gy")
     partial, advanced = call(
         functools.partial(inside_kernel, wide),
         [VMEM] * 4,
         [(vectors, VMEM), (vectors, HBM)],
-        [(4, 8, FRAME, LANES), (4, 4, 8, FRAME, LANES), (2, 4, 8, 8, LANES), pltpu.SemaphoreType.DMA],
+        [(4, 4, 8, FRAME, LANES), (2, 4, 8, 8, LANES), pltpu.SemaphoreType.DMA],
         20_000_000,
         main,
         side,
         damage_bits,
         fields,
     )
-    outer, inner, partial = lax.optimization_barrier((got[0], got[1], partial))
-    outer = jnp.where(partnered("gy", 0), outer, 0.0)
-    inner = jnp.where(partnered("gy", 1), inner, 0.0)
-    below = jnp.where(even, inner, outer)
-    above = jnp.where(even, outer, inner)
+    first, second, third, partial = lax.optimization_barrier((got[0], got[1], got[2], partial))
+    below, above = sorted_out("gy", (first, second, third))
     deep_msg = ((4 * DEEP + 8, LANES), VMEM)
     low, top = call(
         functools.partial(deep_kernel, wide),
@@ -478,12 +508,12 @@
         below,
         above,
     )
-    even, got = traded(low, top, "gx")
+    got = traded(low, top, "gx")
     (partial,) = call(
         functools.partial(rim_kernel, wide),
         [VMEM] * 5,
         [(vectors, VMEM)],
-        [(2, 3, 4, FRAME, LANES), (4, 2, 2, 4, FRAME, LANES)],
+        [(4, 8, FRAME, LANES), (2, 3, 4, FRAME, LANES), (4, 2, 2, 4, FRAME, LANES)],
         4_000_000,
         main,
         below,
@@ -492,17 +522,19 @@
         partial,
     )
     windows = [(2, 4, FRAME, LANES), (4, 2, 4, FRAME, LANES)]
-    (partial,) = call(
-        functools.partial(first_face_kernel, wide),
-        [VMEM] * 4,
-        [(vectors, VMEM)],
-        windows,
-        2_000_000,
-        main,
-        got[0],
-        damage_bits,
-        partial,
-    )
+    for turn in range(2):
+        (partial,) = call(
+            functools.partial(face_kernel, wide, turn),
+            [VMEM] * 4,
+            [(vectors, VMEM)],
+            windows,
+            2_000_000,
+            main,
+            got[turn],
+            damage_bits,
+            partial,
+        )
+    last = jnp.where(lax.axis_index("gx") < 2, got[1], got[2])
     force, moved = call(
         functools.partial(last_face_kernel, wide),
         [VMEM] * 5,
@@ -510,7 +542,7 @@
         [*windows, vectors, vectors, pltpu.SemaphoreType.DMA((2, 8))],
         2_000_000,
         main,
-        got[1],
+        last,
         damage_bits,
         kept,
         partial,

time: 16.8 us -> 16.1 us (0.958)
  the two profiles are of different devices: /device:TPU:16 before, /device:TPU:20 now
where the time goes in v6:
time: 16.1 us; the launch traced here: 16 us
  Pallas kernels  6.57 us (41%)
  starting transfers between devices  4.28 us (27%)
  waiting for transfers between devices  4.27 us (27%)
  between operations  0.77 us (5%)
    pallas_call x8, Pallas kernels, call(): pl.pallas_call(kernel, out_shape=shapes, in_specs=ins, out_specs=[place f...  6.57 us
    ppermute x6, starting transfers between devices, traded(): lax.ppermute(block, AXES, pairs_of(axis, turn))  4.21 us
    ppermute x6, waiting for transfers between devices, traded(): lax.ppermute(block, AXES, pairs_of(axis, turn))  3.13 us
    ppermute x1, waiting for transfers between devices, body(): other = lax.ppermute(z_msg, 'gz', [(0, 1), (1, 0)])  1.14 us
  transfers between devices with their start and end apart: 7, of which 4 were waited for; matrix products, arithmetic and copies ran while one was open for 0% of the time, Pallas kernels for 24%

profile of v6, /device:TPU:20, one launch (start us, length us, event | category | flops | bytes accessed | tf_op | source)
XLA Modules:
  0.0 16.0 jit_solution(9937064458613018946)
XLA Ops:
  0.6 0.0 copy-start
  0.6 1.2 %shard_map.67 = (f32[4,64,128]{2,1,0:T(8,128)S(1)}, f32[3,64,128]{2,1,0:T(8,128)S(1)}, f32[4,8,128]{2,1,0:T(8,128)S(1)}) custom-call(f32[3,64,128]{2,1,0:T(8,128)} %bitcast.12, f32[3,64,128]{2,1,0:T(8,128)} %bitcast.13, f32[64,128]{1,0:T(8,128)} %bitcast.14), custom_call_target="tpu_custom_call" | custom-call | flops 100000 | bytes 475136 | tf_op jit(solution)/shard_map/pallas_call | solution.py:386
  1.8 0.1 collective-permute-start
  1.9 1.1 %collective-permute-done = f32[4,8,128]{2,1,0:T(8,128)S(1)} collective-permute-done((f32[4,8,128]{2,1,0:T(8,128)S(1)}, f32[4,8,128]{2,1,0:T(8,128)S(1)}, u32[]{:S(2)}, u32[]{:S(2)}) %collective-permute-start) | collective-permute-done | bytes 16416 | tf_op jit(solution)/shard_map/ppermute | solution.py:470
  3.1 0.2 %shard_map.68 = (f32[4,64,128]{2,1,0:T(8,128)S(1)}, f32[4,64,128]{2,1,0:T(8,128)S(1)}, f32[104,128]{1,0:T(8,128)S(1)}, f32[104,128]{1,0:T(8,128)S(1)}) custom-call(f32[4,64,128]{2,1,0:T(8,128)S(1)} %get-tuple-element.20.fields, f32[4,8,128]{2,1,0:T(8,128)S(1)} %broadcast_select_fusion.5.arrived), custom_call_target="tpu_custom_call" | custom-call | flops 100000 | bytes 516096 | tf_op jit(solution)/shard_map/pallas_call | solution.py:386
  3.3 0.2 %collective-permute-start.1 = (f32[104,128]{1,0:T(8,128)S(1)}, f32[104,128]{1,0:T(8,128)S(1)}, u32[]{:S(2)}, u32[]{:S(2)}) collective-permute-start(f32[104,128]{1,0:T(8,128)S(1)} %get-tuple-element.42), channel_id=1, source_target_pairs={{0,2},{1,3},{2,0},{3,1},{4,5},{5,4},{6,7},{7,6},{8,10},{9,11},{10,... | collective-permute-start | bytes 159752 | tf_op jit(solution)/shard_map/ppermute | solution.py:431
  3.5 1.8 %collective-permute-start.2 = (f32[104,128]{1,0:T(8,128)S(1)}, f32[104,128]{1,0:T(8,128)S(1)}, u32[]{:S(2)}, u32[]{:S(2)}) collective-permute-start(f32[104,128]{1,0:T(8,128)S(1)} %get-tuple-element.41), channel_id=1, source_target_pairs={{0,1},{1,0},{2,4},{3,5},{4,2},{5,3},{6,7},{7,6},{8,9},{9,8},{10,12... | collective-permute-start | bytes 159752 | tf_op jit(solution)/shard_map/ppermute | solution.py:431
  5.3 0.0 collective-permute-start.3
  5.4 0.0 copy-done
  5.4 2.3 %shard_map.69 = (f32[3,64,128]{2,1,0:T(8,128)S(1)}, f32[3,64,128]{2,1,0:T(8,128)}) custom-call(f32[4,64,128]{2,1,0:T(8,128)S(1)} %get-tuple-element.22.main, f32[4,64,128]{2,1,0:T(8,128)S(1)} %get-tuple-element.23.side, s32[12,64,128]{2,1,0:T(8,128)S(1)} %bitcast.7, f32[4,64,128]{2,1,0:T(8,128)S(1)} %get-tuple-element.20.fields), custom_call_target="tpu_custom_call" | custom-call | flops 20000000 | bytes 983040 | tf_op jit(solution)/shard_map/pallas_call | solution.py:386
  7.7 0.0 collective-permute-done.1
  7.7 0.9 %collective-permute-done.2 = f32[104,128]{1,0:T(8,128)S(1)} collective-permute-done((f32[104,128]{1,0:T(8,128)S(1)}, f32[104,128]{1,0:T(8,128)S(1)}, u32[]{:S(2)}, u32[]{:S(2)}) %collective-permute-start.2) | collective-permute-done | bytes 53280 | tf_op jit(solution)/shard_map/ppermute | solution.py:431
  8.6 0.9 %collective-permute-done.3 = f32[104,128]{1,0:T(8,128)S(1)} collective-permute-done((f32[104,128]{1,0:T(8,128)S(1)}, f32[104,128]{1,0:T(8,128)S(1)}, u32[]{:S(2)}, u32[]{:S(2)}) %collective-permute-start.3) | collective-permute-done | bytes 53280 | tf_op jit(solution)/shard_map/ppermute | solution.py:431
  9.5 0.2 %shard_map.70 = (f32[136,128]{1,0:T(8,128)S(1)}, f32[136,128]{1,0:T(8,128)S(1)}) custom-call(f32[4,64,128]{2,1,0:T(8,128)S(1)} %get-tuple-element.22.main, f32[4,64,128]{2,1,0:T(8,128)S(1)} %get-tuple-element.23.side, f32[104,128]{1,0:T(8,128)S(1)} %get-tuple-element.38.below, f32[104,128]{1,0:T(8,128)S(1)} %get-tuple-element.37.above), custom_call_target="tpu_custom_call" | custom-call | flops 100000 | bytes 507904 | tf_op jit(solution)/shard_map/pallas_call | solution.py:386
  9.7 0.1 collective-permute-start.6
  9.8 0.5 %collective-permute-start.4 = (f32[136,128]{1,0:T(8,128)S(1)}, f32[136,128]{1,0:T(8,128)S(1)}, u32[]{:S(2)}, u32[]{:S(2)}) collective-permute-start(f32[136,128]{1,0:T(8,128)S(1)} %get-tuple-element.40), channel_id=1, source_target_pairs={{0,1},{1,0},{2,3},{3,2},{4,5},{5,4},{6,7},{7,6},{8,16},{9,17},{10,... | collective-permute-start | bytes 208904 | tf_op jit(solution)/shard_map/ppermute | solution.py:431
  10.3 1.6 %collective-permute-start.5 = (f32[136,128]{1,0:T(8,128)S(1)}, f32[136,128]{1,0:T(8,128)S(1)}, u32[]{:S(2)}, u32[]{:S(2)}) collective-permute-start(f32[136,128]{1,0:T(8,128)S(1)} %get-tuple-element.39), channel_id=1, source_target_pairs={{0,1},{1,0},{2,3},{3,2},{4,5},{5,4},{6,7},{7,6},{8,9},{9,8},{10,11... | collective-permute-start | bytes 208904 | tf_op jit(solution)/shard_map/ppermute | solution.py:431
  11.9 1.1 %shard_map.71.partial = f32[3,64,128]{2,1,0:T(8,128)S(1)} custom-call(f32[4,64,128]{2,1,0:T(8,128)S(1)} %get-tuple-element.22.main, f32[104,128]{1,0:T(8,128)S(1)} %get-tuple-element.38.below, f32[104,128]{1,0:T(8,128)S(1)} %get-tuple-element.37.above, s32[12,64,128]{2,1,0:T(8,128)S(1)} %bitcast.8, f32[3,64,128]{2,1,0:T(8,128)S(1)} %get-tuple-element.33.partial), custom_call_target="tpu_custom_call" | custom-call | flops 4000000 | bytes 827392 | tf_op jit(solution)/shard_map/pallas_call | solution.py:386
  13.0 0.0 collective-permute-done.6.block
  13.0 1.3 %collective-permute-done.4.block = f32[136,128]{1,0:T(8,128)S(1)} collective-permute-done((f32[136,128]{1,0:T(8,128)S(1)}, f32[136,128]{1,0:T(8,128)S(1)}, u32[]{:S(2)}, u32[]{:S(2)}) %collective-permute-start.4) | collective-permute-done | bytes 69664 | tf_op jit(solution)/shard_map/ppermute | solution.py:431
  14.4 0.4 %shard_map.73.partial = f32[3,64,128]{2,1,0:T(8,128)S(1)} custom-call(f32[4,64,128]{2,1,0:T(8,128)S(1)} %get-tuple-element.22.main, f32[136,128]{1,0:T(8,128)S(1)} %collective-permute-done.4.block, s32[12,64,128]{2,1,0:T(8,128)S(1)} %bitcast.10, f32[3,64,128]{2,1,0:T(8,128)S(1)} %shard_map.72.partial), custom_call_target="tpu_custom_call" | custom-call | flops 2000000 | bytes 790528 | tf_op jit(solution)/shard_map/pallas_call | solution.py:386
  14.8 0.0 collective-permute-done.5
  14.8 1.2 %shard_map.74 = (f32[3,64,128]{2,1,0:T(8,128)}, f32[3,64,128]{2,1,0:T(8,128)}) custom-call(f32[4,64,128]{2,1,0:T(8,128)S(1)} %get-tuple-element.22.main, f32[136,128]{1,0:T(8,128)S(1)} %broadcast_select_fusion.2.block, s32[12,64,128]{2,1,0:T(8,128)S(1)} %bitcast.11, f32[3,64,128]{2,1,0:T(8,128)S(1)} %get-tuple-element.32.vel, ...), custom_call_target="tpu_custom_call" | custom-call | flops 2000000 | bytes 987136 | tf_op jit(solution)/shard_map/pallas_call | solution.py:386
  (7 shorter events, 0.1 us)
Async XLA Ops:
  0.6 4.7 %copy-start = (s32[12,8,8,128]{3,2,1,0:T(8,128)S(1)}, s32[12,8,8,128]{3,2,1,0:T(8,128)}, u32[]{:S(2)}) copy-start(s32[12,8,8,128]{3,2,1,0:T(8,128)} %param.7) | copy-start | bytes 1179652
  1.8 1.2 %collective-permute-start = (f32[4,8,128]{2,1,0:T(8,128)S(1)}, f32[4,8,128]{2,1,0:T(8,128)S(1)}, u32[]{:S(2)}, u32[]{:S(2)}) collective-permute-start(f32[4,8,128]{2,1,0:T(8,128)S(1)} %get-tuple-element.21), channel_id=1, source_target_pairs={{0,1},{1,0},{2,3},{3,2},{4,5},{5,4},{6,7},{7,6},{8,9},{9,8},{10,11... | collective-permute-start | bytes 49160 | tf_op jit(solution)/shard_map/ppermute | solution.py:470
  3.3 4.4 %collective-permute-start.1 = (f32[104,128]{1,0:T(8,128)S(1)}, f32[104,128]{1,0:T(8,128)S(1)}, u32[]{:S(2)}, u32[]{:S(2)}) collective-permute-start(f32[104,128]{1,0:T(8,128)S(1)} %get-tuple-element.42), channel_id=1, source_target_pairs={{0,2},{1,3},{2,0},{3,1},{4,5},{5,4},{6,7},{7,6},{8,10},{9,11},{10,... | collective-permute-start | bytes 159752 | tf_op jit(solution)/shard_map/ppermute | solution.py:431
  3.5 5.1 %collective-permute-start.2 = (f32[104,128]{1,0:T(8,128)S(1)}, f32[104,128]{1,0:T(8,128)S(1)}, u32[]{:S(2)}, u32[]{:S(2)}) collective-permute-start(f32[104,128]{1,0:T(8,128)S(1)} %get-tuple-element.41), channel_id=1, source_target_pairs={{0,1},{1,0},{2,4},{3,5},{4,2},{5,3},{6,7},{7,6},{8,9},{9,8},{10,12... | collective-permute-start | bytes 159752 | tf_op jit(solution)/shard_map/ppermute | solution.py:431
  5.3 4.1 %collective-permute-start.3 = (f32[104,128]{1,0:T(8,128)S(1)}, f32[104,128]{1,0:T(8,128)S(1)}, u32[]{:S(2)}, u32[]{:S(2)}) collective-permute-start(f32[104,128]{1,0:T(8,128)S(1)} %get-tuple-element.42), channel_id=1, source_target_pairs={{0,1},{1,0},{2,3},{3,2},{4,6},{5,7},{6,4},{7,5},{8,9},{9,8},{10,11... | collective-permute-start | bytes 159752 | tf_op jit(solution)/shard_map/ppermute | solution.py:431
  9.7 3.3 %collective-permute-start.6 = (f32[136,128]{1,0:T(8,128)S(1)}, f32[136,128]{1,0:T(8,128)S(1)}, u32[]{:S(2)}, u32[]{:S(2)}) collective-permute-start(f32[136,128]{1,0:T(8,128)S(1)} %get-tuple-element.39), channel_id=1, source_target_pairs={{0,8},{1,9},{2,10},{3,11},{4,12},{5,13},{6,14},{7,15},{8,0},{9,1},... | collective-permute-start | bytes 208904 | tf_op jit(solution)/shard_map/ppermute | solution.py:431
  9.8 4.6 %collective-permute-start.4 = (f32[136,128]{1,0:T(8,128)S(1)}, f32[136,128]{1,0:T(8,128)S(1)}, u32[]{:S(2)}, u32[]{:S(2)}) collective-permute-start(f32[136,128]{1,0:T(8,128)S(1)} %get-tuple-element.40), channel_id=1, source_target_pairs={{0,1},{1,0},{2,3},{3,2},{4,5},{5,4},{6,7},{7,6},{8,16},{9,17},{10,... | collective-permute-start | bytes 208904 | tf_op jit(solution)/shard_map/ppermute | solution.py:431
  10.3 4.5 %collective-permute-start.5 = (f32[136,128]{1,0:T(8,128)S(1)}, f32[136,128]{1,0:T(8,128)S(1)}, u32[]{:S(2)}, u32[]{:S(2)}) collective-permute-start(f32[136,128]{1,0:T(8,128)S(1)} %get-tuple-element.39), channel_id=1, source_target_pairs={{0,1},{1,0},{2,3},{3,2},{4,5},{5,4},{6,7},{7,6},{8,9},{9,8},{10,11... | collective-permute-start | bytes 208904 | tf_op jit(solution)/shard_map/ppermute | solution.py:431

commit v7 on v6

--- a/solution.py
+++ b/solution.py
@@ -99,7 +99,12 @@
     return total
 
 
-def advance_kernel(cells_z, disp, vel, mod, field_out, vel_out, msg_out, hold, hold_mod, sem):
+def rim_lane(field, x):
+    return 4 * (8 * field + x)
+
+
+def advance_kernel(cells_z, paired, disp, vel, mod, field_out, vel_out, *rest):
+    msg_out, (hold, hold_mod, sem) = rest[:-3], rest[-3:]
     copies = [
         pltpu.make_async_copy(disp, hold, sem.at[0]),
         pltpu.make_async_copy(vel, vel_out, sem.at[1]),
@@ -109,9 +114,13 @@
         copy.start()
     for copy in copies:
         copy.wait()
+    if paired:
+        starts = [jnp.where(lax.axis_index("gz") == 0, cells_z - 3, 0)]
+    else:
+        starts = [0, cells_z - 3]
     lane = lane_ids()
-    for field in range(4):
-        packed = nothing()
+    packed = [nothing() for _ in starts]
+    for field in (3, 0, 1, 2):
         for x in range(8):
             rows = layer_rows(x)
             if field < 3:
@@ -119,27 +128,31 @@
             else:
                 own = jnp.sqrt(hold_mod[rows])
             field_out[field, rows] = own
-            top = rolled(own, 8 * x - (cells_z - 3))
-            low = rolled(own, 64 + 8 * x)
-            packed = jnp.where((lane >= 8 * x) & (lane < 8 * x + 3), top, packed)
-            packed = jnp.where((lane >= 64 + 8 * x) & (lane < 64 + 8 * x + 3), low, packed)
-        msg_out[field] = packed
-
-
-def side_kernel(cells_z, fields, arrived, main_out, side_out, low_out, top_out):
+            place = rim_lane(field, x)
+            for side, start in enumerate(starts):
+                moved = pltpu.roll(own, (place - start + LANES) % LANES, axis=1)
+                packed[side] = jnp.where((lane >= place) & (lane < place + 3), moved, packed[side])
+    for out, block in zip(msg_out, packed):
+        out[...] = block
+
+
+def side_kernel(cells_z, paired, fields, *rest):
+    arrived, (main_out, side_out, low_out, top_out) = rest[:-4], rest[-4:]
     wide = cells_z == LANES
     lane = lane_ids()
     first = cells_z % LANES
+    starts = [jnp.where(lax.axis_index("gz") == 0, first, 125)] if paired else [125, first]
+    masks = [(lane >= start) & (lane < start + 3) for start in starts]
+    blocks = [ref[...] for ref in arrived]
     packed = [nothing(), nothing()]
     for field in range(4):
-        got = arrived[field]
         for x in range(8):
             rows = layer_rows(x)
             own = fields[field, rows]
-            below = rolled(got, 125 - 8 * x)
-            above = rolled(got, first - (64 + 8 * x))
-            side = jnp.where((lane >= first) & (lane < first + 3), above, 0.0)
-            side = jnp.where(lane >= 125, below, side)
+            side = nothing()
+            for block, start, mask in zip(blocks, starts, masks):
+                moved = pltpu.roll(block, (start - rim_lane(field, x) + LANES) % LANES, axis=1)
+                side = jnp.where(mask, moved, side)
             if not wide:
                 own = jnp.where(lane < cells_z, own, side)
             main_out[field, rows] = own
@@ -405,7 +418,7 @@
 
 def span(count, turn):
     start = turn
-    return start, 2 if turn == 0 else start + (count - start) // 2 * 2
+    return start, min(2, count // 2 * 2) if turn == 0 else start + (count - start) // 2 * 2
 
 
 def pairs_of(axis, turn):
@@ -456,31 +469,29 @@
     damage_bits = damage_bits.reshape(12, ROWS, LANES)
     vectors = (3, ROWS, LANES)
     all_fields = (4, ROWS, LANES)
-    fields, kept, z_msg = call(
-        functools.partial(advance_kernel, cells_z),
+    paired = lax.axis_size("gz") == 2
+    z_msg = ((8, LANES), VMEM)
+    fields, kept, *z_sent = call(
+        functools.partial(advance_kernel, cells_z, paired),
         [HBM] * 3,
-        [(all_fields, VMEM), (vectors, VMEM), ((4, 8, LANES), VMEM)],
+        [(all_fields, VMEM), (vectors, VMEM), *[z_msg] * (1 if paired else 2)],
         [vectors, (ROWS, LANES), pltpu.SemaphoreType.DMA((3,))],
         100_000,
         *(pltpu.with_memory_space_constraint(a, pltpu.HBM) for a in (displacement, velocity, micromodulus)),
     )
-    first_half = lax.broadcasted_iota(jnp.int32, z_msg.shape, 2) < 64
-    place = lax.axis_index("gz")
-    if lax.axis_size("gz") == 2:
-        other = lax.ppermute(z_msg, "gz", [(0, 1), (1, 0)])
-        z_got = jnp.where(first_half == (place == 1), other, 0.0)
+    if paired:
+        z_got = [lax.ppermute(z_sent[0], "gz", [(0, 1), (1, 0)])]
     else:
-        before, after = sorted_out("gz", traded(z_msg, z_msg, "gz"))
-        z_got = jnp.where(first_half, before, after)
+        z_got = sorted_out("gz", traded(*z_sent, "gz"))
     rim_msg = ((4 * RIM + 8, LANES), VMEM)
     main, side, low, top = call(
-        functools.partial(side_kernel, cells_z),
-        [VMEM] * 2,
+        functools.partial(side_kernel, cells_z, paired),
+        [VMEM] * (1 + len(z_got)),
         [(all_fields, VMEM), (all_fields, VMEM), rim_msg, rim_msg],
         [],
         100_000,
         fields,
-        z_got,
+        *z_got,
     )
     got = traded(low, top, "gy")
     partial, advanced = call(

time: 16.1 us -> 16.1 us (level)
  no operation moved by 1% of the time
where the time goes in v7:
time: 16.1 us; the launch traced here: 15.9 us
  Pallas kernels  6.58 us (41%)
  starting transfers between devices  4.28 us (27%)
  waiting for transfers between devices  4.27 us (27%)
  between operations  0.76 us (5%)
    pallas_call x8, Pallas kernels, call(): pl.pallas_call(kernel, out_shape=shapes, in_specs=ins, out_specs=[place f...  6.58 us
    ppermute x6, starting transfers between devices, traded(): lax.ppermute(block, AXES, pairs_of(axis, turn))  4.21 us
    ppermute x6, waiting for transfers between devices, traded(): lax.ppermute(block, AXES, pairs_of(axis, turn))  3.13 us
    ppermute x1, waiting for transfers between devices, body(): z_got = [lax.ppermute(z_sent[0], 'gz', [(0, 1), (1, 0)])]  1.14 us
  transfers between devices with their start and end apart: 7, of which 4 were waited for; matrix products, arithmetic and copies ran while one was open for 0% of the time, Pallas kernels for 24%

profile of v7, /device:TPU:20, one launch (start us, length us, event | category | flops | bytes accessed | tf_op | source)
XLA Modules:
  0.0 15.9 jit_solution(6993054277420526127)
XLA Ops:
  0.6 0.0 copy-start
  0.6 1.2 %shard_map.67 = (f32[4,64,128]{2,1,0:T(8,128)S(1)}, f32[3,64,128]{2,1,0:T(8,128)S(1)}, f32[8,128]{1,0:T(8,128)S(1)}) custom-call(f32[3,64,128]{2,1,0:T(8,128)} %bitcast.12, f32[3,64,128]{2,1,0:T(8,128)} %bitcast.13, f32[64,128]{1,0:T(8,128)} %bitcast.14), custom_call_target="tpu_custom_call" | custom-call | flops 100000 | bytes 462848 | tf_op jit(solution)/shard_map/pallas_call | solution.py:399
  1.8 0.1 collective-permute-start
  1.9 1.1 %collective-permute-done.rest_0_ = f32[8,128]{1,0:T(8,128)S(1)} collective-permute-done((f32[8,128]{1,0:T(8,128)S(1)}, f32[8,128]{1,0:T(8,128)S(1)}, u32[]{:S(2)}, u32[]{:S(2)}) %collective-permute-start) | collective-permute-done | bytes 4128 | tf_op jit(solution)/shard_map/ppermute | solution.py:483
  3.0 0.2 %shard_map.68 = (f32[4,64,128]{2,1,0:T(8,128)S(1)}, f32[4,64,128]{2,1,0:T(8,128)S(1)}, f32[104,128]{1,0:T(8,128)S(1)}, f32[104,128]{1,0:T(8,128)S(1)}) custom-call(f32[4,64,128]{2,1,0:T(8,128)S(1)} %get-tuple-element.20.fields, f32[8,128]{1,0:T(8,128)S(1)} %collective-permute-done.rest_0_), custom_call_target="tpu_custom_call" | custom-call | flops 100000 | bytes 503808 | tf_op jit(solution)/shard_map/pallas_call | solution.py:399
  3.3 0.2 %collective-permute-start.1 = (f32[104,128]{1,0:T(8,128)S(1)}, f32[104,128]{1,0:T(8,128)S(1)}, u32[]{:S(2)}, u32[]{:S(2)}) collective-permute-start(f32[104,128]{1,0:T(8,128)S(1)} %get-tuple-element.42), channel_id=1, source_target_pairs={{0,2},{1,3},{2,0},{3,1},{4,5},{5,4},{6,7},{7,6},{8,10},{9,11},{10,... | collective-permute-start | bytes 159752 | tf_op jit(solution)/shard_map/ppermute | solution.py:444
  3.5 1.8 %collective-permute-start.2 = (f32[104,128]{1,0:T(8,128)S(1)}, f32[104,128]{1,0:T(8,128)S(1)}, u32[]{:S(2)}, u32[]{:S(2)}) collective-permute-start(f32[104,128]{1,0:T(8,128)S(1)} %get-tuple-element.41), channel_id=1, source_target_pairs={{0,1},{1,0},{2,4},{3,5},{4,2},{5,3},{6,7},{7,6},{8,9},{9,8},{10,12... | collective-permute-start | bytes 159752 | tf_op jit(solution)/shard_map/ppermute | solution.py:444
  5.3 0.0 collective-permute-start.3
  5.3 0.0 copy-done
  5.4 2.3 %shard_map.69 = (f32[3,64,128]{2,1,0:T(8,128)S(1)}, f32[3,64,128]{2,1,0:T(8,128)}) custom-call(f32[4,64,128]{2,1,0:T(8,128)S(1)} %get-tuple-element.22.main, f32[4,64,128]{2,1,0:T(8,128)S(1)} %get-tuple-element.23.side, s32[12,64,128]{2,1,0:T(8,128)S(1)} %bitcast.7, f32[4,64,128]{2,1,0:T(8,128)S(1)} %get-tuple-element.20.fields), custom_call_target="tpu_custom_call" | custom-call | flops 20000000 | bytes 983040 | tf_op jit(solution)/shard_map/pallas_call | solution.py:399
  7.7 0.0 collective-permute-done.1
  7.7 0.9 %collective-permute-done.2 = f32[104,128]{1,0:T(8,128)S(1)} collective-permute-done((f32[104,128]{1,0:T(8,128)S(1)}, f32[104,128]{1,0:T(8,128)S(1)}, u32[]{:S(2)}, u32[]{:S(2)}) %collective-permute-start.2) | collective-permute-done | bytes 53280 | tf_op jit(solution)/shard_map/ppermute | solution.py:444
  8.6 0.9 %collective-permute-done.3 = f32[104,128]{1,0:T(8,128)S(1)} collective-permute-done((f32[104,128]{1,0:T(8,128)S(1)}, f32[104,128]{1,0:T(8,128)S(1)}, u32[]{:S(2)}, u32[]{:S(2)}) %collective-permute-start.3) | collective-permute-done | bytes 53280 | tf_op jit(solution)/shard_map/ppermute | solution.py:444
  9.5 0.2 %shard_map.70 = (f32[136,128]{1,0:T(8,128)S(1)}, f32[136,128]{1,0:T(8,128)S(1)}) custom-call(f32[4,64,128]{2,1,0:T(8,128)S(1)} %get-tuple-element.22.main, f32[4,64,128]{2,1,0:T(8,128)S(1)} %get-tuple-element.23.side, f32[104,128]{1,0:T(8,128)S(1)} %get-tuple-element.38.below, f32[104,128]{1,0:T(8,128)S(1)} %get-tuple-element.37.above), custom_call_target="tpu_custom_call" | custom-call | flops 100000 | bytes 507904 | tf_op jit(solution)/shard_map/pallas_call | solution.py:399
  9.7 0.1 collective-permute-start.6
  9.8 0.5 %collective-permute-start.4 = (f32[136,128]{1,0:T(8,128)S(1)}, f32[136,128]{1,0:T(8,128)S(1)}, u32[]{:S(2)}, u32[]{:S(2)}) collective-permute-start(f32[136,128]{1,0:T(8,128)S(1)} %get-tuple-element.40), channel_id=1, source_target_pairs={{0,1},{1,0},{2,3},{3,2},{4,5},{5,4},{6,7},{7,6},{8,16},{9,17},{10,... | collective-permute-start | bytes 208904 | tf_op jit(solution)/shard_map/ppermute | solution.py:444
  10.3 1.6 %collective-permute-start.5 = (f32[136,128]{1,0:T(8,128)S(1)}, f32[136,128]{1,0:T(8,128)S(1)}, u32[]{:S(2)}, u32[]{:S(2)}) collective-permute-start(f32[136,128]{1,0:T(8,128)S(1)} %get-tuple-element.39), channel_id=1, source_target_pairs={{0,1},{1,0},{2,3},{3,2},{4,5},{5,4},{6,7},{7,6},{8,9},{9,8},{10,11... | collective-permute-start | bytes 208904 | tf_op jit(solution)/shard_map/ppermute | solution.py:444
  11.8 1.1 %shard_map.71.partial = f32[3,64,128]{2,1,0:T(8,128)S(1)} custom-call(f32[4,64,128]{2,1,0:T(8,128)S(1)} %get-tuple-element.22.main, f32[104,128]{1,0:T(8,128)S(1)} %get-tuple-element.38.below, f32[104,128]{1,0:T(8,128)S(1)} %get-tuple-element.37.above, s32[12,64,128]{2,1,0:T(8,128)S(1)} %bitcast.8, f32[3,64,128]{2,1,0:T(8,128)S(1)} %get-tuple-element.33.partial), custom_call_target="tpu_custom_call" | custom-call | flops 4000000 | bytes 827392 | tf_op jit(solution)/shard_map/pallas_call | solution.py:399
  13.0 0.0 collective-permute-done.6.block
  13.0 1.3 %collective-permute-done.4.block = f32[136,128]{1,0:T(8,128)S(1)} collective-permute-done((f32[136,128]{1,0:T(8,128)S(1)}, f32[136,128]{1,0:T(8,128)S(1)}, u32[]{:S(2)}, u32[]{:S(2)}) %collective-permute-start.4) | collective-permute-done | bytes 69664 | tf_op jit(solution)/shard_map/ppermute | solution.py:444
  14.4 0.4 %shard_map.73.partial = f32[3,64,128]{2,1,0:T(8,128)S(1)} custom-call(f32[4,64,128]{2,1,0:T(8,128)S(1)} %get-tuple-element.22.main, f32[136,128]{1,0:T(8,128)S(1)} %collective-permute-done.4.block, s32[12,64,128]{2,1,0:T(8,128)S(1)} %bitcast.10, f32[3,64,128]{2,1,0:T(8,128)S(1)} %shard_map.72.partial), custom_call_target="tpu_custom_call" | custom-call | flops 2000000 | bytes 790528 | tf_op jit(solution)/shard_map/pallas_call | solution.py:399
  14.7 0.0 collective-permute-done.5
  14.8 1.2 %shard_map.74 = (f32[3,64,128]{2,1,0:T(8,128)}, f32[3,64,128]{2,1,0:T(8,128)}) custom-call(f32[4,64,128]{2,1,0:T(8,128)S(1)} %get-tuple-element.22.main, f32[136,128]{1,0:T(8,128)S(1)} %broadcast_select_fusion.2.block, s32[12,64,128]{2,1,0:T(8,128)S(1)} %bitcast.11, f32[3,64,128]{2,1,0:T(8,128)S(1)} %get-tuple-element.32.vel, ...), custom_call_target="tpu_custom_call" | custom-call | flops 2000000 | bytes 987136 | tf_op jit(solution)/shard_map/pallas_call | solution.py:399
  (5 shorter events, 0.1 us)
Async XLA Ops:
  0.6 4.7 %copy-start = (s32[12,8,8,128]{3,2,1,0:T(8,128)S(1)}, s32[12,8,8,128]{3,2,1,0:T(8,128)}, u32[]{:S(2)}) copy-start(s32[12,8,8,128]{3,2,1,0:T(8,128)} %param.7) | copy-start | bytes 1179652
  1.8 1.2 %collective-permute-start = (f32[8,128]{1,0:T(8,128)S(1)}, f32[8,128]{1,0:T(8,128)S(1)}, u32[]{:S(2)}, u32[]{:S(2)}) collective-permute-start(f32[8,128]{1,0:T(8,128)S(1)} %get-tuple-element.21), channel_id=1, source_target_pairs={{0,1},{1,0},{2,3},{3,2},{4,5},{5,4},{6,7},{7,6},{8,9},{9,8},{10,11... | collective-permute-start | bytes 12296 | tf_op jit(solution)/shard_map/ppermute | solution.py:483
  3.3 4.4 %collective-permute-start.1 = (f32[104,128]{1,0:T(8,128)S(1)}, f32[104,128]{1,0:T(8,128)S(1)}, u32[]{:S(2)}, u32[]{:S(2)}) collective-permute-start(f32[104,128]{1,0:T(8,128)S(1)} %get-tuple-element.42), channel_id=1, source_target_pairs={{0,2},{1,3},{2,0},{3,1},{4,5},{5,4},{6,7},{7,6},{8,10},{9,11},{10,... | collective-permute-start | bytes 159752 | tf_op jit(solution)/shard_map/ppermute | solution.py:444
  3.5 5.1 %collective-permute-start.2 = (f32[104,128]{1,0:T(8,128)S(1)}, f32[104,128]{1,0:T(8,128)S(1)}, u32[]{:S(2)}, u32[]{:S(2)}) collective-permute-start(f32[104,128]{1,0:T(8,128)S(1)} %get-tuple-element.41), channel_id=1, source_target_pairs={{0,1},{1,0},{2,4},{3,5},{4,2},{5,3},{6,7},{7,6},{8,9},{9,8},{10,12... | collective-permute-start | bytes 159752 | tf_op jit(solution)/shard_map/ppermute | solution.py:444
  5.3 4.1 %collective-permute-start.3 = (f32[104,128]{1,0:T(8,128)S(1)}, f32[104,128]{1,0:T(8,128)S(1)}, u32[]{:S(2)}, u32[]{:S(2)}) collective-permute-start(f32[104,128]{1,0:T(8,128)S(1)} %get-tuple-element.42), channel_id=1, source_target_pairs={{0,1},{1,0},{2,3},{3,2},{4,6},{5,7},{6,4},{7,5},{8,9},{9,8},{10,11... | collective-permute-start | bytes 159752 | tf_op jit(solution)/shard_map/ppermute | solution.py:444
  9.7 3.3 %collective-permute-start.6 = (f32[136,128]{1,0:T(8,128)S(1)}, f32[136,128]{1,0:T(8,128)S(1)}, u32[]{:S(2)}, u32[]{:S(2)}) collective-permute-start(f32[136,128]{1,0:T(8,128)S(1)} %get-tuple-element.39), channel_id=1, source_target_pairs={{0,8},{1,9},{2,10},{3,11},{4,12},{5,13},{6,14},{7,15},{8,0},{9,1},... | collective-permute-start | bytes 208904 | tf_op jit(solution)/shard_map/ppermute | solution.py:444
  9.8 4.6 %collective-permute-start.4 = (f32[136,128]{1,0:T(8,128)S(1)}, f32[136,128]{1,0:T(8,128)S(1)}, u32[]{:S(2)}, u32[]{:S(2)}) collective-permute-start(f32[136,128]{1,0:T(8,128)S(1)} %get-tuple-element.40), channel_id=1, source_target_pairs={{0,1},{1,0},{2,3},{3,2},{4,5},{5,4},{6,7},{7,6},{8,16},{9,17},{10,... | collective-permute-start | bytes 208904 | tf_op jit(solution)/shard_map/ppermute | solution.py:444
  10.3 4.5 %collective-permute-start.5 = (f32[136,128]{1,0:T(8,128)S(1)}, f32[136,128]{1,0:T(8,128)S(1)}, u32[]{:S(2)}, u32[]{:S(2)}) collective-permute-start(f32[136,128]{1,0:T(8,128)S(1)} %get-tuple-element.39), channel_id=1, source_target_pairs={{0,1},{1,0},{2,3},{3,2},{4,5},{5,4},{6,7},{7,6},{8,9},{9,8},{10,11... | collective-permute-start | bytes 208904 | tf_op jit(solution)/shard_map/ppermute | solution.py:444

commit v8 on v7

--- a/solution.py
+++ b/solution.py
@@ -106,14 +106,12 @@
 def advance_kernel(cells_z, paired, disp, vel, mod, field_out, vel_out, *rest):
     msg_out, (hold, hold_mod, sem) = rest[:-3], rest[-3:]
     copies = [
-        pltpu.make_async_copy(disp, hold, sem.at[0]),
-        pltpu.make_async_copy(vel, vel_out, sem.at[1]),
-        pltpu.make_async_copy(mod, hold_mod, sem.at[2]),
+        pltpu.make_async_copy(mod, hold_mod, sem.at[0]),
+        pltpu.make_async_copy(disp, hold, sem.at[1]),
+        pltpu.make_async_copy(vel, vel_out, sem.at[2]),
     ]
     for copy in copies:
         copy.start()
-    for copy in copies:
-        copy.wait()
     if paired:
         starts = [jnp.where(lax.axis_index("gz") == 0, cells_z - 3, 0)]
     else:
@@ -121,6 +119,8 @@
     lane = lane_ids()
     packed = [nothing() for _ in starts]
     for field in (3, 0, 1, 2):
+        for copy in {3: copies[:1], 0: copies[1:]}.get(field, ()):
+            copy.wait()
         for x in range(8):
             rows = layer_rows(x)
             if field < 3:
@@ -351,15 +351,18 @@
 def last_face_kernel(
     wide, main, block, bits, vel, partial, force_out, vel_out, frame, near, force_buf, vel_buf, sem
 ):
-    def finish(x, total, copies):
+    def finish(x, total):
         rows = layer_rows(x)
         root = main[3, rows]
         for axis in range(3):
             force = root * total[axis]
             force_buf[axis, rows] = force
             vel_buf[axis, rows] = vel[axis, rows] + DT_STEP * force
+
+    def send(first, last, copies):
+        rows = slice(8 * first, 8 * last)
         for slot, (buf, out) in enumerate(((force_buf, force_out), (vel_buf, vel_out))):
-            copies.append(pltpu.make_async_copy(buf.at[:, rows], out.at[:, rows], sem.at[slot, x]))
+            copies.append(pltpu.make_async_copy(buf.at[:, rows], out.at[:, rows], sem.at[slot, first]))
             copies[-1].start()
 
     used, upper = face_turn(2)
@@ -368,7 +371,8 @@
     def _():
         copies = []
         for x in range(8):
-            finish(x, [partial[axis, layer_rows(x)] for axis in range(3)], copies)
+            finish(x, [partial[axis, layer_rows(x)] for axis in range(3)])
+        send(0, 8, copies)
         for copy in copies:
             copy.wait()
 
@@ -378,13 +382,15 @@
         def _(face=face):
             copies = []
             layers = face_layers(face)
+            face_windows(wide, block, frame, near)
             for x in range(8):
                 if x not in layers:
-                    finish(x, [partial[axis, layer_rows(x)] for axis in range(3)], copies)
-            face_windows(wide, block, frame, near)
+                    finish(x, [partial[axis, layer_rows(x)] for axis in range(3)])
+            send(*((0, 5) if face else (3, 8)), copies)
             for x in layers[::-1]:
                 total = tuple(partial[axis, layer_rows(x)] for axis in range(3))
-                finish(x, face_sum(face, x, main, block, bits, frame, near, total), copies)
+                finish(x, face_sum(face, x, main, block, bits, frame, near, total))
+                send(x, x + 1, copies)
             for copy in copies:
                 copy.wait()
 

time: 16.1 us -> 16.1 us (level)
  no operation moved by 1% of the time
where the time goes in v8:
time: 16.1 us; the launch traced here: 15.9 us
  Pallas kernels  6.56 us (41%)
  starting transfers between devices  4.28 us (27%)
  waiting for transfers between devices  4.27 us (27%)
  between operations  0.76 us (5%)
    pallas_call x8, Pallas kernels, call(): pl.pallas_call(kernel, out_shape=shapes, in_specs=ins, out_specs=[place f...  6.56 us
    ppermute x6, starting transfers between devices, traded(): lax.ppermute(block, AXES, pairs_of(axis, turn))  4.21 us
    ppermute x6, waiting for transfers between devices, traded(): lax.ppermute(block, AXES, pairs_of(axis, turn))  3.13 us
    ppermute x1, waiting for transfers between devices, body(): z_got = [lax.ppermute(z_sent[0], 'gz', [(0, 1), (1, 0)])]  1.14 us
  transfers between devices with their start and end apart: 7, of which 4 were waited for; matrix products, arithmetic and copies ran while one was open for 0% of the time, Pallas kernels for 24%

profile of v8, /device:TPU:20, one launch (start us, length us, event | category | flops | bytes accessed | tf_op | source)
XLA Modules:
  0.0 15.9 jit_solution(14245774111231643279)
XLA Ops:
  0.6 0.0 copy-start
  0.6 1.2 %shard_map.67 = (f32[4,64,128]{2,1,0:T(8,128)S(1)}, f32[3,64,128]{2,1,0:T(8,128)S(1)}, f32[8,128]{1,0:T(8,128)S(1)}) custom-call(f32[3,64,128]{2,1,0:T(8,128)} %bitcast.12, f32[3,64,128]{2,1,0:T(8,128)} %bitcast.13, f32[64,128]{1,0:T(8,128)} %bitcast.14), custom_call_target="tpu_custom_call" | custom-call | flops 100000 | bytes 462848 | tf_op jit(solution)/shard_map/pallas_call | solution.py:405
  1.8 0.1 collective-permute-start
  1.9 1.1 %collective-permute-done.rest_0_ = f32[8,128]{1,0:T(8,128)S(1)} collective-permute-done((f32[8,128]{1,0:T(8,128)S(1)}, f32[8,128]{1,0:T(8,128)S(1)}, u32[]{:S(2)}, u32[]{:S(2)}) %collective-permute-start) | collective-permute-done | bytes 4128 | tf_op jit(solution)/shard_map/ppermute | solution.py:489
  3.0 0.2 %shard_map.68 = (f32[4,64,128]{2,1,0:T(8,128)S(1)}, f32[4,64,128]{2,1,0:T(8,128)S(1)}, f32[104,128]{1,0:T(8,128)S(1)}, f32[104,128]{1,0:T(8,128)S(1)}) custom-call(f32[4,64,128]{2,1,0:T(8,128)S(1)} %get-tuple-element.20.fields, f32[8,128]{1,0:T(8,128)S(1)} %collective-permute-done.rest_0_), custom_call_target="tpu_custom_call" | custom-call | flops 100000 | bytes 503808 | tf_op jit(solution)/shard_map/pallas_call | solution.py:405
  3.3 0.2 %collective-permute-start.1 = (f32[104,128]{1,0:T(8,128)S(1)}, f32[104,128]{1,0:T(8,128)S(1)}, u32[]{:S(2)}, u32[]{:S(2)}) collective-permute-start(f32[104,128]{1,0:T(8,128)S(1)} %get-tuple-element.42), channel_id=1, source_target_pairs={{0,2},{1,3},{2,0},{3,1},{4,5},{5,4},{6,7},{7,6},{8,10},{9,11},{10,... | collective-permute-start | bytes 159752 | tf_op jit(solution)/shard_map/ppermute | solution.py:450
  3.5 1.8 %collective-permute-start.2 = (f32[104,128]{1,0:T(8,128)S(1)}, f32[104,128]{1,0:T(8,128)S(1)}, u32[]{:S(2)}, u32[]{:S(2)}) collective-permute-start(f32[104,128]{1,0:T(8,128)S(1)} %get-tuple-element.41), channel_id=1, source_target_pairs={{0,1},{1,0},{2,4},{3,5},{4,2},{5,3},{6,7},{7,6},{8,9},{9,8},{10,12... | collective-permute-start | bytes 159752 | tf_op jit(solution)/shard_map/ppermute | solution.py:450
  5.3 0.0 collective-permute-start.3
  5.3 0.0 copy-done
  5.3 2.3 %shard_map.69 = (f32[3,64,128]{2,1,0:T(8,128)S(1)}, f32[3,64,128]{2,1,0:T(8,128)}) custom-call(f32[4,64,128]{2,1,0:T(8,128)S(1)} %get-tuple-element.22.main, f32[4,64,128]{2,1,0:T(8,128)S(1)} %get-tuple-element.23.side, s32[12,64,128]{2,1,0:T(8,128)S(1)} %bitcast.7, f32[4,64,128]{2,1,0:T(8,128)S(1)} %get-tuple-element.20.fields), custom_call_target="tpu_custom_call" | custom-call | flops 20000000 | bytes 983040 | tf_op jit(solution)/shard_map/pallas_call | solution.py:405
  7.6 0.0 collective-permute-done.1
  7.7 0.9 %collective-permute-done.2 = f32[104,128]{1,0:T(8,128)S(1)} collective-permute-done((f32[104,128]{1,0:T(8,128)S(1)}, f32[104,128]{1,0:T(8,128)S(1)}, u32[]{:S(2)}, u32[]{:S(2)}) %collective-permute-start.2) | collective-permute-done | bytes 53280 | tf_op jit(solution)/shard_map/ppermute | solution.py:450
  8.6 0.9 %collective-permute-done.3 = f32[104,128]{1,0:T(8,128)S(1)} collective-permute-done((f32[104,128]{1,0:T(8,128)S(1)}, f32[104,128]{1,0:T(8,128)S(1)}, u32[]{:S(2)}, u32[]{:S(2)}) %collective-permute-start.3) | collective-permute-done | bytes 53280 | tf_op jit(solution)/shard_map/ppermute | solution.py:450
  9.5 0.2 %shard_map.70 = (f32[136,128]{1,0:T(8,128)S(1)}, f32[136,128]{1,0:T(8,128)S(1)}) custom-call(f32[4,64,128]{2,1,0:T(8,128)S(1)} %get-tuple-element.22.main, f32[4,64,128]{2,1,0:T(8,128)S(1)} %get-tuple-element.23.side, f32[104,128]{1,0:T(8,128)S(1)} %get-tuple-element.38.below, f32[104,128]{1,0:T(8,128)S(1)} %get-tuple-element.37.above), custom_call_target="tpu_custom_call" | custom-call | flops 100000 | bytes 507904 | tf_op jit(solution)/shard_map/pallas_call | solution.py:405
  9.7 0.1 collective-permute-start.6
  9.8 0.5 %collective-permute-start.4 = (f32[136,128]{1,0:T(8,128)S(1)}, f32[136,128]{1,0:T(8,128)S(1)}, u32[]{:S(2)}, u32[]{:S(2)}) collective-permute-start(f32[136,128]{1,0:T(8,128)S(1)} %get-tuple-element.40), channel_id=1, source_target_pairs={{0,1},{1,0},{2,3},{3,2},{4,5},{5,4},{6,7},{7,6},{8,16},{9,17},{10,... | collective-permute-start | bytes 208904 | tf_op jit(solution)/shard_map/ppermute | solution.py:450
  10.3 1.6 %collective-permute-start.5 = (f32[136,128]{1,0:T(8,128)S(1)}, f32[136,128]{1,0:T(8,128)S(1)}, u32[]{:S(2)}, u32[]{:S(2)}) collective-permute-start(f32[136,128]{1,0:T(8,128)S(1)} %get-tuple-element.39), channel_id=1, source_target_pairs={{0,1},{1,0},{2,3},{3,2},{4,5},{5,4},{6,7},{7,6},{8,9},{9,8},{10,11... | collective-permute-start | bytes 208904 | tf_op jit(solution)/shard_map/ppermute | solution.py:450
  11.8 1.1 %shard_map.71.partial = f32[3,64,128]{2,1,0:T(8,128)S(1)} custom-call(f32[4,64,128]{2,1,0:T(8,128)S(1)} %get-tuple-element.22.main, f32[104,128]{1,0:T(8,128)S(1)} %get-tuple-element.38.below, f32[104,128]{1,0:T(8,128)S(1)} %get-tuple-element.37.above, s32[12,64,128]{2,1,0:T(8,128)S(1)} %bitcast.8, f32[3,64,128]{2,1,0:T(8,128)S(1)} %get-tuple-element.33.partial), custom_call_target="tpu_custom_call" | custom-call | flops 4000000 | bytes 827392 | tf_op jit(solution)/shard_map/pallas_call | solution.py:405
  13.0 0.0 collective-permute-done.6.block
  13.0 1.3 %collective-permute-done.4.block = f32[136,128]{1,0:T(8,128)S(1)} collective-permute-done((f32[136,128]{1,0:T(8,128)S(1)}, f32[136,128]{1,0:T(8,128)S(1)}, u32[]{:S(2)}, u32[]{:S(2)}) %collective-permute-start.4) | collective-permute-done | bytes 69664 | tf_op jit(solution)/shard_map/ppermute | solution.py:450
  14.3 0.4 %shard_map.73.partial = f32[3,64,128]{2,1,0:T(8,128)S(1)} custom-call(f32[4,64,128]{2,1,0:T(8,128)S(1)} %get-tuple-element.22.main, f32[136,128]{1,0:T(8,128)S(1)} %collective-permute-done.4.block, s32[12,64,128]{2,1,0:T(8,128)S(1)} %bitcast.10, f32[3,64,128]{2,1,0:T(8,128)S(1)} %shard_map.72.partial), custom_call_target="tpu_custom_call" | custom-call | flops 2000000 | bytes 790528 | tf_op jit(solution)/shard_map/pallas_call | solution.py:405
  14.7 0.0 collective-permute-done.5
  14.8 1.2 %shard_map.74 = (f32[3,64,128]{2,1,0:T(8,128)}, f32[3,64,128]{2,1,0:T(8,128)}) custom-call(f32[4,64,128]{2,1,0:T(8,128)S(1)} %get-tuple-element.22.main, f32[136,128]{1,0:T(8,128)S(1)} %broadcast_select_fusion.2.block, s32[12,64,128]{2,1,0:T(8,128)S(1)} %bitcast.11, f32[3,64,128]{2,1,0:T(8,128)S(1)} %get-tuple-element.32.vel, ...), custom_call_target="tpu_custom_call" | custom-call | flops 2000000 | bytes 987136 | tf_op jit(solution)/shard_map/pallas_call | solution.py:405
  (5 shorter events, 0.1 us)
Async XLA Ops:
  0.6 4.7 %copy-start = (s32[12,8,8,128]{3,2,1,0:T(8,128)S(1)}, s32[12,8,8,128]{3,2,1,0:T(8,128)}, u32[]{:S(2)}) copy-start(s32[12,8,8,128]{3,2,1,0:T(8,128)} %param.7) | copy-start | bytes 1179652
  1.8 1.2 %collective-permute-start = (f32[8,128]{1,0:T(8,128)S(1)}, f32[8,128]{1,0:T(8,128)S(1)}, u32[]{:S(2)}, u32[]{:S(2)}) collective-permute-start(f32[8,128]{1,0:T(8,128)S(1)} %get-tuple-element.21), channel_id=1, source_target_pairs={{0,1},{1,0},{2,3},{3,2},{4,5},{5,4},{6,7},{7,6},{8,9},{9,8},{10,11... | collective-permute-start | bytes 12296 | tf_op jit(solution)/shard_map/ppermute | solution.py:489
  3.3 4.4 %collective-permute-start.1 = (f32[104,128]{1,0:T(8,128)S(1)}, f32[104,128]{1,0:T(8,128)S(1)}, u32[]{:S(2)}, u32[]{:S(2)}) collective-permute-start(f32[104,128]{1,0:T(8,128)S(1)} %get-tuple-element.42), channel_id=1, source_target_pairs={{0,2},{1,3},{2,0},{3,1},{4,5},{5,4},{6,7},{7,6},{8,10},{9,11},{10,... | collective-permute-start | bytes 159752 | tf_op jit(solution)/shard_map/ppermute | solution.py:450
  3.5 5.1 %collective-permute-start.2 = (f32[104,128]{1,0:T(8,128)S(1)}, f32[104,128]{1,0:T(8,128)S(1)}, u32[]{:S(2)}, u32[]{:S(2)}) collective-permute-start(f32[104,128]{1,0:T(8,128)S(1)} %get-tuple-element.41), channel_id=1, source_target_pairs={{0,1},{1,0},{2,4},{3,5},{4,2},{5,3},{6,7},{7,6},{8,9},{9,8},{10,12... | collective-permute-start | bytes 159752 | tf_op jit(solution)/shard_map/ppermute | solution.py:450
  5.3 4.1 %collective-permute-start.3 = (f32[104,128]{1,0:T(8,128)S(1)}, f32[104,128]{1,0:T(8,128)S(1)}, u32[]{:S(2)}, u32[]{:S(2)}) collective-permute-start(f32[104,128]{1,0:T(8,128)S(1)} %get-tuple-element.42), channel_id=1, source_target_pairs={{0,1},{1,0},{2,3},{3,2},{4,6},{5,7},{6,4},{7,5},{8,9},{9,8},{10,11... | collective-permute-start | bytes 159752 | tf_op jit(solution)/shard_map/ppermute | solution.py:450
  9.7 3.3 %collective-permute-start.6 = (f32[136,128]{1,0:T(8,128)S(1)}, f32[136,128]{1,0:T(8,128)S(1)}, u32[]{:S(2)}, u32[]{:S(2)}) collective-permute-start(f32[136,128]{1,0:T(8,128)S(1)} %get-tuple-element.39), channel_id=1, source_target_pairs={{0,8},{1,9},{2,10},{3,11},{4,12},{5,13},{6,14},{7,15},{8,0},{9,1},... | collective-permute-start | bytes 208904 | tf_op jit(solution)/shard_map/ppermute | solution.py:450
  9.8 4.6 %collective-permute-start.4 = (f32[136,128]{1,0:T(8,128)S(1)}, f32[136,128]{1,0:T(8,128)S(1)}, u32[]{:S(2)}, u32[]{:S(2)}) collective-permute-start(f32[136,128]{1,0:T(8,128)S(1)} %get-tuple-element.40), channel_id=1, source_target_pairs={{0,1},{1,0},{2,3},{3,2},{4,5},{5,4},{6,7},{7,6},{8,16},{9,17},{10,... | collective-permute-start | bytes 208904 | tf_op jit(solution)/shard_map/ppermute | solution.py:450
  10.3 4.5 %collective-permute-start.5 = (f32[136,128]{1,0:T(8,128)S(1)}, f32[136,128]{1,0:T(8,128)S(1)}, u32[]{:S(2)}, u32[]{:S(2)}) collective-permute-start(f32[136,128]{1,0:T(8,128)S(1)} %get-tuple-element.39), channel_id=1, source_target_pairs={{0,1},{1,0},{2,3},{3,2},{4,5},{5,4},{6,7},{7,6},{8,9},{9,8},{10,11... | collective-permute-start | bytes 208904 | tf_op jit(solution)/shard_map/ppermute | solution.py:450
